TPU v7x, 32 devices: a whole 2x2x4 slice. The times are simulated.
32 devices in a mesh: batch: 16 (over z, x, core), tm: 2 (over y).
Axes of the slice: x: 2, y: 2, z: 4, core: 2. Of those that a mesh axis runs over, the one named last changes fastest.
Arguments:
- audio: bfloat16 [64, 256, 768], P('batch', 'tm'), as said below
- video: bfloat16 [64, 128, 1024], P('batch'), as said below
- pair_ids: int32 [64], P('batch'), may hold values from 0 to 63, each once
- windows: int32 [64], P('batch'), may hold values from 1 to 32, as said below
- lengths: int32 [64], P('batch'), may hold values from 64 to 256, as said below
- w_qkv: bfloat16 [768, 2304], replicated, as said below
- w_out: bfloat16 [768, 768], replicated, may hold values from -0.21875 to 0.21875
- w_query: bfloat16 [1024, 768], replicated, may hold values from -0.1875 to 0.1875
- w_audio_embed: bfloat16 [768, 768], replicated, may hold values from -0.21875 to 0.21875
- w_video_embed: bfloat16 [768, 768], replicated, may hold values from -0.21875 to 0.21875
Outputs:
- audio_mixed: bfloat16 [64, 256, 768], P('batch', 'tm')
- audio_embed: float32 [64, 768], P('batch')
- video_embed: float32 [64, 768], P('batch')
- logits: float32 [64, 64], P('batch')
- row_loss: float32 [64], P('batch')
Inputs may be any that keep to these rules, and one draw needn't show every extreme that they name: `pair_ids`: a permutation of the clip numbers. `windows`: some clip reaches 32 in every draw. `lengths`: some clip is valid over all 256 frames in every draw. `audio`: frame features. `video`: token features. `w_qkv`: projection weights of scale 768 to the minus one half.
All inputs are finite; a program needn't handle non-finite values.
Results may differ from a plain program's by a relative error of at most 0.0065.
Values may be sent and summed in bfloat16 or wider, within the bound.
No kernel may reach another device: no remote copies, remote signals or barrier semaphores. Data moves between devices by JAX's collectives and lax.ppermute only.
A program may use at most 128 MiB of HBM per device.

v0:
```python
import jax
import jax.numpy as jnp
from jax import lax
from jax.sharding import PartitionSpec as P

HA = 12
HS = 64


NEG_LARGE = -1e30
LOGIT_SCALE = 10.0
LOGIT_BIAS = -10.0


def extended(block, sides, width):
    for axis, dim in sides:
        count = lax.axis_size(axis)
        forward = [(i, i + 1) for i in range(count - 1)]
        backward = [(target, source) for source, target in forward]
        low = lax.ppermute(
            lax.slice_in_dim(block, block.shape[dim] - width, None, axis=dim), axis, forward
        )
        high = lax.ppermute(lax.slice_in_dim(block, 0, width, axis=dim), axis, backward)
        block = jnp.concatenate([low, block, high], axis=dim)
    return block


def softmax_parts(scores, allowed):
    scores = jnp.where(allowed, scores, NEG_LARGE)
    highest = jnp.max(scores, axis=-1, keepdims=True)
    weights = jnp.where(allowed, jnp.exp(scores - highest), 0.0)
    return (highest, weights, jnp.sum(weights, axis=-1))


def unit_rows(matrix):
    return matrix / jnp.sqrt(jnp.sum(matrix * matrix, axis=1, keepdims=True) + 1e-06)


def per_device(
    audio, video, pair_ids, windows, lengths, w_qkv, w_out, w_query, w_audio_embed, w_video_embed
):
    clip_count, frame_count, model_width = audio.shape
    token_count = video.shape[1]
    tm_size = lax.axis_size("tm")
    tm_index = lax.axis_index("tm")
    local_width = model_width // tm_size
    local_heads = HA // tm_size
    total_frames = frame_count * tm_size
    halo_reach = frame_count // 4
    key_span = frame_count + 2 * halo_reach
    head_scale = HS ** (-0.5)
    flat_audio = audio.reshape(clip_count * frame_count, model_width)
    projected = jnp.dot(flat_audio, w_qkv, preferred_element_type=jnp.float32).astype(jnp.bfloat16)
    projected = projected.reshape(clip_count, frame_count, 3 * model_width)
    queries = projected[:, :, :model_width].reshape(clip_count, frame_count, HA, HS)
    key_value = projected[:, :, model_width:]
    padded = extended(key_value, (("tm", 1),), halo_reach)
    near_keys = padded[:, :, :model_width].reshape(clip_count, key_span, HA, HS)
    near_values = padded[:, :, model_width:].reshape(clip_count, key_span, HA, HS)
    query_pos = tm_index * frame_count + jnp.arange(frame_count, dtype=jnp.int32)
    key_pos = tm_index * frame_count - halo_reach + jnp.arange(key_span, dtype=jnp.int32)
    distance = jnp.abs(query_pos[:, None] - key_pos[None, :])
    inside = (key_pos >= 0) & (key_pos < total_frames)
    allowed = (distance[None] <= windows[:, None, None]) & inside[None, None, :]
    allowed = allowed & ((key_pos[None, None, :] < lengths[:, None, None]) | (distance == 0)[None])
    scores = (
        jnp.einsum("cqhd,ckhd->chqk", queries, near_keys, preferred_element_type=jnp.float32)
        * head_scale
    )
    highest, weights, totals = softmax_parts(scores, allowed[:, None])
    context = jnp.einsum(
        "chqk,ckhd->cqhd",
        weights.astype(jnp.bfloat16),
        near_values,
        preferred_element_type=jnp.float32,
    )
    context = context / jnp.transpose(totals, (0, 2, 1))[..., None]
    context = context.astype(jnp.bfloat16).reshape(clip_count * frame_count, model_width)
    mixed_rows = flat_audio.astype(jnp.float32) + jnp.dot(
        context, w_out, preferred_element_type=jnp.float32
    )
    audio_mixed = mixed_rows.astype(jnp.bfloat16).reshape(clip_count, frame_count, model_width)
    in_clip = query_pos[None, :] < lengths[:, None]
    frame_sum = jnp.sum(
        jnp.where(in_clip[:, :, None], audio_mixed.astype(jnp.float32), 0.0), axis=1
    )
    video_flat = video.reshape(clip_count * token_count, video.shape[2])
    query_cols = lax.dynamic_slice_in_dim(w_query, tm_index * local_width, local_width, 1)
    asking = jnp.dot(video_flat, query_cols, preferred_element_type=jnp.float32).astype(
        jnp.bfloat16
    )
    asking = asking.reshape(clip_count, token_count, local_heads, HS)
    far_keys, far_values = (
        lax.all_to_all(
            key_value[:, :, :model_width], "tm", split_axis=2, concat_axis=1, tiled=True
        ),
        lax.all_to_all(
            key_value[:, :, model_width:], "tm", split_axis=2, concat_axis=1, tiled=True
        ),
    )
    far_keys = far_keys.reshape(clip_count, total_frames, local_heads, HS)
    far_values = far_values.reshape(clip_count, total_frames, local_heads, HS)
    frame_valid = jnp.arange(total_frames, dtype=jnp.int32)[None, :] < lengths[:, None]
    cross_scores = (
        jnp.einsum("cqhd,ckhd->chqk", asking, far_keys, preferred_element_type=jnp.float32)
        * head_scale
    )
    cross_peak, cross_weights, cross_totals = softmax_parts(
        cross_scores, frame_valid[:, None, None, :]
    )
    heard_ctx = jnp.einsum(
        "chqk,ckhd->cqhd",
        cross_weights.astype(jnp.bfloat16),
        far_values,
        preferred_element_type=jnp.float32,
    )
    heard_ctx = heard_ctx / jnp.transpose(cross_totals, (0, 2, 1))[..., None]
    video_local = jnp.mean(heard_ctx, axis=1).reshape(clip_count, local_width).astype(jnp.bfloat16)
    embed_rows = lax.dynamic_slice_in_dim(w_video_embed, tm_index * local_width, local_width, 0)
    video_part = jnp.dot(video_local, embed_rows, preferred_element_type=jnp.float32)
    frame_sum, video_part = lax.psum((frame_sum, video_part), "tm")
    audio_pool = (frame_sum / lengths[:, None].astype(jnp.float32)).astype(jnp.bfloat16)
    audio_embed = unit_rows(jnp.dot(audio_pool, w_audio_embed, preferred_element_type=jnp.float32))
    video_embed = unit_rows(video_part)
    logits = (
        LOGIT_SCALE
        * jnp.dot(
            audio_embed,
            lax.all_gather(video_embed, "batch", axis=0, tiled=True).T,
            precision=lax.Precision.HIGHEST,
        )
        + LOGIT_BIAS
    )
    columns = jnp.arange(logits.shape[1], dtype=jnp.int32)
    pair_signs = jnp.where(columns[None, :] == pair_ids[:, None], 1.0, -1.0)
    row_loss = jnp.sum(jnp.logaddexp(0.0, -pair_signs * logits), axis=1)
    return (audio_mixed, audio_embed, video_embed, logits, row_loss)


def solution(mesh):
    in_specs = (
        P("batch", "tm", None),
        P("batch", None, None),
        P("batch"),
        P("batch"),
        P("batch"),
        P(),
        P(),
        P(),
        P(),
        P(),
    )
    out_specs = (
        P("batch", "tm", None),
        P("batch", None),
        P("batch", None),
        P("batch", None),
        P("batch"),
    )
    return jax.shard_map(
        per_device, mesh=mesh, in_specs=in_specs, out_specs=out_specs, check_vma=False
    )
```

profile of v0, /device:TPU:0, one launch (start us, length us, event | category | flops | bytes accessed | tf_op | source)
XLA Modules:
  0.0 123.2 jit_solution(2267838837984791829)
XLA Ops:
  0.6 0.0 copy-start
  0.6 2.0 %copy-done = bf16[768,2304]{1,0:T(8,128)(2,1)S(1)} copy-done((bf16[768,2304]{1,0:T(8,128)(2,1)S(1)}, bf16[768,2304]{1,0:T(8,128)(2,1)}, u32[]{:S(2)}) %copy-start) | copy-done | bytes 3538968
  2.6 3.1 %convolution_convert_fusion = bf16[512,2304]{1,0:T(8,128)(2,1)S(1)} fusion(bf16[512,768]{1,0:T(8,128)(2,1)} %bitcast.73, bf16[768,2304]{1,0:T(8,128)(2,1)S(1)} %copy-done), kind=kOutput, calls=%fused_computation.4 | convolution fusion | flops 1813118976 | bytes 6684672 | tf_op jit(solution)/shard_map/dot_general | solution.py:53
  5.8 0.0 copy-start.1
  5.8 1.0 fusion.47
  6.8 5.6 %collective-permute-start = (bf16[4,32,1536]{2,1,0:T(8,128)(2,1)}, bf16[4,32,1536]{2,1,0:T(8,128)(2,1)}, u32[]{:S(2)}, u32[]{:S(2)}) collective-permute-start(bf16[4,32,1536]{2,1,0:T(8,128)(2,1)} %get-tuple-element.12), channel_id=1, source_target_pairs={{0,1},{2,3},{4,5},{6,7},{8,9},{10,11},{12,13},{14,15},{16,17},{18,... | collective-permute-start | bytes 1179656 | tf_op jit(solution)/shard_map/ppermute | solution.py:20
  12.4 1.3 %collective-permute-start.1 = (bf16[4,32,1536]{2,1,0:T(8,128)(2,1)}, bf16[4,32,1536]{2,1,0:T(8,128)(2,1)}, u32[]{:S(2)}, u32[]{:S(2)}) collective-permute-start(bf16[4,32,1536]{2,1,0:T(8,128)(2,1)} %get-tuple-element.13), channel_id=1, source_target_pairs={{1,0},{3,2},{5,4},{7,6},{9,8},{11,10},{13,12},{15,14},{17,16},{19,... | collective-permute-start | bytes 1179656 | tf_op jit(solution)/shard_map/ppermute | solution.py:23
  13.7 1.5 %fusion.45 = (bf16[4,128,768]{2,1,0:T(8,128)(2,1)}, bf16[4,128,768]{2,1,0:T(8,128)(2,1)}, bf16[4,128,768]{2,1,0:T(8,128)(2,1)}) fusion(bf16[4,128,2304]{2,1,0:T(8,128)(2,1)S(1)} %bitcast.63), kind=kLoop, calls=%fused_computation.69 | loop fusion | bytes 4718592 | tf_op jit(solution)/shard_map/slice | solution.py:95
  15.2 0.0 copy-done.1
  15.2 2.2 %copy.38 = bf16[4,128,768]{1,0,2:T(4,128)(2,1)} copy(bf16[4,128,768]{2,1,0:T(8,128)(2,1)} %get-tuple-element.7) | data formatting | bytes 1572864
  17.3 4.6 %all-to-all-start.1 = ((bf16[4,128,768]{1,0,2:T(4,128)(2,1)}), bf16[4,128,768]{1,0,2:T(4,128)(2,1)}, u32[]{:S(2)}, u32[]{:S(2)}) async-start(bf16[4,128,768]{1,0,2:T(4,128)(2,1)} %copy.38), calls=%async_computation.1 | async-start | bytes 1572864 | tf_op jit(solution)/shard_map/all_to_all | solution.py:94
  22.0 0.7 subtract_abs_fusion
  22.7 0.7 broadcast_compare_fusion
  23.4 0.0 copy-done.9
  23.4 0.1 broadcast_compare_fusion.1
  23.5 0.6 broadcast_compare_fusion.2
  24.1 3.0 %fusion.26 = bf16[512,384]{0,1:T(8,128)(2,1)} fusion(bf16[512,1024]{1,0:T(8,128)(2,1)} %bitcast.72, bf16[1024,768]{1,0:T(8,128)(2,1)} %param.17, s32[]{:T(128)S(6)} %select_n.32), kind=kOutput, calls=%fused_computation.28 | convolution fusion | flops 402849792 | bytes 2228228 | tf_op jit(solution)/shard_map/dot_general | solution.py:89
  27.0 0.1 iota_compare_fusion
  27.1 0.0 copy-done.2
  27.1 1.3 %slice.37 = bf16[4,128,1536]{2,1,0:T(8,128)(2,1)} slice(bf16[4,128,2304]{2,1,0:T(8,128)(2,1)S(1)} %bitcast.64), slice={[0:4], [0:128], [768:2304]} | slice | bytes 3145728 | tf_op jit(solution)/shard_map/slice | solution.py:56
  28.4 0.5 convert_element_type.46
  28.9 2.3 %copy.29 = bf16[4,128,768]{1,2,0:T(8,128)(2,1)} copy(bf16[4,128,768]{2,1,0:T(8,128)(2,1)} %get-tuple-element.9) | data formatting | bytes 1572864 | tf_op jit(solution)/shard_map/slice | solution.py:55
  31.2 1.8 %reshape.231 = bf16[4,128,6,64]{1,0,3,2:T(4,128)(2,1)} reshape(bf16[512,384]{0,1:T(8,128)(2,1)} %fusion.26) | data formatting | bytes 786432 | tf_op jit(solution)/shard_map/reshape | solution.py:92
  33.0 2.2 %copy.37 = bf16[4,128,768]{1,0,2:T(4,128)(2,1)} copy(bf16[4,128,768]{2,1,0:T(8,128)(2,1)} %get-tuple-element.8) | data formatting | bytes 1572864
  35.2 0.0 copy-done.7
  35.2 1.7 %or_and_fusion = pred[4,128,192]{1,2,0:T(8,128)(4,1)} fusion(s32[128,192]{0,1:T(8,128)} %subtract_abs_fusion, s32[4]{0:T(128)S(1)} %copy-done.7, pred[192]{0:T(512)(128)(4,1)S(1)} %compare_and_fusion, pred[128,192]{0,1:T(8,128)(4,1)} %broadcast_compare_fusion, pred[4,192]{1,0:T(4,128)(4,1)S(1)} %broadcast_compare_fusion.1), kind=kLoop, calls=%fused_computation.40 | loop fusion | flops 393216 | bytes 222160 | tf_op jit(solution)/shard_map/and | solution.py:65
  36.9 0.0 collective-permute-done
  37.0 0.0 collective-permute-done.1
  37.0 1.7 %pad_maximum_fusion = bf16[4,192,1536]{2,1,0:T(8,128)(2,1)S(1)} fusion(bf16[4,32,1536]{2,1,0:T(8,128)(2,1)} %collective-permute-done.1, bf16[4,128,1536]{2,1,0:T(8,128)(2,1)} %slice.37, bf16[4,32,1536]{2,1,0:T(8,128)(2,1)} %collective-permute-done), kind=kLoop, calls=%fused_computation.9 | loop fusion | flops 7077888 | bytes 4718592 | tf_op jit(solution)/shard_map/concatenate | solution.py:24
  38.7 1.6 %fusion.46 = (bf16[4,192,768]{2,1,0:T(8,128)(2,1)}, bf16[4,192,768]{2,1,0:T(8,128)(2,1)}) fusion(bf16[4,192,1536]{2,1,0:T(8,128)(2,1)S(1)} %pad_maximum_fusion), kind=kLoop, calls=%fused_computation.70 | loop fusion | bytes 4718592 | tf_op jit(solution)/shard_map/slice | solution.py:58
  40.3 2.5 %copy.30 = bf16[4,192,768]{1,2,0:T(8,128)(2,1)} copy(bf16[4,192,768]{2,1,0:T(8,128)(2,1)} %get-tuple-element.10) | data formatting | bytes 2359296 | tf_op jit(solution)/shard_map/slice | solution.py:58
  42.8 2.5 %copy.28 = bf16[4,192,768]{1,2,0:T(8,128)(2,1)} copy(bf16[4,192,768]{2,1,0:T(8,128)(2,1)} %get-tuple-element.11) | data formatting | bytes 2359296 | tf_op jit(solution)/shard_map/slice | solution.py:59
  45.3 6.0 %fusion.48 = (f32[4,12,128]{2,1,0:T(8,128)}, bf16[4,12,128,192]{2,3,1,0:T(8,128)(2,1)}) fusion(pred[4,128,192]{1,2,0:T(8,128)(4,1)} %or_and_fusion, bf16[4,128,12,64]{1,3,2,0:T(8,128)(2,1)} %bitcast.69, bf16[4,192,12,64]{1,3,2,0:T(8,128)(2,1)} %bitcast.68), kind=kOutput, calls=%fused_computation.72 | convolution fusion | flops 158073024 | bytes 4448256 | tf_op jit(solution)/shard_map/sub | solution.py:31
  51.3 0.0 all-to-all-done.1
  51.3 4.5 %all-to-all-start = ((bf16[4,128,768]{1,0,2:T(4,128)(2,1)}), bf16[4,128,768]{1,0,2:T(4,128)(2,1)}, u32[]{:S(2)}, u32[]{:S(2)}) async-start(bf16[4,128,768]{1,0,2:T(4,128)(2,1)} %copy.37), calls=%async_computation | async-start | bytes 1572864 | tf_op jit(solution)/shard_map/all_to_all | solution.py:97
  55.8 3.1 %fusion.9 = bf16[4,128,12,64]{1,3,2,0:T(8,128)(2,1)S(1)} fusion(bf16[4,192,12,64]{1,3,2,0:T(8,128)(2,1)} %bitcast.67, bf16[4,12,128,192]{2,3,1,0:T(8,128)(2,1)} %get-tuple-element.15, f32[4,128,12]{1,2,0:T(8,128)} %bitcast.75), kind=kOutput, calls=%fused_computation.16 | convolution fusion | flops 151781376 | bytes 4349952 | tf_op jit(solution)/shard_map/chqk,ckhd->cqhd/dot_general | solution.py:71
  58.9 1.5 %copy.31 = bf16[4,128,12,64]{1,0,3,2:T(4,128)(2,1)} copy(bf16[4,128,12,64]{1,3,2,0:T(8,128)(2,1)S(1)} %fusion.9) | data formatting | bytes 1572864 | tf_op jit(solution)/shard_map/convert_element_type | solution.py:78
  60.4 2.8 %copy.48 = bf16[4,128,2,384]{1,2,3,0:T(2,128)(2,1)} copy(bf16[4,128,2,384]{1,0,3,2:T(4,128)(2,1)} %bitcast.12) | data formatting | bytes 1572864 | tf_op jit(solution)/shard_map/all_to_all | solution.py:94
  63.3 3.1 %reshape.232 = bf16[4,256,6,64]{1,3,2,0:T(8,128)(2,1)} reshape(bf16[4,2,128,384]{2,1,3,0:T(2,128)(2,1)} %bitcast.65) | data formatting | bytes 1572864 | tf_op jit(solution)/shard_map/reshape | solution.py:101
  66.4 1.3 %all-to-all-done = bf16[4,128,768]{1,0,2:T(4,128)(2,1)} async-done(((bf16[4,128,768]{1,0,2:T(4,128)(2,1)}), bf16[4,128,768]{1,0,2:T(4,128)(2,1)}, u32[]{:S(2)}, u32[]{:S(2)}) %all-to-all-start) | async-done | bytes 786464 | tf_op jit(solution)/shard_map/all_to_all | solution.py:97
  67.7 2.8 %copy.49 = bf16[4,128,2,384]{1,2,3,0:T(2,128)(2,1)} copy(bf16[4,128,2,384]{1,0,3,2:T(4,128)(2,1)} %bitcast.8) | data formatting | bytes 1572864 | tf_op jit(solution)/shard_map/all_to_all | solution.py:97
  70.5 3.1 %reshape.229 = bf16[4,256,6,64]{1,3,2,0:T(8,128)(2,1)} reshape(bf16[4,2,128,384]{2,1,3,0:T(2,128)(2,1)} %bitcast.66) | data formatting | bytes 1572864 | tf_op jit(solution)/shard_map/reshape | solution.py:102
  73.6 1.9 %fusion.33 = f32[4,6,128,256]{3,2,1,0:T(8,128)S(1)} fusion(bf16[4,256,6,64]{1,3,2,0:T(8,128)(2,1)} %reshape.232, bf16[4,128,6,64]{1,0,3,2:T(4,128)(2,1)} %reshape.231), kind=kOutput, calls=%fused_computation.38 | convolution fusion | flops 100663296 | bytes 4325376 | tf_op jit(solution)/shard_map/cqhd,ckhd->chqk/dot_general | solution.py:105
  75.5 0.0 copy-start.3
  75.5 1.6 %fusion.49 = (f32[4,6,128]{2,1,0:T(8,128)S(1)}, bf16[4,6,128,256]{3,2,1,0:T(8,128)(2,1)S(1)}) fusion(f32[4,6,128,256]{3,2,1,0:T(8,128)S(1)} %fusion.33, pred[4,256]{1,0:T(4,128)(4,1)S(1)} %iota_compare_fusion), kind=kOutput, calls=%fused_computation.73 | output fusion | flops 6291711 | bytes 4731904 | tf_op jit(solution)/shard_map/sub | solution.py:31
  77.1 0.0 copy-done.3
  77.1 0.7 fusion.23
  77.9 0.1 convert_element_type.52
  78.0 2.6 %add_convert_fusion = bf16[512,768]{1,0:T(8,128)(2,1)S(1)} fusion(bf16[512,768]{1,0:T(8,128)(2,1)} %bitcast.74, bf16[768,768]{1,0:T(8,128)(2,1)} %param.16, bf16[96,8,4,128]{3,2,1,0:T(4,128)(2,1)} %bitcast.70), kind=kOutput, calls=%fused_computation.22 | convolution fusion | flops 605159424 | bytes 3538944 | tf_op jit(solution)/shard_map/dot_general | solution.py:79
  80.6 0.0 copy-start.4
  80.6 0.9 copy-done.4
  81.5 0.9 select_reduce_fusion
  82.4 0.0 copy-done.5
  82.4 0.8 fusion.31
  83.2 9.7 %all-reduce = (f32[4,768]{1,0:T(4,128)}, f32[4,768]{1,0:T(4,128)S(1)}) all-reduce(f32[4,768]{1,0:T(4,128)} %select_reduce_fusion, f32[4,768]{1,0:T(4,128)} %fusion.31), channel_id=1, replica_groups=mesh['batch'=16,'tm'=2] {'tm'}, use_global_device_ids=true, to_apply=%region_3.4 | all-reduce | flops 6144 | bytes 49152 | tf_op jit(solution)/shard_map/psum | solution.py:121
  92.9 0.1 multiply_reduce_fusion
  93.0 0.1 fusion.67
  93.1 0.7 broadcast_divide_fusion
  93.8 23.5 %all-gather = f32[16,4,768]{2,1,0:T(4,128)} all-gather(f32[1,4,768]{2,1,0:T(4,128)S(1)} %fusion.67), channel_id=1, replica_groups=mesh['batch'=16,'tm'=2] {'batch'}, dimensions={0}, use_global_device_ids=true | all-gather | bytes 208896 | tf_op jit(solution)/shard_map/all_gather | solution.py:129
  117.3 1.7 %reshape.234 = f32[64,768]{1,0:T(8,128)} reshape(f32[16,4,768]{2,1,0:T(4,128)} %all-gather) | data formatting | bytes 393216
  119.0 1.7 %multiply_reduce_fusion.1 = (f32[4]{0:T(128)S(1)}, f32[4,768]{1,0:T(4,128)S(1)}) fusion(bf16[768,768]{1,0:T(8,128)(2,1)} %param.18, f32[4,768]{1,0:T(4,128)} %get-tuple-element.5, f32[4]{0:T(128)} %convert_element_type.46), kind=kOutput, calls=%fused_computation.46 | convolution fusion | flops 4730876 | bytes 1204256 | tf_op jit(solution)/shard_map/dot_general | solution.py:123
  120.7 0.1 broadcast_divide_fusion.1
  120.8 2.4 %select_reduce_fusion.1 = (f32[4]{0:T(128)}, f32[4,64]{1,0:T(4,128)}) fusion(s32[4]{0:T(128)S(1)} %copy-done.8, f32[4,768]{1,0:T(4,128)S(1)} %broadcast_divide_fusion.1, f32[64,768]{1,0:T(8,128)} %reshape.234), kind=kOutput, calls=%fused_computation.53 | convolution fusion | flops 2362876 | bytes 209952 | tf_op jit(solution)/shard_map/dot_general | solution.py:127
  123.2 0.0 copy-done.6
  (15 shorter events, 0.1 us)
Async XLA Ops:
  0.6 2.0 %copy-start = (bf16[768,2304]{1,0:T(8,128)(2,1)S(1)}, bf16[768,2304]{1,0:T(8,128)(2,1)}, u32[]{:S(2)}) copy-start(bf16[768,2304]{1,0:T(8,128)(2,1)} %param.15) | copy-start | bytes 10616836
  5.8 9.4 %copy-start.1 = (bf16[512,2304]{1,0:T(8,128)(2,1)}, bf16[512,2304]{1,0:T(8,128)(2,1)S(1)}, u32[]{:S(2)}) copy-start(bf16[512,2304]{1,0:T(8,128)(2,1)S(1)} %convolution_convert_fusion) | copy-start | bytes 7077892
  6.8 30.1 %collective-permute-start = (bf16[4,32,1536]{2,1,0:T(8,128)(2,1)}, bf16[4,32,1536]{2,1,0:T(8,128)(2,1)}, u32[]{:S(2)}, u32[]{:S(2)}) collective-permute-start(bf16[4,32,1536]{2,1,0:T(8,128)(2,1)} %get-tuple-element.12), channel_id=1, source_target_pairs={{0,1},{2,3},{4,5},{6,7},{8,9},{10,11},{12,13},{14,15},{16,17},{18,... | collective-permute-start | bytes 1179656 | tf_op jit(solution)/shard_map/ppermute | solution.py:20
  12.4 24.5 %collective-permute-start.1 = (bf16[4,32,1536]{2,1,0:T(8,128)(2,1)}, bf16[4,32,1536]{2,1,0:T(8,128)(2,1)}, u32[]{:S(2)}, u32[]{:S(2)}) collective-permute-start(bf16[4,32,1536]{2,1,0:T(8,128)(2,1)} %get-tuple-element.13), channel_id=1, source_target_pairs={{1,0},{3,2},{5,4},{7,6},{9,8},{11,10},{13,12},{15,14},{17,16},{19,... | collective-permute-start | bytes 1179656 | tf_op jit(solution)/shard_map/ppermute | solution.py:23
  15.2 8.3 %copy-start.9 = (s32[4]{0:T(128)S(1)}, s32[4]{0:T(128)}, u32[]{:S(2)}) copy-start(s32[4]{0:T(128)} %param.14) | copy-start | bytes 52
  17.3 34.0 %all-to-all-start.1 = ((bf16[4,128,768]{1,0,2:T(4,128)(2,1)}), bf16[4,128,768]{1,0,2:T(4,128)(2,1)}, u32[]{:S(2)}, u32[]{:S(2)}) async-start(bf16[4,128,768]{1,0,2:T(4,128)(2,1)} %copy.38), calls=%async_computation.1 | async-start | bytes 1572864 | tf_op jit(solution)/shard_map/all_to_all | solution.py:94
  24.1 3.0 %copy-start.2 = (bf16[512,2304]{1,0:T(8,128)(2,1)S(1)}, bf16[512,2304]{1,0:T(8,128)(2,1)}, u32[]{:S(2)}) copy-start(bf16[512,2304]{1,0:T(8,128)(2,1)} %copy-done.1) | copy-start | bytes 7077892
  28.4 6.8 %copy-start.7 = (s32[4]{0:T(128)S(1)}, s32[4]{0:T(128)}, u32[]{:S(2)}) copy-start(s32[4]{0:T(128)} %param.13) | copy-start | bytes 52
  51.3 16.4 %all-to-all-start = ((bf16[4,128,768]{1,0,2:T(4,128)(2,1)}), bf16[4,128,768]{1,0,2:T(4,128)(2,1)}, u32[]{:S(2)}, u32[]{:S(2)}) async-start(bf16[4,128,768]{1,0,2:T(4,128)(2,1)} %copy.37), calls=%async_computation | async-start | bytes 1572864 | tf_op jit(solution)/shard_map/all_to_all | solution.py:97
  75.5 1.6 %copy-start.3 = (bf16[4,256,6,64]{1,3,2,0:T(8,128)(2,1)S(1)}, bf16[4,256,6,64]{1,3,2,0:T(8,128)(2,1)}, u32[]{:S(2)}) copy-start(bf16[4,256,6,64]{1,3,2,0:T(8,128)(2,1)} %reshape.229) | copy-start | bytes 2359300
  78.0 3.5 %copy-start.10 = (pred[4,128]{1,0:T(4,128)(4,1)S(1)}, pred[4,128]{1,0:T(4,128)(4,1)}, u32[]{:S(2)}) copy-start(pred[4,128]{1,0:T(4,128)(4,1)} %broadcast_compare_fusion.2) | copy-start | bytes 1540
  78.0 4.4 %copy-start.5 = (bf16[768,768]{1,0:T(8,128)(2,1)S(1)}, bf16[768,768]{1,0:T(8,128)(2,1)}, u32[]{:S(2)}) copy-start(bf16[768,768]{1,0:T(8,128)(2,1)} %param.19) | copy-start | bytes 3538948
  80.6 0.9 copy-start.4
  81.5 39.3 %copy-start.8 = (s32[4]{0:T(128)S(1)}, s32[4]{0:T(128)}, u32[]{:S(2)}) copy-start(s32[4]{0:T(128)} %param.12) | copy-start | bytes 52
  120.8 2.4 %copy-start.6 = (f32[4,768]{1,0:T(4,128)}, f32[4,768]{1,0:T(4,128)S(1)}, u32[]{:S(2)}) copy-start(f32[4,768]{1,0:T(4,128)S(1)} %broadcast_divide_fusion.1) | copy-start | bytes 36868
where the time goes:
time: 124 us; the launch traced here: 123 us
  local copies, waits for them, and re-layouts  36.9 us (30%)
  blocking collectives  33.2 us (27%)
  matrix products  25.4 us (20%)
  starting transfers between devices  16 us (13%)
  other arithmetic  9.58 us (8%)
  waiting for transfers between devices  1.31 us (1%)
    all_gather x1, blocking collectives, per_device(): lax.all_gather(video_embed, 'batch', axis=0, tiled=True)  23.5 us
    psum x1, blocking collectives, per_device(): frame_sum, video_part = lax.psum((frame_sum, video_part), 'tm')  9.71 us
    unnamed x25, local copies, waits for them, and re-layouts  8.92 us
    sub x1, matrix products, softmax_parts(): weights = jnp.where(allowed, jnp.exp(scores - highest), 0.0)  6.02 us
    ppermute x1, starting transfers between devices, extended(): lax.ppermute(lax.slice_in_dim(block, block.shape[dim] - width, None, axis...  5.61 us
    all_to_all x1, starting transfers between devices, per_device(): lax.all_to_all(key_value[:, :, :model_width], 'tm', split_axis=2, concat_...  4.64 us
    all_to_all x1, starting transfers between devices, per_device(): lax.all_to_all(key_value[:, :, model_width:], 'tm', split_axis=2, concat_...  4.52 us
    slice x2, local copies, waits for them, and re-layouts, per_device(): near_keys = padded[:, :, :model_width].reshape(clip_count, key_span, HA, HS)  4.07 us
  transfers between devices with their start and end apart: 4, of which 1 were waited for; matrix products, arithmetic and copies ran while one was open for 35% of the time, Pallas kernels for 0%

commit v1 on v0

v1 whole, which is shorter than its diff:
```python
import functools

import jax
import jax.numpy as jnp
from jax import lax
from jax.experimental import pallas as pl
from jax.experimental.pallas import tpu as pltpu
from jax.sharding import PartitionSpec as P

HA = 12
HS = 64
NEG_LARGE = -1e30
LOGIT_SCALE = 10.0
LOGIT_BIAS = -10.0
F32 = jnp.float32
BF16 = jnp.bfloat16
LANES = 128
STAT_ROWS = 16
NT = (((1,), (1,)), ((), ()))
VMEM = pltpu.VMEM
MIB = 1 << 20


def whole(count):
    return [pl.BlockSpec(memory_space=VMEM)] * count


def params(mib):
    return pltpu.CompilerParams(vmem_limit_bytes=mib * MIB)


def cost(flops, moved, exps=0):
    return pl.CostEstimate(flops=flops, bytes_accessed=moved, transcendentals=exps)


def dot_f32(a, b):
    return jnp.dot(a, b, preferred_element_type=F32)


def dot_nt(a, b):
    return lax.dot_general(a, b, NT, preferred_element_type=F32)


def split_heads(rows, scale):
    lane = lax.broadcasted_iota(jnp.int32, (1, LANES), 1)
    low = jnp.where(lane < HS, scale, 0.0).astype(BF16)
    high = jnp.where(lane < HS, 0.0, scale).astype(BF16)
    return jnp.concatenate([rows * low, rows * high], axis=0)


def front_kernel(
    two_sided, lengths, audio_in, video_in, w_qkv, w_query, w_out, w_audio, w_video,
    stats, weights, keys, audio, halo, wq, wk, wv, wout, waudio, wvideo,
    ask_w, video, asking, sems,
):
    clips, frames, width = audio.shape
    tokens = video.shape[1]
    side = halo.shape[2]
    tm = lax.axis_index("tm")
    pairs = [
        (audio_in, audio),
        (w_qkv.at[:, width : 2 * width], wk),
        (w_query, ask_w),
        (video_in, video),
        (w_qkv.at[:, 2 * width : 3 * width], wv),
        (w_qkv.at[:, 0:width], wq),
        (w_out, wout),
        (w_audio, waudio),
        (w_video, wvideo),
    ]
    if two_sided:
        pairs.append((audio_in.at[:, frames - side : frames, :], halo.at[0]))
        pairs.append((audio_in.at[:, 0:side, :], halo.at[1]))
    else:
        start = pl.multiple_of((1 - tm) * (frames - side), side)
        pairs.append((audio_in.at[:, pl.ds(start, side), :], halo.at[0]))
    copies = [pltpu.make_async_copy(src, dst, sems.at[i]) for i, (src, dst) in enumerate(pairs)]
    for copy in copies:
        copy.start()
    copies[0].wait()
    copies[1].wait()
    chunk = 2 * LANES
    flat = audio[...].reshape(clips * frames, width)
    for at in range(0, width, chunk):
        part = dot_f32(flat, wk[:, at : at + chunk]).astype(BF16)
        keys[:, :, at : at + chunk] = part.reshape(clips, frames, chunk)
    copies[2].wait()
    copies[3].wait()
    flat_video = video[...].reshape(clips * tokens, video.shape[2])
    for at in range(0, width, chunk):
        part = dot_f32(flat_video, ask_w[:, at : at + chunk]).astype(BF16)
        asking[:, :, at : at + chunk] = part.reshape(clips, tokens, chunk)

    def one_clip(c, carry):
        place = tm * frames + lax.broadcasted_iota(jnp.int32, (frames, 1), 0)
        valid = place < lengths[c]
        for pair in range(HA // 2):
            cols = slice(pair * LANES, (pair + 1) * LANES)
            both = split_heads(asking[c, :, cols], HS**-0.5)
            scores = jnp.where(valid, dot_nt(keys[c, :, cols], both), NEG_LARGE)
            peak = jnp.max(scores, axis=0, keepdims=True)
            rising = jnp.exp(scores - peak)
            total = jnp.sum(rising, axis=0, keepdims=True)
            weights[c, :, pair * 2 * tokens : (pair + 1) * 2 * tokens] = rising.astype(BF16)
            for k in range(2):
                row = 2 * pair + k
                stats[0, c, row : row + 1, :] = peak[:, k * tokens : (k + 1) * tokens]
                stats[1, c, row : row + 1, :] = total[:, k * tokens : (k + 1) * tokens]
        rest = (STAT_ROWS - HA, tokens)
        stats[0, c, HA:STAT_ROWS, :] = jnp.zeros(rest, F32)
        stats[1, c, HA:STAT_ROWS, :] = jnp.ones(rest, F32)
        return carry

    lax.fori_loop(0, clips, one_clip, 0)
    for copy in copies[4:]:
        copy.wait()


def front(lengths, audio, video, w_qkv, w_query, w_out, w_audio, w_video, two_sided):
    clips, frames, width = audio.shape
    tokens, depth = video.shape[1:]
    side = frames // 4
    square = VMEM((width, width), BF16)
    copies = 11 if two_sided else 10
    return pl.pallas_call(
        functools.partial(front_kernel, two_sided),
        name="front",
        out_shape=[
            VMEM((2, clips, STAT_ROWS, tokens), F32),
            VMEM((clips, frames, HA * tokens), BF16),
            VMEM((clips, frames, width), BF16),
            VMEM((clips, frames, width), BF16),
            VMEM((copies - 9, clips, side, width), BF16),
        ]
        + [square] * 6,
        in_specs=[pl.BlockSpec(memory_space=pltpu.SMEM)] + [pl.BlockSpec(memory_space=pl.ANY)] * 7,
        out_specs=whole(11),
        scratch_shapes=[
            VMEM((depth, width), BF16),
            VMEM((clips, tokens, depth), BF16),
            VMEM((clips, tokens, width), BF16),
            pltpu.SemaphoreType.DMA((copies,)),
        ],
        compiler_params=params(24),
        cost_estimate=cost(2_000_000_000, 12_000_000, 800_000),
    )(lengths, audio, video, w_qkv, w_query, w_out, w_audio, w_video)


def project_kernel(audio, wq, wv, queries, values):
    clips, frames, width = audio.shape
    chunk = 2 * LANES
    flat = audio[...].reshape(clips * frames, width)
    for weight, out in ((wv, values), (wq, queries)):
        for at in range(0, width, chunk):
            part = dot_f32(flat, weight[:, at : at + chunk]).astype(BF16)
            out[:, :, at : at + chunk] = part.reshape(clips, frames, chunk)


def project(audio, wq, wv):
    out = VMEM(audio.shape, BF16)
    return pl.pallas_call(
        project_kernel,
        name="project",
        out_shape=[out, out],
        in_specs=whole(3),
        out_specs=whole(2),
        compiler_params=params(16),
        cost_estimate=cost(1_200_000_000, 5_000_000),
    )(audio, wq, wv)


def pool_kernel(stats, others, weights, values, wvideo, out, pooled):
    clips, frames, width = values.shape
    tokens = stats.shape[3]
    core = lax.rem(lax.axis_index("batch"), 2)
    peak = stats[0]
    for k in range(others.shape[0]):
        peak = jnp.maximum(peak, others[k, 0])
    mine = jnp.exp(stats[0] - peak)
    total = stats[1] * mine
    for k in range(others.shape[0]):
        total = total + others[k, 1] * jnp.exp(others[k, 0] - peak)
    alpha = mine / (total * tokens)
    head = lax.broadcasted_iota(jnp.int32, (STAT_ROWS, tokens), 0)
    owner = lax.broadcasted_iota(jnp.int32, (STAT_ROWS, width), 0)
    lane_head = lax.broadcasted_iota(jnp.int32, (STAT_ROWS, width), 1) // HS
    pooled[...] = jnp.zeros(pooled.shape, F32)
    for c in range(clips):
        spread = jnp.concatenate(
            [jnp.where(head == h, alpha[c], 0.0).astype(BF16) for h in range(HA)], axis=1
        )
        share = dot_nt(spread, weights[c])
        high = share.astype(BF16)
        low = (share - high.astype(F32)).astype(BF16)
        heard = dot_f32(jnp.concatenate([high, low], axis=0), values[c])
        heard = heard[:STAT_ROWS] + heard[STAT_ROWS:]
        row = jnp.sum(jnp.where(owner == lane_head, heard, 0.0), axis=0, keepdims=True)
        pooled[pl.ds(core * clips + c, 1), :] = row
    rows = pooled[...]
    high = rows.astype(BF16)
    low = (rows - high.astype(F32)).astype(BF16)
    both = dot_f32(jnp.concatenate([high, low], axis=0), wvideo[...])
    out[...] = both[: 2 * clips] + both[2 * clips :]


def pool(stats, others, weights, values, wvideo):
    clips, frames, width = values.shape
    return pl.pallas_call(
        pool_kernel,
        name="pool",
        out_shape=VMEM((2 * clips, wvideo.shape[1]), F32),
        in_specs=whole(5),
        out_specs=pl.BlockSpec(memory_space=VMEM),
        scratch_shapes=[VMEM((2 * clips, width), F32)],
        compiler_params=params(16),
        cost_estimate=cost(200_000_000, 2_000_000),
    )(stats, others, weights, values, wvideo)


def attend(two_sided, c, windows, lengths, queries, keys, values, near_k, near_v, ext_k, ext_v, context, to):
    clips, frames, width = queries.shape
    side = frames // 4
    block = 2 * side
    span = 4 * side
    tm = lax.axis_index("tm")
    for own, near, ext in ((keys, near_k, ext_k), (values, near_v, ext_v)):
        if two_sided:
            ext[0:side, :] = near[0, c]
            ext[side : side + frames, :] = own[c]
            ext[side + frames : 2 * side + frames, :] = near[1, c]
        else:
            ext[pl.ds(pl.multiple_of(tm * side, side), frames), :] = own[c]
            ext[pl.ds(pl.multiple_of((1 - tm) * frames, side), side), :] = near[0, c]
    first = tm * frames - side if two_sided else tm * (frames - side)
    last = lax.axis_size("tm") * frames
    lane = lax.broadcasted_iota(jnp.int32, (block, LANES), 1)
    ones = jnp.ones((span, LANES), BF16)
    for b in range(frames // block):
        at = b * block if two_sided else b * side
        key_pos = first + at + lax.broadcasted_iota(jnp.int32, (block, span), 1)
        query_pos = tm * frames + b * block + lax.broadcasted_iota(jnp.int32, (block, span), 0)
        distance = jnp.abs(query_pos - key_pos)
        allowed = (distance <= windows[c]) & ((key_pos < lengths[c]) | (distance == 0))
        if two_sided:
            allowed = allowed & (key_pos >= 0) & (key_pos < last)
        allowed = jnp.concatenate([allowed, allowed], axis=0)
        for pair in range(HA // 2):
            cols = slice(pair * LANES, (pair + 1) * LANES)
            both = split_heads(queries[c, b * block : (b + 1) * block, cols], HS**-0.5)
            scores = jnp.where(allowed, dot_nt(both, ext_k[at : at + span, cols]), NEG_LARGE)
            rising = jnp.exp(scores - jnp.max(scores, axis=1, keepdims=True)).astype(BF16)
            mix = dot_f32(rising, jnp.concatenate([ext_v[at : at + span, cols], ones], axis=1))
            top = jnp.where(lane < HS, mix[:block, :LANES], mix[block:, :LANES])
            total = jnp.where(lane < HS, mix[:block, LANES:], mix[block:, LANES:])
            context[to, b * block : (b + 1) * block, cols] = (top / total).astype(BF16)


def window_first_kernel(
    two_sided, done, windows, lengths, queries, keys, values, near, wk, wv,
    context, near_k, near_v, ext_k, ext_v,
):
    sides, clips, side, width = near.shape
    flat = near[...].reshape(sides * clips * side, width)
    chunk = 2 * LANES
    for weight, out in ((wk, near_k), (wv, near_v)):
        for at in range(0, width, chunk):
            part = dot_f32(flat, weight[:, at : at + chunk]).astype(BF16)
            out[:, :, :, at : at + chunk] = part.reshape(sides, clips, side, chunk)

    def one_clip(c, carry):
        attend(two_sided, c, windows, lengths, queries, keys, values, near_k, near_v, ext_k, ext_v, context, c)
        return carry

    lax.fori_loop(0, done, one_clip, 0)


def ext_scratch(frames, width, two_sided):
    rows = frames + (frames // 4) * (2 if two_sided else 1)
    return [VMEM((rows, width), BF16)] * 2


def window_first(done, windows, lengths, queries, keys, values, near, wk, wv, two_sided):
    clips, frames, width = queries.shape
    smem = pl.BlockSpec(memory_space=pltpu.SMEM)
    return pl.pallas_call(
        functools.partial(window_first_kernel, two_sided, done),
        name="window_first",
        out_shape=[VMEM((done, frames, width), BF16), VMEM(near.shape, BF16), VMEM(near.shape, BF16)],
        in_specs=[smem, smem] + whole(6),
        out_specs=whole(3),
        scratch_shapes=ext_scratch(frames, width, two_sided),
        compiler_params=params(16),
        cost_estimate=cost(1_000_000_000, 5_000_000, 400_000),
    )(windows, lengths, queries, keys, values, near, wk, wv)


def window_last_kernel(
    two_sided, done, windows, lengths, queries, keys, values, near_k, near_v, before, audio, wout,
    mixed, frame_sum, context, ext_k, ext_v,
):
    clips, frames, width = queries.shape
    context[0:done] = before[...]

    def one_clip(c, carry):
        attend(two_sided, c, windows, lengths, queries, keys, values, near_k, near_v, ext_k, ext_v, context, c)
        return carry

    lax.fori_loop(done, clips, one_clip, 0)
    place = lax.axis_index("tm") * frames + lax.broadcasted_iota(jnp.int32, (frames, 1), 0)
    flat = context[...].reshape(clips * frames, width)
    chunk = 2 * LANES
    for at in range(0, width, chunk):
        cols = slice(at, at + chunk)
        part = dot_f32(flat, wout[:, cols]).reshape(clips, frames, chunk)
        part = (audio[:, :, cols].astype(F32) + part).astype(BF16)
        mixed[:, :, cols] = part
        for c in range(clips):
            kept = jnp.where(place < lengths[c], part[c].astype(F32), 0.0)
            frame_sum[c : c + 1, cols] = jnp.sum(kept, axis=0, keepdims=True)


def window_last(done, windows, lengths, queries, keys, values, near_k, near_v, before, audio, wout, two_sided):
    clips, frames, width = queries.shape
    smem = pl.BlockSpec(memory_space=pltpu.SMEM)
    return pl.pallas_call(
        functools.partial(window_last_kernel, two_sided, done),
        name="window_last",
        out_shape=[jax.ShapeDtypeStruct(audio.shape, BF16), VMEM((clips, width), F32)],
        in_specs=[smem, smem] + whole(8),
        out_specs=whole(2),
        scratch_shapes=[VMEM((clips, frames, width), BF16)] + ext_scratch(frames, width, two_sided),
        compiler_params=params(16),
        cost_estimate=cost(1_000_000_000, 5_000_000, 400_000),
    )(windows, lengths, queries, keys, values, near_k, near_v, before, audio, wout)


def unit_rows(matrix):
    return matrix / jnp.sqrt(jnp.sum(matrix * matrix, axis=1, keepdims=True) + 1e-06)


def audio_head_kernel(lengths, mine, other, waudio, out):
    clips = mine.shape[0]
    row = lax.broadcasted_iota(jnp.int32, (clips, 1), 0)
    count = jnp.zeros((clips, 1), F32)
    for c in range(clips):
        count = jnp.where(row == c, lengths[c].astype(F32), count)
    mean = ((mine[...] + other[...]) / count).astype(BF16)
    out[...] = unit_rows(dot_f32(mean, waudio[...]))


def audio_head(lengths, mine, other, waudio):
    return pl.pallas_call(
        audio_head_kernel,
        name="audio_head",
        out_shape=jax.ShapeDtypeStruct((mine.shape[0], waudio.shape[1]), F32),
        in_specs=[pl.BlockSpec(memory_space=pltpu.SMEM)] + whole(3),
        out_specs=pl.BlockSpec(memory_space=VMEM),
        compiler_params=params(8),
        cost_estimate=cost(20_000_000, 1_200_000),
    )(lengths, mine, other, waudio)


def logits_kernel(masks, pair_ids, audio, kept, received, logits, row_loss, video_embed, units):
    clips = audio.shape[0]
    place = lax.axis_index("batch")
    core = lax.rem(place, 2)
    chip = lax.div(place, 2)
    chosen = jnp.where(core == 1, kept[...].astype(F32), received[...].astype(F32))
    chosen = unit_rows(chosen)
    rows = 2 * clips
    for j, mask in enumerate(masks):
        at = pl.multiple_of((chip ^ mask) * rows, rows)
        units[pl.ds(at, rows), :] = chosen[j * rows : (j + 1) * rows]
    own = units[pl.ds(pl.multiple_of(chip * rows, rows), rows), :]
    video_embed[...] = jnp.where(core == 0, own[:clips], own[clips:])
    found = LOGIT_SCALE * lax.dot_general(
        audio[...], units[...], NT, precision=lax.Precision.HIGHEST, preferred_element_type=F32
    )
    found = found + LOGIT_BIAS
    logits[...] = found
    column = lax.broadcasted_iota(jnp.int32, found.shape, 1)
    row = lax.broadcasted_iota(jnp.int32, found.shape, 0)
    wanted = jnp.zeros(found.shape, jnp.int32)
    for c in range(clips):
        wanted = jnp.where(row == c, pair_ids[c], wanted)
    signed = jnp.where(column == wanted, -found, found)
    loss = jnp.maximum(signed, 0.0) + jnp.log1p(jnp.exp(-jnp.abs(signed)))
    loss = jnp.sum(loss, axis=1, keepdims=True)
    square = lax.broadcasted_iota(jnp.int32, (clips, clips), 0) == lax.broadcasted_iota(
        jnp.int32, (clips, clips), 1
    )
    row_loss[...] = jnp.sum(jnp.where(square, loss, 0.0), axis=0, keepdims=True)


def logits_and_loss(masks, pair_ids, audio, kept, received):
    clips, width = audio.shape
    total = kept.shape[0]
    return pl.pallas_call(
        functools.partial(logits_kernel, masks),
        name="logits_and_loss",
        out_shape=[
            jax.ShapeDtypeStruct((clips, total), F32),
            jax.ShapeDtypeStruct((1, clips), F32),
            jax.ShapeDtypeStruct((clips, width), F32),
        ],
        in_specs=[pl.BlockSpec(memory_space=pltpu.SMEM)] + whole(3),
        out_specs=whole(3),
        scratch_shapes=[VMEM((total, width), F32)],
        compiler_params=params(8),
        cost_estimate=cost(20_000_000, 300_000),
    )(pair_ids, audio, kept, received)


def others_on_tm(x):
    count = lax.axis_size("tm")
    moved = [
        lax.ppermute(x, "tm", [(i, (i + shift) % count) for i in range(count)])
        for shift in range(1, count)
    ]
    return jnp.stack(moved)


def swap_tm(x, cores):
    batch = lax.axis_size("batch")
    pairs = [(2 * b + t, 2 * b + 1 - t) for b in range(batch) if b % 2 in cores for t in range(2)]
    return lax.ppermute(x, ("batch", "tm"), pairs)


def gather_video(mine):
    batch = lax.axis_size("batch")
    tm = lax.axis_size("tm")

    def among_cores(x, source):
        return lax.ppermute(x, "batch", [(b, b ^ 1) for b in range(batch) if b % 2 == source])

    def among_chips(x, mask):
        return lax.ppermute(x, "batch", [(b, b ^ (2 * mask)) for b in range(batch) if b % 2 == 1])

    mine = mine + among_cores(mine, 0)
    if tm == 2:
        mine = mine + swap_tm(mine, (1,))
    else:
        mine = lax.psum(mine, "tm")
    held = mine.astype(BF16)
    masks = [0]
    chips = batch // 2
    top = chips
    while top > 1:
        step = 4 if top % 4 == 0 else 2
        top //= step
        moves = [k * top for k in range(1, step)]
        held = jnp.concatenate([held] + [among_chips(held, move) for move in moves], axis=0)
        masks = masks + [mask ^ move for move in moves for mask in masks]
    return held, among_cores(held, 1), masks


def per_device(
    audio, video, pair_ids, windows, lengths, w_qkv, w_out, w_query, w_audio_embed, w_video_embed
):
    clips = audio.shape[0]
    tm = lax.axis_size("tm")
    two_sided = tm > 2
    stats, weights, keys, held_audio, halo, wq, wk, wv, wout, waudio, wvideo = front(
        lengths, audio, video, w_qkv, w_query, w_out, w_audio_embed, w_video_embed, two_sided
    )
    others = others_on_tm(stats)
    if two_sided:
        near = jnp.stack(
            [
                lax.ppermute(halo[0], "tm", [(i, i + 1) for i in range(tm - 1)]),
                lax.ppermute(halo[1], "tm", [(i + 1, i) for i in range(tm - 1)]),
            ]
        )
    else:
        near = swap_tm(halo, (0, 1))
    queries, values = project(held_audio, wq, wv)
    video_part = pool(stats, others, weights, values, wvideo)
    kept, received, masks = gather_video(video_part)
    done = clips // 2
    context, near_k, near_v = window_first(
        done, windows, lengths, queries, keys, values, near, wk, wv, two_sided
    )
    audio_mixed, frame_sum = window_last(
        done, windows, lengths, queries, keys, values, near_k, near_v, context, held_audio, wout, two_sided
    )
    if two_sided:
        frame_sum = lax.psum(frame_sum, "tm")
        other_sum = jnp.zeros_like(frame_sum)
    else:
        other_sum = swap_tm(frame_sum, (0, 1))
    audio_embed = audio_head(lengths, frame_sum, other_sum, waudio)
    logits, row_loss, video_embed = logits_and_loss(masks, pair_ids, audio_embed, kept, received)
    return (audio_mixed, audio_embed, video_embed, logits, row_loss.reshape(clips))


def solution(mesh):
    in_specs = (
        P("batch", "tm", None),
        P("batch", None, None),
        P("batch"),
        P("batch"),
        P("batch"),
        P(),
        P(),
        P(),
        P(),
        P(),
    )
    out_specs = (
        P("batch", "tm", None),
        P("batch", None),
        P("batch", None),
        P("batch", None),
        P("batch"),
    )
    return jax.shard_map(
        per_device, mesh=mesh, in_specs=in_specs, out_specs=out_specs, check_vma=False
    )
```

time: 124 us -> 73 us (0.59)
  the two profiles are of different devices: /device:TPU:0 before, /device:TPU:1 now
where the time goes in v1:
time: 73 us; the launch traced here: 72.4 us
  Pallas kernels  27.5 us (38%)
  starting transfers between devices  23.6 us (32%)
  local copies, waits for them, and re-layouts  11 us (15%)
  waiting for transfers between devices  9.62 us (13%)
  between operations  0.78 us (1%)
    ppermute x4, starting transfers between devices, among_chips(): lax.ppermute(x, 'batch', [(b, b ^ 2 * mask) for b in range(batch) if b %...  12.7 us
    unnamed x25, local copies, waits for them, and re-layouts  10.9 us
    pallas_call x1, Pallas kernels, window_last(): pl.pallas_call(functools.partial(window_last_kernel, two_sided, done), na...  8.3 us
    pallas_call x1, Pallas kernels, window_first(): pl.pallas_call(functools.partial(window_first_kernel, two_sided, done), n...  7 us
    ppermute x3, starting transfers between devices, swap_tm(): return lax.ppermute(x, ('batch', 'tm'), pairs)  6.21 us
    pallas_call x1, Pallas kernels, front(): pl.pallas_call(functools.partial(front_kernel, two_sided), name='front',...  5.79 us
    ppermute x4, waiting for transfers between devices, among_chips(): lax.ppermute(x, 'batch', [(b, b ^ 2 * mask) for b in range(batch) if b %...  4.67 us
    ppermute x2, starting transfers between devices, among_cores(): lax.ppermute(x, 'batch', [(b, b ^ 1) for b in range(batch) if b % 2 == so...  2.58 us
  transfers between devices with their start and end apart: 10, of which 6 were waited for; matrix products, arithmetic and copies ran while one was open for 0% of the time, Pallas kernels for 25%

profile of v1, /device:TPU:1, one launch (start us, length us, event | category | flops | bytes accessed | tf_op | source)
XLA Modules:
  0.0 72.4 jit_solution(4294225219527489259)
XLA Ops:
  0.6 0.0 copy-start
  0.6 2.0 %copy-done = bf16[768,2304]{1,0:T(8,128)(2,1)S(1)} copy-done((bf16[768,2304]{1,0:T(8,128)(2,1)S(1)}, bf16[768,2304]{1,0:T(8,128)(2,1)}, u32[]{:S(2)}) %copy-start) | copy-done | bytes 3538968
  2.6 0.0 copy-start.1
  2.6 1.4 %copy-done.1 = bf16[1024,768]{1,0:T(8,128)(2,1)S(1)} copy-done((bf16[1024,768]{1,0:T(8,128)(2,1)S(1)}, bf16[1024,768]{1,0:T(8,128)(2,1)}, u32[]{:S(2)}) %copy-start.1) | copy-done | bytes 1572888
  4.0 0.0 copy-start.2
  4.0 1.3 %copy-done.2 = bf16[768,768]{1,0:T(8,128)(2,1)S(1)} copy-done((bf16[768,768]{1,0:T(8,128)(2,1)S(1)}, bf16[768,768]{1,0:T(8,128)(2,1)}, u32[]{:S(2)}) %copy-start.2) | copy-done | bytes 1179672
  5.3 0.0 copy-start.3
  5.3 1.3 %copy-done.3 = bf16[768,768]{1,0:T(8,128)(2,1)S(1)} copy-done((bf16[768,768]{1,0:T(8,128)(2,1)S(1)}, bf16[768,768]{1,0:T(8,128)(2,1)}, u32[]{:S(2)}) %copy-start.3) | copy-done | bytes 1179672
  6.6 0.0 copy-start.4
  6.6 1.3 %copy-done.4 = bf16[768,768]{1,0:T(8,128)(2,1)S(1)} copy-done((bf16[768,768]{1,0:T(8,128)(2,1)S(1)}, bf16[768,768]{1,0:T(8,128)(2,1)}, u32[]{:S(2)}) %copy-start.4) | copy-done | bytes 1179672
  7.9 0.0 copy-start.5
  7.9 1.2 %copy-done.5 = bf16[4,128,1024]{2,1,0:T(8,128)(2,1)S(1)} copy-done((bf16[4,128,1024]{2,1,0:T(8,128)(2,1)S(1)}, bf16[4,128,1024]{2,1,0:T(8,128)(2,1)}, u32[]{:S(2)}) %copy-start.5) | copy-done | bytes 1048600
  9.1 0.0 copy-start.6
  9.1 1.1 %copy-done.6 = bf16[4,128,768]{2,1,0:T(8,128)(2,1)S(1)} copy-done((bf16[4,128,768]{2,1,0:T(8,128)(2,1)S(1)}, bf16[4,128,768]{2,1,0:T(8,128)(2,1)}, u32[]{:S(2)}) %copy-start.6) | copy-done | bytes 786456
  10.2 0.0 copy-start.8
  10.2 0.7 copy-done.8
  10.9 5.8 %front.1 = (f32[2,4,16,128]{3,2,1,0:T(8,128)S(1)}, bf16[4,128,1536]{2,1,0:T(8,128)(2,1)S(1)}, bf16[4,128,768]{2,1,0:T(8,128)(2,1)S(1)}, bf16[4,128,768]{2,1,0:T(...) custom-call(s32[4]{0:T(128)S(1)} %copy-done.8, ...), custom_call_target="tpu_custom_call" | custom-call | flops 2000000000 | bytes 12000000 | tf_op jit(solution)/shard_map/front/pallas_call | solution.py:125
  16.7 2.1 %collective-permute-start.2 = (f32[2,4,16,128]{3,2,1,0:T(8,128)S(1)}, f32[2,4,16,128]{3,2,1,0:T(8,128)S(1)}, u32[]{:S(2)}, u32[]{:S(2)}) collective-permute-start(f32[2,4,16,128]{3,2,1,0:T(8,128)S(1)} %get-tuple-element.41.stats), channel_id=1, source_target_pairs={{0,1},{1,0},{2,3},{3,2},{4,5},{5,4},{6,7},{7,6},{8,9},{9,8},{10,11... | collective-permute-start | bytes 196616 | tf_op jit(solution)/shard_map/ppermute | solution.py:417
  18.8 1.4 %project.1 = (bf16[4,128,768]{2,1,0:T(8,128)(2,1)S(1)}, bf16[4,128,768]{2,1,0:T(8,128)(2,1)S(1)}) custom-call(bf16[4,128,768]{2,1,0:T(8,128)(2,1)S(1)} %get-tuple-element.26.audio, bf16[768,768]{1,0:T(8,128)(2,1)S(1)} %get-tuple-element.27.wq, bf16[768,768]{1,0:T(8,128)(2,1)S(1)} %get-tuple-element.28.wv), custom_call_target="tpu_custom_call" | custom-call | flops 1200000000 | bytes 5000000 | tf_op jit(solution)/shard_map/project/pallas_call | solution.py:161
  20.2 0.3 collective-permute-done.2
  20.5 0.0 copy-start.9
  20.5 1.8 %pool.1 = f32[8,768]{1,0:T(8,128)S(1)} custom-call(f32[2,4,16,128]{3,2,1,0:T(8,128)S(1)} %get-tuple-element.41.stats, f32[1,2,4,16,128]{4,3,2,1,0:T(8,128)S(1)} %bitcast.2, bf16[4,128,1536]{2,1,0:T(8,128)(2,1)S(1)} %get-tuple-element.42.weights, bf16[4,128,768]{2,1,0:T(8,128)(2,1)S(1)} %get-tuple-element.31.values, bf16[768,768]{1,0:T(8,128)(2,1)S(1)} %get-tuple-element.43.wvideo), custom_call_target="tpu_custom_call" | custom-call | flops 200000000 | bytes 2000000 | tf_op jit(solution)/shard_map/pool/pallas_call | solution.py:208
  22.3 1.3 %collective-permute-start.3 = (f32[8,768]{1,0:T(8,128)S(1)}, f32[8,768]{1,0:T(8,128)S(1)}, u32[]{:S(2)}, u32[]{:S(2)}) collective-permute-start(f32[8,768]{1,0:T(8,128)S(1)} %pool.1), channel_id=1, source_target_pairs={{0,2},{4,6},{8,10},{12,14},{16,18},{20,22},{24,26},{28,30},{1,3},{... | collective-permute-start | bytes 73736 | tf_op jit(solution)/shard_map/ppermute | solution.py:434
  23.6 2.2 %collective-permute-done.3 = f32[8,768]{1,0:T(8,128)S(1)} collective-permute-done((f32[8,768]{1,0:T(8,128)S(1)}, f32[8,768]{1,0:T(8,128)S(1)}, u32[]{:S(2)}, u32[]{:S(2)}) %collective-permute-start.3) | collective-permute-done | bytes 24608 | tf_op jit(solution)/shard_map/ppermute | solution.py:434
  25.8 3.6 %collective-permute-start.4 = (f32[8,768]{1,0:T(8,128)S(1)}, f32[8,768]{1,0:T(8,128)S(1)}, u32[]{:S(2)}, u32[]{:S(2)}) collective-permute-start(f32[8,768]{1,0:T(8,128)S(1)} %add.6), channel_id=1, source_target_pairs={{2,3},{3,2},{6,7},{7,6},{10,11},{11,10},{14,15},{15,14},{18,19},{1... | collective-permute-start | bytes 73736 | tf_op jit(solution)/shard_map/ppermute | solution.py:426
  29.4 1.2 %collective-permute-done.4 = f32[8,768]{1,0:T(8,128)S(1)} collective-permute-done((f32[8,768]{1,0:T(8,128)S(1)}, f32[8,768]{1,0:T(8,128)S(1)}, u32[]{:S(2)}, u32[]{:S(2)}) %collective-permute-start.4) | collective-permute-done | bytes 24608 | tf_op jit(solution)/shard_map/ppermute | solution.py:426
  30.6 3.4 %collective-permute-start.5 = (bf16[8,768]{1,0:T(8,128)(2,1)S(1)}, bf16[8,768]{1,0:T(8,128)(2,1)S(1)}, u32[]{:S(2)}, u32[]{:S(2)}) collective-permute-start(bf16[8,768]{1,0:T(8,128)(2,1)S(1)} %get-tuple-element.48), channel_id=1, source_target_pairs={{2,10},{6,14},{10,2},{14,6},{18,26},{22,30},{26,18},{30,22},{3,11}... | collective-permute-start | bytes 36872 | tf_op jit(solution)/shard_map/ppermute | solution.py:437
  34.1 4.2 %collective-permute-start.6 = (bf16[8,768]{1,0:T(8,128)(2,1)S(1)}, bf16[8,768]{1,0:T(8,128)(2,1)S(1)}, u32[]{:S(2)}, u32[]{:S(2)}) collective-permute-start(bf16[8,768]{1,0:T(8,128)(2,1)S(1)} %get-tuple-element.48), channel_id=1, source_target_pairs={{2,18},{6,22},{10,26},{14,30},{18,2},{22,6},{26,10},{30,14},{3,19}... | collective-permute-start | bytes 36872 | tf_op jit(solution)/shard_map/ppermute | solution.py:437
  38.3 1.9 %collective-permute-start.7 = (bf16[8,768]{1,0:T(8,128)(2,1)S(1)}, bf16[8,768]{1,0:T(8,128)(2,1)S(1)}, u32[]{:S(2)}, u32[]{:S(2)}) collective-permute-start(bf16[8,768]{1,0:T(8,128)(2,1)S(1)} %get-tuple-element.48), channel_id=1, source_target_pairs={{2,26},{6,30},{10,18},{14,22},{18,10},{22,14},{26,2},{30,6},{3,27}... | collective-permute-start | bytes 36872 | tf_op jit(solution)/shard_map/ppermute | solution.py:437
  40.2 1.3 %collective-permute-start = (bf16[1,4,32,768]{3,2,1,0:T(8,128)(2,1)S(1)}, bf16[1,4,32,768]{3,2,1,0:T(8,128)(2,1)S(1)}, u32[]{:S(2)}, u32[]{:S(2)}) collective-permute-start(bf16[1,4,32,768]{3,2,1,0:T(8,128)(2,1)S(1)} %get-tuple-element.32), channel_id=1, source_target_pairs={{0,1},{1,0},{2,3},{3,2},{4,5},{5,4},{6,7},{7,6},{8,9},{9,8},{10,11... | collective-permute-start | bytes 589832 | tf_op jit(solution)/shard_map/ppermute | solution.py:426
  41.5 0.0 collective-permute-done.5
  41.5 0.0 collective-permute-done.6
  41.5 3.0 %collective-permute-done.7 = bf16[8,768]{1,0:T(8,128)(2,1)S(1)} collective-permute-done((bf16[8,768]{1,0:T(8,128)(2,1)S(1)}, bf16[8,768]{1,0:T(8,128)(2,1)S(1)}, u32[]{:S(2)}, u32[]{:S(2)}) %collective-permute-start.7) | collective-permute-done | bytes 12320 | tf_op jit(solution)/shard_map/ppermute | solution.py:437
  44.5 3.1 %collective-permute-start.8 = (bf16[32,768]{1,0:T(8,128)(2,1)S(1)}, bf16[32,768]{1,0:T(8,128)(2,1)S(1)}, u32[]{:S(2)}, u32[]{:S(2)}) collective-permute-start(bf16[32,768]{1,0:T(8,128)(2,1)S(1)} %pad_maximum_fusion), channel_id=1, source_target_pairs={{2,6},{6,2},{10,14},{14,10},{18,22},{22,18},{26,30},{30,26},{3,7},... | collective-permute-start | bytes 147464 | tf_op jit(solution)/shard_map/ppermute | solution.py:437
  47.7 1.7 %collective-permute-done.8 = bf16[32,768]{1,0:T(8,128)(2,1)S(1)} collective-permute-done((bf16[32,768]{1,0:T(8,128)(2,1)S(1)}, bf16[32,768]{1,0:T(8,128)(2,1)S(1)}, u32[]{:S(2)}, u32[]{:S(2)}) %collective-permute-start.8) | collective-permute-done | bytes 49184 | tf_op jit(solution)/shard_map/ppermute | solution.py:437
  49.3 1.3 %collective-permute-start.9 = (bf16[64,768]{1,0:T(8,128)(2,1)S(1)}, bf16[64,768]{1,0:T(8,128)(2,1)S(1)}, u32[]{:S(2)}, u32[]{:S(2)}) collective-permute-start(bf16[64,768]{1,0:T(8,128)(2,1)S(1)} %constant_dynamic-update-slice_fusion.kept), channel_id=1, source_target_pairs={{2,0},{6,4},{10,8},{14,12},{18,16},{22,20},{26,24},{30,28},{3,1},{... | collective-permute-start | bytes 294920 | tf_op jit(solution)/shard_map/ppermute | solution.py:434
  50.6 0.0 collective-permute-done.near
  50.6 0.0 copy-done.9
  50.7 7.0 %window_first.1 = (bf16[2,128,768]{2,1,0:T(8,128)(2,1)S(1)}, bf16[1,4,32,768]{3,2,1,0:T(8,128)(2,1)S(1)}, bf16[1,4,32,768]{3,2,1,0:T(8,128)(2,1)S(1)}) custom-call(s32[4]{0:T(128)S(1)} %copy-done.9, s32[4]{0:T(128)S(1)} %copy-done.8, bf16[4,128,768]{2,1,0:T(8,128)(2,1)S(1)} %get-tuple-element.29.queries, bf16[4,128,768]{2,1,0:T(8,128)(2,1)S(1)} %get-tuple-element.30.keys, ...), custom_call_target="tpu_custom_call" | custom-call | flops 1000000000 | bytes 5000000 | tf_op jit(solution)/shard_map/window_first/pallas_call | solution.py:285
  57.7 8.3 %window_last.1 = (bf16[4,128,768]{2,1,0:T(8,128)(2,1)}, f32[4,768]{1,0:T(4,128)S(1)}) custom-call(s32[4]{0:T(128)S(1)} %copy-done.9, s32[4]{0:T(128)S(1)} %copy-done.8, bf16[4,128,768]{2,1,0:T(8,128)(2,1)S(1)} %get-tuple-element.29.queries, bf16[4,128,768]{2,1,0:T(8,128)(2,1)S(1)} %get-tuple-element.30.keys, ...), custom_call_target="tpu_custom_call" | custom-call | flops 1000000000 | bytes 5000000 | tf_op jit(solution)/shard_map/window_last/pallas_call | solution.py:325
  66.0 0.0 copy-start.10
  66.0 1.3 %collective-permute-start.1 = (f32[4,768]{1,0:T(4,128)S(1)}, f32[4,768]{1,0:T(4,128)S(1)}, u32[]{:S(2)}, u32[]{:S(2)}) collective-permute-start(f32[4,768]{1,0:T(4,128)S(1)} %get-tuple-element.39.mine), channel_id=1, source_target_pairs={{0,1},{1,0},{2,3},{3,2},{4,5},{5,4},{6,7},{7,6},{8,9},{9,8},{10,11... | collective-permute-start | bytes 36872 | tf_op jit(solution)/shard_map/ppermute | solution.py:426
  67.2 1.3 %collective-permute-done.1.other = f32[4,768]{1,0:T(4,128)S(1)} collective-permute-done((f32[4,768]{1,0:T(4,128)S(1)}, f32[4,768]{1,0:T(4,128)S(1)}, u32[]{:S(2)}, u32[]{:S(2)}) %collective-permute-start.1) | collective-permute-done | bytes 12320 | tf_op jit(solution)/shard_map/ppermute | solution.py:426
  68.5 1.5 %audio_head.1.audio = f32[4,768]{1,0:T(4,128)} custom-call(s32[4]{0:T(128)S(1)} %copy-done.8, f32[4,768]{1,0:T(4,128)S(1)} %get-tuple-element.39.mine, f32[4,768]{1,0:T(4,128)S(1)} %collective-permute-done.1.other, bf16[768,768]{1,0:T(8,128)(2,1)S(1)} %get-tuple-element.40.waudio), custom_call_target="tpu_custom_call" | custom-call | flops 20000000 | bytes 1200000 | tf_op jit(solution)/shard_map/audio_head/pallas_call | solution.py:352
  70.0 0.0 collective-permute-done.9.received
  70.0 0.0 copy-done.10
  70.0 0.0 copy-start.7
  70.0 0.7 copy-done.7
  70.8 1.7 %logits_and_loss.1 = (f32[4,64]{1,0:T(4,128)}, f32[1,4]{1,0:T(1,128)}, f32[4,768]{1,0:T(4,128)}) custom-call(s32[4]{0:T(128)S(1)} %copy-done.10, f32[4,768]{1,0:T(4,128)S(1)} %copy-done.7, bf16[64,768]{1,0:T(8,128)(2,1)S(1)} %constant_dynamic-update-slice_fusion.kept, bf16[64,768]{1,0:T(8,128)(2,1)S(1)} %collective-permute-done.9.received), custom_call_target="tpu_custom_call" | custom-call | flops 20000000 | bytes 300000 | tf_op jit(solution)/shard_map/logits_and_loss/pallas_call | solution.py:398
  (7 shorter events, 0.0 us)
Async XLA Ops:
  0.6 2.0 %copy-start = (bf16[768,2304]{1,0:T(8,128)(2,1)S(1)}, bf16[768,2304]{1,0:T(8,128)(2,1)}, u32[]{:S(2)}) copy-start(bf16[768,2304]{1,0:T(8,128)(2,1)} %w_qkv.1) | copy-start | bytes 10616836
  2.6 1.4 %copy-start.1 = (bf16[1024,768]{1,0:T(8,128)(2,1)S(1)}, bf16[1024,768]{1,0:T(8,128)(2,1)}, u32[]{:S(2)}) copy-start(bf16[1024,768]{1,0:T(8,128)(2,1)} %w_query.1) | copy-start | bytes 4718596
  4.0 1.3 %copy-start.2 = (bf16[768,768]{1,0:T(8,128)(2,1)S(1)}, bf16[768,768]{1,0:T(8,128)(2,1)}, u32[]{:S(2)}) copy-start(bf16[768,768]{1,0:T(8,128)(2,1)} %w_out.1) | copy-start | bytes 3538948
  5.3 1.3 %copy-start.3 = (bf16[768,768]{1,0:T(8,128)(2,1)S(1)}, bf16[768,768]{1,0:T(8,128)(2,1)}, u32[]{:S(2)}) copy-start(bf16[768,768]{1,0:T(8,128)(2,1)} %w_audio.1) | copy-start | bytes 3538948
  6.6 1.3 %copy-start.4 = (bf16[768,768]{1,0:T(8,128)(2,1)S(1)}, bf16[768,768]{1,0:T(8,128)(2,1)}, u32[]{:S(2)}) copy-start(bf16[768,768]{1,0:T(8,128)(2,1)} %w_video.1) | copy-start | bytes 3538948
  7.9 1.2 %copy-start.5 = (bf16[4,128,1024]{2,1,0:T(8,128)(2,1)S(1)}, bf16[4,128,1024]{2,1,0:T(8,128)(2,1)}, u32[]{:S(2)}) copy-start(bf16[4,128,1024]{2,1,0:T(8,128)(2,1)} %video_in.1) | copy-start | bytes 3145732
  9.1 1.1 %copy-start.6 = (bf16[4,128,768]{2,1,0:T(8,128)(2,1)S(1)}, bf16[4,128,768]{2,1,0:T(8,128)(2,1)}, u32[]{:S(2)}) copy-start(bf16[4,128,768]{2,1,0:T(8,128)(2,1)} %audio_in.1) | copy-start | bytes 2359300
  10.2 0.7 copy-start.8
  16.7 3.8 %collective-permute-start.2 = (f32[2,4,16,128]{3,2,1,0:T(8,128)S(1)}, f32[2,4,16,128]{3,2,1,0:T(8,128)S(1)}, u32[]{:S(2)}, u32[]{:S(2)}) collective-permute-start(f32[2,4,16,128]{3,2,1,0:T(8,128)S(1)} %get-tuple-element.41.stats), channel_id=1, source_target_pairs={{0,1},{1,0},{2,3},{3,2},{4,5},{5,4},{6,7},{7,6},{8,9},{9,8},{10,11... | collective-permute-start | bytes 196616 | tf_op jit(solution)/shard_map/ppermute | solution.py:417
  20.5 30.2 %copy-start.9 = (s32[4]{0:T(128)S(1)}, s32[4]{0:T(128)}, u32[]{:S(2)}) copy-start(s32[4]{0:T(128)} %windows.3) | copy-start | bytes 52
  22.3 3.5 %collective-permute-start.3 = (f32[8,768]{1,0:T(8,128)S(1)}, f32[8,768]{1,0:T(8,128)S(1)}, u32[]{:S(2)}, u32[]{:S(2)}) collective-permute-start(f32[8,768]{1,0:T(8,128)S(1)} %pool.1), channel_id=1, source_target_pairs={{0,2},{4,6},{8,10},{12,14},{16,18},{20,22},{24,26},{28,30},{1,3},{... | collective-permute-start | bytes 73736 | tf_op jit(solution)/shard_map/ppermute | solution.py:434
  25.8 4.8 %collective-permute-start.4 = (f32[8,768]{1,0:T(8,128)S(1)}, f32[8,768]{1,0:T(8,128)S(1)}, u32[]{:S(2)}, u32[]{:S(2)}) collective-permute-start(f32[8,768]{1,0:T(8,128)S(1)} %add.6), channel_id=1, source_target_pairs={{2,3},{3,2},{6,7},{7,6},{10,11},{11,10},{14,15},{15,14},{18,19},{1... | collective-permute-start | bytes 73736 | tf_op jit(solution)/shard_map/ppermute | solution.py:426
  30.6 10.9 %collective-permute-start.5 = (bf16[8,768]{1,0:T(8,128)(2,1)S(1)}, bf16[8,768]{1,0:T(8,128)(2,1)S(1)}, u32[]{:S(2)}, u32[]{:S(2)}) collective-permute-start(bf16[8,768]{1,0:T(8,128)(2,1)S(1)} %get-tuple-element.48), channel_id=1, source_target_pairs={{2,10},{6,14},{10,2},{14,6},{18,26},{22,30},{26,18},{30,22},{3,11}... | collective-permute-start | bytes 36872 | tf_op jit(solution)/shard_map/ppermute | solution.py:437
  34.1 7.5 %collective-permute-start.6 = (bf16[8,768]{1,0:T(8,128)(2,1)S(1)}, bf16[8,768]{1,0:T(8,128)(2,1)S(1)}, u32[]{:S(2)}, u32[]{:S(2)}) collective-permute-start(bf16[8,768]{1,0:T(8,128)(2,1)S(1)} %get-tuple-element.48), channel_id=1, source_target_pairs={{2,18},{6,22},{10,26},{14,30},{18,2},{22,6},{26,10},{30,14},{3,19}... | collective-permute-start | bytes 36872 | tf_op jit(solution)/shard_map/ppermute | solution.py:437
  38.3 6.2 %collective-permute-start.7 = (bf16[8,768]{1,0:T(8,128)(2,1)S(1)}, bf16[8,768]{1,0:T(8,128)(2,1)S(1)}, u32[]{:S(2)}, u32[]{:S(2)}) collective-permute-start(bf16[8,768]{1,0:T(8,128)(2,1)S(1)} %get-tuple-element.48), channel_id=1, source_target_pairs={{2,26},{6,30},{10,18},{14,22},{18,10},{22,14},{26,2},{30,6},{3,27}... | collective-permute-start | bytes 36872 | tf_op jit(solution)/shard_map/ppermute | solution.py:437
  40.2 10.4 %collective-permute-start = (bf16[1,4,32,768]{3,2,1,0:T(8,128)(2,1)S(1)}, bf16[1,4,32,768]{3,2,1,0:T(8,128)(2,1)S(1)}, u32[]{:S(2)}, u32[]{:S(2)}) collective-permute-start(bf16[1,4,32,768]{3,2,1,0:T(8,128)(2,1)S(1)} %get-tuple-element.32), channel_id=1, source_target_pairs={{0,1},{1,0},{2,3},{3,2},{4,5},{5,4},{6,7},{7,6},{8,9},{9,8},{10,11... | collective-permute-start | bytes 589832 | tf_op jit(solution)/shard_map/ppermute | solution.py:426
  44.5 4.8 %collective-permute-start.8 = (bf16[32,768]{1,0:T(8,128)(2,1)S(1)}, bf16[32,768]{1,0:T(8,128)(2,1)S(1)}, u32[]{:S(2)}, u32[]{:S(2)}) collective-permute-start(bf16[32,768]{1,0:T(8,128)(2,1)S(1)} %pad_maximum_fusion), channel_id=1, source_target_pairs={{2,6},{6,2},{10,14},{14,10},{18,22},{22,18},{26,30},{30,26},{3,7},... | collective-permute-start | bytes 147464 | tf_op jit(solution)/shard_map/ppermute | solution.py:437
  49.3 20.7 %collective-permute-start.9 = (bf16[64,768]{1,0:T(8,128)(2,1)S(1)}, bf16[64,768]{1,0:T(8,128)(2,1)S(1)}, u32[]{:S(2)}, u32[]{:S(2)}) collective-permute-start(bf16[64,768]{1,0:T(8,128)(2,1)S(1)} %constant_dynamic-update-slice_fusion.kept), channel_id=1, source_target_pairs={{2,0},{6,4},{10,8},{14,12},{18,16},{22,20},{26,24},{30,28},{3,1},{... | collective-permute-start | bytes 294920 | tf_op jit(solution)/shard_map/ppermute | solution.py:434
  66.0 4.1 %copy-start.10 = (s32[4]{0:T(128)S(1)}, s32[4]{0:T(128)}, u32[]{:S(2)}) copy-start(s32[4]{0:T(128)} %pair_ids.1) | copy-start | bytes 52
  66.0 2.5 %collective-permute-start.1 = (f32[4,768]{1,0:T(4,128)S(1)}, f32[4,768]{1,0:T(4,128)S(1)}, u32[]{:S(2)}, u32[]{:S(2)}) collective-permute-start(f32[4,768]{1,0:T(4,128)S(1)} %get-tuple-element.39.mine), channel_id=1, source_target_pairs={{0,1},{1,0},{2,3},{3,2},{4,5},{5,4},{6,7},{7,6},{8,9},{9,8},{10,11... | collective-permute-start | bytes 36872 | tf_op jit(solution)/shard_map/ppermute | solution.py:426
  70.0 0.7 copy-start.7

commit v2 on v1

v2 whole, which is shorter than its diff:
```python
import functools

import jax
import jax.numpy as jnp
from jax import lax
from jax.experimental import pallas as pl
from jax.experimental.pallas import tpu as pltpu
from jax.sharding import PartitionSpec as P

HA = 12
HS = 64
NEG_LARGE = -1e30
LOGIT_SCALE = 10.0
LOGIT_BIAS = -10.0
F32 = jnp.float32
BF16 = jnp.bfloat16
LANES = 128
STAT_ROWS = 16
NT = (((1,), (1,)), ((), ()))
VMEM = pltpu.VMEM
MIB = 1 << 20


def whole(count):
    return [pl.BlockSpec(memory_space=VMEM)] * count


def params(mib):
    return pltpu.CompilerParams(vmem_limit_bytes=mib * MIB)


def cost(flops, moved, exps=0):
    return pl.CostEstimate(flops=flops, bytes_accessed=moved, transcendentals=exps)


def dot_f32(a, b):
    return jnp.dot(a, b, preferred_element_type=F32)


def dot_nt(a, b):
    return lax.dot_general(a, b, NT, preferred_element_type=F32)


def split_heads(rows, scale):
    lane = lax.broadcasted_iota(jnp.int32, (1, LANES), 1)
    low = jnp.where(lane < HS, scale, 0.0).astype(BF16)
    high = jnp.where(lane < HS, 0.0, scale).astype(BF16)
    return jnp.concatenate([rows * low, rows * high], axis=0)


def load_all(pairs, sems):
    copies = [pltpu.make_async_copy(src, dst, sems.at[i]) for i, (src, dst) in enumerate(pairs)]
    for copy in copies:
        copy.start()
    return copies


def front_kernel(
    two_sided, lengths, windows, pair_ids, audio_in, video_in, w_qkv, w_query,
    peaks, spans, info, weights, keys, audio, halo, wq, wk, wv,
    small, ask_w, video, asking, totals, sems,
):
    clips, frames, width = audio.shape
    tokens = video.shape[1]
    side = halo.shape[2]
    tm = lax.axis_index("tm")
    pairs = [
        (lengths, small.at[0]),
        (windows, small.at[1]),
        (pair_ids, small.at[2]),
        (audio_in, audio),
        (w_qkv.at[:, width : 2 * width], wk),
        (video_in, video),
        (w_query, ask_w),
        (w_qkv.at[:, 2 * width : 3 * width], wv),
        (w_qkv.at[:, 0:width], wq),
    ]
    if two_sided:
        pairs.append((audio_in.at[:, frames - side : frames, :], halo.at[0]))
        pairs.append((audio_in.at[:, 0:side, :], halo.at[1]))
    else:
        start = pl.multiple_of((1 - tm) * (frames - side), side)
        pairs.append((audio_in.at[:, pl.ds(start, side), :], halo.at[0]))
    copies = load_all(pairs, sems)
    for copy in copies[:5]:
        copy.wait()
    for k in range(3):
        for c in range(clips):
            info[k, c] = jnp.full(info.shape[2:], small[k, c], jnp.int32)
    chunk = 2 * LANES
    flat = audio[...].reshape(clips * frames, width)
    for at in range(0, width, chunk):
        part = dot_f32(flat, wk[:, at : at + chunk]).astype(BF16)
        keys[:, :, at : at + chunk] = part.reshape(clips, frames, chunk)
    copies[5].wait()
    copies[6].wait()
    flat_video = video[...].reshape(clips * tokens, video.shape[2])
    for at in range(0, width, chunk):
        part = dot_f32(flat_video, ask_w[:, at : at + chunk]).astype(BF16)
        asking[:, :, at : at + chunk] = part.reshape(clips, tokens, chunk)
    place = tm * frames + lax.broadcasted_iota(jnp.int32, (frames, 1), 0)
    columns = [slice(pair * LANES, (pair + 1) * LANES) for pair in range(HA // 2)]
    for c in range(clips):
        valid = place < small[0, c]
        scores = [
            dot_nt(keys[c, :, cols], split_heads(asking[c, :, cols], HS**-0.5)) for cols in columns
        ]
        scores = [jnp.where(valid, s, NEG_LARGE) for s in scores]
        highest = [jnp.max(s, axis=0, keepdims=True) for s in scores]
        rising = [jnp.exp(s - peak) for s, peak in zip(scores, highest)]
        sums = [jnp.sum(r, axis=0, keepdims=True) for r in rising]
        for pair in range(HA // 2):
            weights[c, :, pair * 2 * tokens : (pair + 1) * 2 * tokens] = rising[pair].astype(BF16)
            for k in range(2):
                row = slice(2 * pair + k, 2 * pair + k + 1)
                peaks[c, row, :] = highest[pair][:, k * tokens : (k + 1) * tokens]
                totals[c, row, :] = sums[pair][:, k * tokens : (k + 1) * tokens]
        rest = (STAT_ROWS - HA, tokens)
        peaks[c, HA:STAT_ROWS, :] = jnp.zeros(rest, F32)
        totals[c, HA:STAT_ROWS, :] = jnp.ones(rest, F32)
    spans[...] = peaks[...] + jnp.log(totals[...])
    for copy in copies[7:]:
        copy.wait()


def in_hbm(*arrays):
    return [pltpu.with_memory_space_constraint(x, pltpu.HBM) for x in arrays]


def from_hbm(count):
    return [pl.BlockSpec(memory_space=pltpu.HBM)] * count


def front(lengths, windows, pair_ids, audio, video, w_qkv, w_query, two_sided):
    clips, frames, width = audio.shape
    tokens, depth = video.shape[1:]
    side = frames // 4
    square = VMEM((width, width), BF16)
    sides = 2 if two_sided else 1
    stat = VMEM((clips, STAT_ROWS, tokens), F32)
    return pl.pallas_call(
        functools.partial(front_kernel, two_sided),
        name="front",
        out_shape=[
            stat,
            stat,
            VMEM((3, clips, 8, LANES), jnp.int32),
            VMEM((clips, frames, HA * tokens), BF16),
            VMEM((clips, frames, width), BF16),
            VMEM((clips, frames, width), BF16),
            VMEM((sides, clips, side, width), BF16),
            square,
            square,
            square,
        ],
        in_specs=from_hbm(7),
        out_specs=whole(10),
        scratch_shapes=[
            pltpu.SMEM((3, clips), jnp.int32),
            VMEM((depth, width), BF16),
            VMEM((clips, tokens, depth), BF16),
            VMEM((clips, tokens, width), BF16),
            stat,
            pltpu.SemaphoreType.DMA((9 + sides,)),
        ],
        compiler_params=params(24),
        cost_estimate=cost(2_000_000_000, 8_000_000, 800_000),
    )(*in_hbm(lengths, windows, pair_ids, audio, video, w_qkv, w_query))


def attend(two_sided, tasks, info, queries, keys, values, near_k, near_v, ext_k, ext_v, out):
    clips, frames, width = queries.shape
    side = frames // 4
    block = 2 * side
    span = 4 * side
    tm = lax.axis_index("tm")
    last = lax.axis_size("tm") * frames
    lane = lax.broadcasted_iota(jnp.int32, (block, LANES), 1)
    ones = jnp.ones((span, LANES), BF16)
    columns = [slice(pair * LANES, (pair + 1) * LANES) for pair in range(HA // 2)]
    for i, (c, half) in enumerate(tasks):
        if half == "inner":
            b = tm
            key, value, first = keys.at[c], values.at[c], tm * frames
        else:
            b = 1 - tm if half == "outer" else half
            way = 0 if half == "outer" else half
            key, value = ext_k.at[i % 2], ext_v.at[i % 2]
            first = tm * frames + b * block - side
            for own, near, ext in ((keys, near_k, key), (values, near_v, value)):
                if half == "outer":
                    ext[pl.ds(pl.multiple_of(tm * side, side), 3 * side), :] = own[
                        c, pl.ds(pl.multiple_of((1 - tm) * side, side), 3 * side), :
                    ]
                    ext[pl.ds(pl.multiple_of((1 - tm) * 3 * side, side), side), :] = near[way, c]
                else:
                    ext[(1 - b) * side : (1 - b) * side + 3 * side, :] = own[c, b * side : b * side + 3 * side, :]
                    ext[b * 3 * side : b * 3 * side + side, :] = near[way, c]
        key_pos = first + lax.broadcasted_iota(jnp.int32, (block, span), 1)
        query_pos = tm * frames + b * block + lax.broadcasted_iota(jnp.int32, (block, span), 0)
        distance = jnp.abs(query_pos - key_pos)
        length, window = info[0, c, 0:1, :], info[1, c, 0:1, :]
        allowed = (distance <= window) & ((key_pos < length) | (distance == 0))
        if two_sided:
            allowed = allowed & (key_pos >= 0) & (key_pos < last)
        allowed = jnp.concatenate([allowed, allowed], axis=0)
        rows = pl.ds(pl.multiple_of(b * block, block), block)
        scores = [
            dot_nt(split_heads(queries[c, rows, cols], HS**-0.5), key[:, cols]) for cols in columns
        ]
        scores = [jnp.where(allowed, s, NEG_LARGE) for s in scores]
        highest = [jnp.max(s, axis=1, keepdims=True) for s in scores]
        rising = [jnp.exp(s - peak).astype(BF16) for s, peak in zip(scores, highest)]
        mixes = [
            dot_f32(r, jnp.concatenate([value[:, cols], ones], axis=1))
            for r, cols in zip(rising, columns)
        ]
        for mix, cols in zip(mixes, columns):
            top = jnp.where(lane < HS, mix[:block, :LANES], mix[block:, :LANES])
            total = jnp.where(lane < HS, mix[:block, LANES:], mix[block:, LANES:])
            out[i, :, cols] = (top / total).astype(BF16)


def project_kernel(
    two_sided, tasks, info, audio, keys, wq, wv, w_out, w_audio, w_video,
    queries, values, wout, waudio, wvideo, done, sems,
):
    clips, frames, width = audio.shape
    copies = load_all([(w_video, wvideo), (w_out, wout), (w_audio, waudio)], sems)
    chunk = 2 * LANES
    flat = audio[...].reshape(clips * frames, width)
    for weight, out in ((wv, values), (wq, queries)):
        for at in range(0, width, chunk):
            part = dot_f32(flat, weight[:, at : at + chunk]).astype(BF16)
            out[:, :, at : at + chunk] = part.reshape(clips, frames, chunk)
    attend(two_sided, tasks, info, queries, keys, values, None, None, None, None, done)
    for copy in copies:
        copy.wait()


def context_of(tasks, frames, width):
    return VMEM((max(len(tasks), 1), frames // 2, width), BF16)


def project(two_sided, tasks, info, audio, keys, wq, wv, w_out, w_audio, w_video):
    clips, frames, width = audio.shape
    out = VMEM(audio.shape, BF16)
    square = VMEM((width, width), BF16)
    return pl.pallas_call(
        functools.partial(project_kernel, two_sided, tasks),
        name="project",
        out_shape=[out, out, square, square, square, context_of(tasks, frames, width)],
        in_specs=whole(5) + from_hbm(3),
        out_specs=whole(6),
        scratch_shapes=[pltpu.SemaphoreType.DMA((3,))],
        compiler_params=params(16),
        cost_estimate=cost(1_200_000_000, 5_000_000),
    )(info, audio, keys, wq, wv, *in_hbm(w_out, w_audio, w_video))


def inner_kernel(two_sided, tasks, info, queries, keys, values, done):
    attend(two_sided, tasks, info, queries, keys, values, None, None, None, None, done)


def inner(two_sided, tasks, info, queries, keys, values):
    clips, frames, width = queries.shape
    return pl.pallas_call(
        functools.partial(inner_kernel, two_sided, tasks),
        name="inner",
        out_shape=context_of(tasks, frames, width),
        in_specs=whole(4),
        out_specs=pl.BlockSpec(memory_space=VMEM),
        compiler_params=params(16),
        cost_estimate=cost(300_000_000, 2_000_000, 100_000),
    )(info, queries, keys, values)


def outer_kernel(
    two_sided, tasks, info, queries, keys, values, near, wk, wv, done, near_k, near_v, ext_k, ext_v
):
    sides, clips, side, width = near.shape
    flat = near[...].reshape(sides * clips * side, width)
    chunk = 2 * LANES
    for weight, out in ((wk, near_k), (wv, near_v)):
        for at in range(0, width, chunk):
            part = dot_f32(flat, weight[:, at : at + chunk]).astype(BF16)
            out[:, :, :, at : at + chunk] = part.reshape(sides, clips, side, chunk)
    attend(two_sided, tasks, info, queries, keys, values, near_k, near_v, ext_k, ext_v, done)


def outer(two_sided, tasks, info, queries, keys, values, near, wk, wv):
    clips, frames, width = queries.shape
    beyond = VMEM(near.shape, BF16)
    return pl.pallas_call(
        functools.partial(outer_kernel, two_sided, tasks),
        name="outer",
        out_shape=[context_of(tasks, frames, width), beyond, beyond],
        in_specs=whole(7),
        out_specs=whole(3),
        scratch_shapes=[VMEM((2, frames, width), BF16)] * 2,
        compiler_params=params(16),
        cost_estimate=cost(1_000_000_000, 5_000_000, 400_000),
    )(info, queries, keys, values, near, wk, wv)


def mix_kernel(
    two_sided, plan, info, queries, keys, values, near_k, near_v, audio, wout, *rest
):
    count = len(plan) - 1
    before = rest[:count]
    mixed, frame_sum, context, done, ext_k, ext_v = rest[count:]
    clips, frames, width = queries.shape
    block = frames // 2
    tm = lax.axis_index("tm")
    attend(two_sided, plan[-1], info, queries, keys, values, near_k, near_v, ext_k, ext_v, done)
    for tasks, held in zip(plan, (*before, done)):
        for i, (c, half) in enumerate(tasks):
            b = tm if half == "inner" else 1 - tm if half == "outer" else half
            context[c, pl.ds(pl.multiple_of(b * block, block), block), :] = held[i]
    place = tm * frames + lax.broadcasted_iota(jnp.int32, (frames, 1), 0)
    flat = context[...].reshape(clips * frames, width)
    chunk = 2 * LANES
    for at in range(0, width, chunk):
        cols = slice(at, at + chunk)
        part = dot_f32(flat, wout[:, cols]).reshape(clips, frames, chunk)
        part = (audio[:, :, cols].astype(F32) + part).astype(BF16)
        mixed[:, :, cols] = part
        for c in range(clips):
            kept = jnp.where(place < info[0, c, 0:1, 0:1], part[c].astype(F32), 0.0)
            frame_sum[c : c + 1, cols] = jnp.sum(kept, axis=0, keepdims=True)


def mix(two_sided, plan, info, queries, keys, values, near_k, near_v, audio, wout, before):
    clips, frames, width = queries.shape
    return pl.pallas_call(
        functools.partial(mix_kernel, two_sided, plan),
        name="mix",
        out_shape=[VMEM(audio.shape, BF16), VMEM((clips, width), F32)],
        in_specs=whole(8 + len(before)),
        out_specs=whole(2),
        scratch_shapes=[VMEM((clips, frames, width), BF16), context_of(plan[-1], frames, width)]
        + [VMEM((2, frames, width), BF16)] * 2,
        compiler_params=params(16),
        cost_estimate=cost(1_000_000_000, 5_000_000, 400_000),
    )(info, queries, keys, values, near_k, near_v, audio, wout, *before)


def pool_kernel(peaks, spans, others, weights, values, wvideo, out):
    clips, frames, width = values.shape
    tokens = peaks.shape[2]
    core = lax.rem(lax.axis_index("batch"), 2)
    top = spans[...]
    for k in range(others.shape[0]):
        top = jnp.maximum(top, others[k])
    total = jnp.exp(spans[...] - top)
    for k in range(others.shape[0]):
        total = total + jnp.exp(others[k] - top)
    alpha = jnp.exp(peaks[...] - top) / (total * tokens)
    head = lax.broadcasted_iota(jnp.int32, (STAT_ROWS, tokens), 0)
    owner = lax.broadcasted_iota(jnp.int32, (STAT_ROWS, width), 0)
    lane_head = lax.broadcasted_iota(jnp.int32, (STAT_ROWS, width), 1) // HS
    spread = [
        jnp.concatenate([jnp.where(head == h, alpha[c], 0.0).astype(BF16) for h in range(HA)], axis=1)
        for c in range(clips)
    ]
    share = [dot_nt(spread[c], weights[c]) for c in range(clips)]
    high = [s.astype(BF16) for s in share]
    low = [(s - h.astype(F32)).astype(BF16) for s, h in zip(share, high)]
    heard = [dot_f32(jnp.concatenate([high[c], low[c]], axis=0), values[c]) for c in range(clips)]
    heard = [h[:STAT_ROWS] + h[STAT_ROWS:] for h in heard]
    pooled = jnp.concatenate(
        [jnp.sum(jnp.where(owner == lane_head, h, 0.0), axis=0, keepdims=True) for h in heard], axis=0
    )
    rows = jnp.concatenate(
        [jnp.where(core == 0, pooled, 0.0), jnp.where(core == 0, 0.0, pooled)], axis=0
    )
    high = rows.astype(BF16)
    low = (rows - high.astype(F32)).astype(BF16)
    both = dot_f32(jnp.concatenate([high, low], axis=0), wvideo[...])
    out[...] = both[: 2 * clips] + both[2 * clips :]


def pool(peaks, spans, others, weights, values, wvideo):
    clips, frames, width = values.shape
    return pl.pallas_call(
        pool_kernel,
        name="pool",
        out_shape=VMEM((2 * clips, wvideo.shape[1]), F32),
        in_specs=whole(6),
        out_specs=pl.BlockSpec(memory_space=VMEM),
        compiler_params=params(16),
        cost_estimate=cost(200_000_000, 2_000_000),
    )(peaks, spans, others, weights, values, wvideo)


def unit_rows(matrix):
    return matrix / jnp.sqrt(jnp.sum(matrix * matrix, axis=1, keepdims=True) + 1e-06)


def column_of(info, k):
    return jnp.concatenate([info[k, c, 0:1, 0:1] for c in range(info.shape[1])], axis=0)


def audio_head_kernel(info, mine, other, waudio, out, held):
    mean = ((mine[...] + other[...]) / column_of(info, 0).astype(F32)).astype(BF16)
    found = unit_rows(dot_f32(mean, waudio[...]))
    out[...] = found
    held[...] = found


def audio_head(info, mine, other, waudio):
    shape = (mine.shape[0], waudio.shape[1])
    return pl.pallas_call(
        audio_head_kernel,
        name="audio_head",
        out_shape=[jax.ShapeDtypeStruct(shape, F32), VMEM(shape, F32)],
        in_specs=whole(4),
        out_specs=whole(2),
        compiler_params=params(8),
        cost_estimate=cost(20_000_000, 1_200_000),
    )(info, mine, other, waudio)


def logits_kernel(masks, info, audio, held, logits, row_loss, video_embed, units):
    clips = audio.shape[0]
    place = lax.axis_index("batch")
    core = lax.rem(place, 2)
    chip = lax.div(place, 2)
    found = unit_rows(held[...].astype(F32))
    rows = 2 * clips
    for j, mask in enumerate(masks):
        at = pl.multiple_of((chip ^ mask) * rows, rows)
        units[pl.ds(at, rows), :] = found[j * rows : (j + 1) * rows]
    video_embed[...] = jnp.where(core == 0, found[:clips], found[clips:rows])
    found = LOGIT_SCALE * lax.dot_general(
        audio[...], units[...], NT, precision=lax.Precision.HIGHEST, preferred_element_type=F32
    )
    found = found + LOGIT_BIAS
    logits[...] = found
    column = lax.broadcasted_iota(jnp.int32, found.shape, 1)
    signed = jnp.where(column == column_of(info, 2), -found, found)
    loss = jnp.maximum(signed, 0.0) + jnp.log1p(jnp.exp(-jnp.abs(signed)))
    loss = jnp.sum(loss, axis=1, keepdims=True)
    square = lax.broadcasted_iota(jnp.int32, (clips, clips), 0) == lax.broadcasted_iota(
        jnp.int32, (clips, clips), 1
    )
    row_loss[...] = jnp.sum(jnp.where(square, loss, 0.0), axis=0, keepdims=True)


def logits_and_loss(masks, info, audio, held):
    clips, width = audio.shape
    total = held.shape[0]
    return pl.pallas_call(
        functools.partial(logits_kernel, masks),
        name="logits_and_loss",
        out_shape=[
            jax.ShapeDtypeStruct((clips, total), F32),
            jax.ShapeDtypeStruct((1, clips), F32),
            jax.ShapeDtypeStruct((clips, width), F32),
        ],
        in_specs=whole(3),
        out_specs=whole(3),
        scratch_shapes=[VMEM((total, width), F32)],
        compiler_params=params(8),
        cost_estimate=cost(20_000_000, 300_000),
    )(info, audio, held)


def others_on_tm(x):
    count = lax.axis_size("tm")
    return jnp.stack(
        [
            lax.ppermute(x, "tm", [(i, (i + shift) % count) for i in range(count)])
            for shift in range(1, count)
        ]
    )


def beside(send, operand, work, inputs):
    operand, inputs = lax.optimization_barrier((operand, inputs))
    moved = send(operand)
    return lax.optimization_barrier((moved, work(*inputs)))


def move(x, mask, flip=0):
    batch = lax.axis_size("batch")
    tm = lax.axis_size("tm")
    pairs = [(b * tm + t, (b ^ mask) * tm + (t ^ flip)) for b in range(batch) for t in range(tm)]
    return lax.ppermute(x, ("batch", "tm"), pairs)


def per_device(
    audio, video, pair_ids, windows, lengths, w_qkv, w_out, w_query, w_audio_embed, w_video_embed
):
    clips = audio.shape[0]
    tm = lax.axis_size("tm")
    chips = lax.axis_size("batch") // 2
    two_sided = tm > 2
    if two_sided:
        plan = ((), (), tuple((c, 0) for c in range(clips)), tuple((c, 1) for c in range(clips)))
    else:
        inside = tuple((c, "inner") for c in range(clips))
        outside = tuple((c, "outer") for c in range(clips))
        cut = clips // 2
        plan = (inside[:1], inside[1:2], inside[2:] + outside[:cut], outside[cut:])
    peaks, spans, info, weights, keys, held_audio, halo, wq, wk, wv = front(
        lengths, windows, pair_ids, audio, video, w_qkv, w_query, two_sided
    )
    others = others_on_tm(spans)
    if two_sided:
        near = jnp.stack(
            [
                lax.ppermute(halo[0], "tm", [(i, i + 1) for i in range(tm - 1)]),
                lax.ppermute(halo[1], "tm", [(i + 1, i) for i in range(tm - 1)]),
            ]
        )
    else:
        near = move(halo, 0, 1)
    queries, values, wout, waudio, wvideo, part_a = project(
        two_sided, plan[0], info, held_audio, keys, wq, wv, w_out, w_audio_embed, w_video_embed
    )
    found = pool(peaks, spans, others, weights, values, wvideo)
    local = (info, queries, keys, values)
    if plan[1]:
        moved, part_b = beside(
            lambda x: move(x, 1), found, lambda *held: inner(two_sided, plan[1], *held), local
        )
    else:
        moved, part_b = move(found, 1), part_a
    found = found + moved

    def share(x):
        return lax.psum(x, "tm") if two_sided else x + move(x, 0, 1)

    found, (part_c, near_k, near_v) = beside(
        share, found, lambda *held: outer(two_sided, plan[2], *held), (*local, near, wk, wv)
    )
    held = found.astype(BF16)
    masks = [0]
    top = chips // 2
    moved, (audio_mixed, frame_sum) = beside(
        lambda x: move(x, 2 * top + 1),
        held,
        lambda *held: mix(two_sided, plan, *held[:8], held[8:]),
        (*local, near_k, near_v, held_audio, wout, part_a, part_b, part_c),
    )
    held = jnp.concatenate([held, moved], axis=0)
    masks = masks + [top]
    other_sum = None
    while top > 1:
        step = 4 if top % 4 == 0 else 2
        top //= step
        moves = [k * top for k in range(1, step)]
        held = jnp.concatenate([held] + [move(held, 2 * m + 1) for m in moves], axis=0)
        masks = masks + [mask ^ m for m in moves for mask in masks]
    if two_sided:
        frame_sum = lax.psum(frame_sum, "tm")
        other_sum = jnp.zeros_like(frame_sum)
    else:
        other_sum = move(frame_sum, 0, 1)
    audio_embed, unit_audio = audio_head(info, frame_sum, other_sum, waudio)
    logits, row_loss, video_embed = logits_and_loss(masks, info, unit_audio, held)
    return (audio_mixed, audio_embed, video_embed, logits, row_loss.reshape(clips))


def solution(mesh):
    in_specs = (
        P("batch", "tm", None),
        P("batch", None, None),
        P("batch"),
        P("batch"),
        P("batch"),
        P(),
        P(),
        P(),
        P(),
        P(),
    )
    out_specs = (
        P("batch", "tm", None),
        P("batch", None),
        P("batch", None),
        P("batch", None),
        P("batch"),
    )
    return jax.shard_map(
        per_device, mesh=mesh, in_specs=in_specs, out_specs=out_specs, check_vma=False
    )
```

time: 73 us -> 33.8 us (0.46)
  the two profiles are of different devices: /device:TPU:1 before, /device:TPU:0 now
where the time goes in v2:
time: 33.8 us; the launch traced here: 33.6 us
  Pallas kernels  15.4 us (46%)
  starting transfers between devices  12 us (36%)
  waiting for transfers between devices  4.67 us (14%)
  local copies, waits for them, and re-layouts  0.9 us (3%)
  between operations  0.71 us (2%)
    ppermute x8, starting transfers between devices, move(): return lax.ppermute(x, ('batch', 'tm'), pairs)  11.9 us
    pallas_call x1, Pallas kernels, front(): pl.pallas_call(functools.partial(front_kernel, two_sided), name='front',...  4.77 us
    pallas_call x1, Pallas kernels, project(): pl.pallas_call(functools.partial(project_kernel, two_sided, tasks), name=...  3.36 us
    ppermute x8, waiting for transfers between devices, move(): return lax.ppermute(x, ('batch', 'tm'), pairs)  2.51 us
    ppermute x1, waiting for transfers between devices, others_on_tm(): lax.ppermute(x, 'tm', [(i, (i + shift) % count) for i in range(count)])  2.16 us
    pallas_call x1, Pallas kernels, outer(): pl.pallas_call(functools.partial(outer_kernel, two_sided, tasks), name='o...  1.91 us
    pallas_call x1, Pallas kernels, mix(): pl.pallas_call(functools.partial(mix_kernel, two_sided, plan), name='mix'...  1.72 us
    pallas_call x1, Pallas kernels, logits_and_loss(): pl.pallas_call(functools.partial(logits_kernel, masks), name='logits_and_...  1.1 us
  transfers between devices with their start and end apart: 9, of which 5 were waited for; matrix products, arithmetic and copies ran while one was open for 3% of the time, Pallas kernels for 28%

profile of v2, /device:TPU:0, one launch (start us, length us, event | category | flops | bytes accessed | tf_op | source)
XLA Modules:
  0.0 33.6 jit_solution(6888698744938076592)
XLA Ops:
  0.6 4.8 %front.1 = (f32[4,16,128]{2,1,0:T(8,128)S(1)}, f32[4,16,128]{2,1,0:T(8,128)S(1)}, s32[3,4,8,128]{3,2,1,0:T(8,128)S(1)}, bf16[4,128,1536]{2,1,0:T(8,128)(2,1)S(1)...) custom-call(s32[4]{0:T(128)} %lengths.1, ...), custom_call_target="tpu_custom_call" | custom-call | flops 2000000000 | bytes 8000000 | tf_op jit(solution)/shard_map/front/pallas_call | solution.py:141
  5.4 3.0 %collective-permute-start.2 = (bf16[1,4,32,768]{3,2,1,0:T(8,128)(2,1)S(1)}, bf16[1,4,32,768]{3,2,1,0:T(8,128)(2,1)S(1)}, u32[]{:S(2)}, u32[]{:S(2)}) collective-permute-start(bf16[1,4,32,768]{3,2,1,0:T(8,128)(2,1)S(1)} %get-tuple-element.82), channel_id=1, source_target_pairs={{0,1},{1,0},{2,3},{3,2},{4,5},{5,4},{6,7},{7,6},{8,9},{9,8},{10,11... | collective-permute-start | bytes 589832 | tf_op jit(solution)/shard_map/ppermute | solution.py:489
  8.4 0.1 collective-permute-start
  8.5 3.4 %project.1 = (bf16[4,128,768]{2,1,0:T(8,128)(2,1)S(1)}, bf16[4,128,768]{2,1,0:T(8,128)(2,1)S(1)}, bf16[768,768]{1,0:T(8,128)(2,1)S(1)}, bf16[768,768]{1,0:T(8,12...) custom-call(s32[3,4,8,128]{3,2,1,0:T(8,128)S(1)} %get-tuple-element.103.info, ...), custom_call_target="tpu_custom_call" | custom-call | flops 1200000000 | bytes 5000000 | tf_op jit(solution)/shard_map/project/pallas_call | solution.py:249
  11.9 2.2 %collective-permute-done = f32[4,16,128]{2,1,0:T(8,128)S(1)} collective-permute-done((f32[4,16,128]{2,1,0:T(8,128)S(1)}, f32[4,16,128]{2,1,0:T(8,128)S(1)}, u32[]{:S(2)}, u32[]{:S(2)}) %collective-permute-start) | collective-permute-done | bytes 32800 | tf_op jit(solution)/shard_map/ppermute | solution.py:473
  14.0 1.0 %pool.1 = f32[8,768]{1,0:T(8,128)S(1)} custom-call(f32[4,16,128]{2,1,0:T(8,128)S(1)} %get-tuple-element.65.peaks, f32[4,16,128]{2,1,0:T(8,128)S(1)} %get-tuple-element.66.spans, f32[1,4,16,128]{3,2,1,0:T(8,128)S(1)} %bitcast.2, bf16[4,128,1536]{2,1,0:T(8,128)(2,1)S(1)} %get-tuple-element.67.weights, bf16[4,128,768]{2,1,0:T(8,128)(2,1)S(1)} %get-tuple-element.106.values, ...), custom_call_target="tpu_custom_call" | custom-call | flops 200000000 | bytes 2000000 | tf_op jit(solution)/shard_map/pool/pallas_call | solution.py:385
  15.0 0.0 collective-permute-start.1
  15.0 0.5 %inner.1.rest_1_ = bf16[1,64,768]{2,1,0:T(8,128)(2,1)S(1)} custom-call(s32[3,4,8,128]{3,2,1,0:T(8,128)S(1)} %get-tuple-element.103.info, bf16[4,128,768]{2,1,0:T(8,128)(2,1)S(1)} %get-tuple-element.104.queries, bf16[4,128,768]{2,1,0:T(8,128)(2,1)S(1)} %get-tuple-element.105.keys, bf16[4,128,768]{2,1,0:T(8,128)(2,1)S(1)} %get-tuple-element.106.values), custom_call_target="tpu_custom_call" | custom-call | flops 300000000 | bytes 2000000 | tf_op jit(solution)/shard_map/inner/pallas_call | solution.py:267
  15.5 0.7 %collective-permute-done.1 = f32[8,768]{1,0:T(8,128)S(1)} collective-permute-done((f32[8,768]{1,0:T(8,128)S(1)}, f32[8,768]{1,0:T(8,128)S(1)}, u32[]{:S(2)}, u32[]{:S(2)}) %collective-permute-start.1) | collective-permute-done | bytes 24608 | tf_op jit(solution)/shard_map/ppermute | solution.py:489
  16.2 0.0 collective-permute-done.2.near
  16.2 1.8 %collective-permute-start.3 = (f32[8,768]{1,0:T(8,128)S(1)}, f32[8,768]{1,0:T(8,128)S(1)}, u32[]{:S(2)}, u32[]{:S(2)}) collective-permute-start(f32[8,768]{1,0:T(8,128)S(1)} %add.6), channel_id=1, source_target_pairs={{0,1},{1,0},{2,3},{3,2},{4,5},{5,4},{6,7},{7,6},{8,9},{9,8},{10,11... | collective-permute-start | bytes 73736 | tf_op jit(solution)/shard_map/ppermute | solution.py:489
  18.0 1.9 %outer.1 = (bf16[4,64,768]{2,1,0:T(8,128)(2,1)S(1)}, bf16[1,4,32,768]{3,2,1,0:T(8,128)(2,1)S(1)}, bf16[1,4,32,768]{3,2,1,0:T(8,128)(2,1)S(1)}) custom-call(s32[3,4,8,128]{3,2,1,0:T(8,128)S(1)} %get-tuple-element.103.info, bf16[4,128,768]{2,1,0:T(8,128)(2,1)S(1)} %get-tuple-element.104.queries, bf16[4,128,768]{2,1,0:T(8,128)(2,1)S(1)} %get-tuple-element.105.keys, ...), custom_call_target="tpu_custom_call" | custom-call | flops 1000000000 | bytes 5000000 | tf_op jit(solution)/shard_map/outer/pallas_call | solution.py:294
  20.0 0.2 collective-permute-done.3
  20.1 2.0 %collective-permute-start.4 = (bf16[8,768]{1,0:T(8,128)(2,1)S(1)}, bf16[8,768]{1,0:T(8,128)(2,1)S(1)}, u32[]{:S(2)}, u32[]{:S(2)}) collective-permute-start(bf16[8,768]{1,0:T(8,128)(2,1)S(1)} %add.7), channel_id=1, source_target_pairs={{0,18},{1,19},{2,16},{3,17},{4,22},{5,23},{6,20},{7,21},{8,26},{9,... | collective-permute-start | bytes 36872 | tf_op jit(solution)/shard_map/ppermute | solution.py:489
  22.1 1.7 %mix.1 = (bf16[4,128,768]{2,1,0:T(8,128)(2,1)S(1)}, f32[4,768]{1,0:T(4,128)S(1)}) custom-call(s32[3,4,8,128]{3,2,1,0:T(8,128)S(1)} %get-tuple-element.103.info, bf16[4,128,768]{2,1,0:T(8,128)(2,1)S(1)} %get-tuple-element.104.queries, bf16[4,128,768]{2,1,0:T(8,128)(2,1)S(1)} %get-tuple-element.105.keys, bf16[4,128,768]{2,1,0:T(8,128)(2,1)S(1)} %get-tuple-element.106.values, ...), custom_call_target="tpu_custom_call" | custom-call | flops 1000000000 | bytes 5000000 | tf_op jit(solution)/shard_map/mix/pallas_call | solution.py:335
  23.9 0.4 %collective-permute-done.4 = bf16[8,768]{1,0:T(8,128)(2,1)S(1)} collective-permute-done((bf16[8,768]{1,0:T(8,128)(2,1)S(1)}, bf16[8,768]{1,0:T(8,128)(2,1)S(1)}, u32[]{:S(2)}, u32[]{:S(2)}) %collective-permute-start.4) | collective-permute-done | bytes 12320 | tf_op jit(solution)/shard_map/ppermute | solution.py:489
  24.2 1.8 %collective-permute-start.6 = (bf16[16,768]{1,0:T(8,128)(2,1)S(1)}, bf16[16,768]{1,0:T(8,128)(2,1)S(1)}, u32[]{:S(2)}, u32[]{:S(2)}) collective-permute-start(bf16[16,768]{1,0:T(8,128)(2,1)S(1)} %pad_maximum_fusion), channel_id=1, source_target_pairs={{0,6},{1,7},{2,4},{3,5},{4,2},{5,3},{6,0},{7,1},{8,14},{9,15},{10,... | collective-permute-start | bytes 73736 | tf_op jit(solution)/shard_map/ppermute | solution.py:489
  26.0 1.2 %collective-permute-start.7 = (bf16[16,768]{1,0:T(8,128)(2,1)S(1)}, bf16[16,768]{1,0:T(8,128)(2,1)S(1)}, u32[]{:S(2)}, u32[]{:S(2)}) collective-permute-start(bf16[16,768]{1,0:T(8,128)(2,1)S(1)} %pad_maximum_fusion), channel_id=1, source_target_pairs={{0,10},{1,11},{2,8},{3,9},{4,14},{5,15},{6,12},{7,13},{8,2},{9,3},... | collective-permute-start | bytes 73736 | tf_op jit(solution)/shard_map/ppermute | solution.py:489
  27.2 0.5 %collective-permute-start.8 = (bf16[16,768]{1,0:T(8,128)(2,1)S(1)}, bf16[16,768]{1,0:T(8,128)(2,1)S(1)}, u32[]{:S(2)}, u32[]{:S(2)}) collective-permute-start(bf16[16,768]{1,0:T(8,128)(2,1)S(1)} %pad_maximum_fusion), channel_id=1, source_target_pairs={{0,14},{1,15},{2,12},{3,13},{4,10},{5,11},{6,8},{7,9},{8,6},{9,7},... | collective-permute-start | bytes 73736 | tf_op jit(solution)/shard_map/ppermute | solution.py:489
  27.7 1.5 %collective-permute-start.5 = (f32[4,768]{1,0:T(4,128)S(1)}, f32[4,768]{1,0:T(4,128)S(1)}, u32[]{:S(2)}, u32[]{:S(2)}) collective-permute-start(f32[4,768]{1,0:T(4,128)S(1)} %get-tuple-element.117.mine), channel_id=1, source_target_pairs={{0,1},{1,0},{2,3},{3,2},{4,5},{5,4},{6,7},{7,6},{8,9},{9,8},{10,11... | collective-permute-start | bytes 36872 | tf_op jit(solution)/shard_map/ppermute | solution.py:489
  29.3 0.9 %copy.19 = bf16[4,128,768]{2,1,0:T(8,128)(2,1)} copy(bf16[4,128,768]{2,1,0:T(8,128)(2,1)S(1)} %get-tuple-element.125) | data formatting | bytes 1572864
  30.2 1.3 %collective-permute-done.5.other = f32[4,768]{1,0:T(4,128)S(1)} collective-permute-done((f32[4,768]{1,0:T(4,128)S(1)}, f32[4,768]{1,0:T(4,128)S(1)}, u32[]{:S(2)}, u32[]{:S(2)}) %collective-permute-start.5) | collective-permute-done | bytes 12320 | tf_op jit(solution)/shard_map/ppermute | solution.py:489
  31.4 1.0 %audio_head.1 = (f32[4,768]{1,0:T(4,128)}, f32[4,768]{1,0:T(4,128)S(1)}) custom-call(s32[3,4,8,128]{3,2,1,0:T(8,128)S(1)} %get-tuple-element.103.info, f32[4,768]{1,0:T(4,128)S(1)} %get-tuple-element.117.mine, f32[4,768]{1,0:T(4,128)S(1)} %collective-permute-done.5.other, bf16[768,768]{1,0:T(8,128)(2,1)S(1)} %get-tuple-element.118.waudio), custom_call_target="tpu_custom_call" | custom-call | flops 20000000 | bytes 1200000 | tf_op jit(solution)/shard_map/audio_head/pallas_call | solution.py:413
  32.5 0.0 collective-permute-done.6
  32.5 0.0 collective-permute-done.7
  32.5 0.0 collective-permute-done.8
  32.5 1.1 %logits_and_loss.1 = (f32[4,64]{1,0:T(4,128)}, f32[1,4]{1,0:T(1,128)}, f32[4,768]{1,0:T(4,128)}) custom-call(s32[3,4,8,128]{3,2,1,0:T(8,128)S(1)} %get-tuple-element.103.info, f32[4,768]{1,0:T(4,128)S(1)} %get-tuple-element.120.audio, bf16[64,768]{1,0:T(8,128)(2,1)S(1)} %constant_dynamic-update-slice_fusion.held), custom_call_target="tpu_custom_call" | custom-call | flops 20000000 | bytes 300000 | tf_op jit(solution)/shard_map/logits_and_loss/pallas_call | solution.py:453
  (8 shorter events, 0.0 us)
Async XLA Ops:
  5.4 10.8 %collective-permute-start.2 = (bf16[1,4,32,768]{3,2,1,0:T(8,128)(2,1)S(1)}, bf16[1,4,32,768]{3,2,1,0:T(8,128)(2,1)S(1)}, u32[]{:S(2)}, u32[]{:S(2)}) collective-permute-start(bf16[1,4,32,768]{3,2,1,0:T(8,128)(2,1)S(1)} %get-tuple-element.82), channel_id=1, source_target_pairs={{0,1},{1,0},{2,3},{3,2},{4,5},{5,4},{6,7},{7,6},{8,9},{9,8},{10,11... | collective-permute-start | bytes 589832 | tf_op jit(solution)/shard_map/ppermute | solution.py:489
  8.4 5.6 %collective-permute-start = (f32[4,16,128]{2,1,0:T(8,128)S(1)}, f32[4,16,128]{2,1,0:T(8,128)S(1)}, u32[]{:S(2)}, u32[]{:S(2)}) collective-permute-start(f32[4,16,128]{2,1,0:T(8,128)S(1)} %get-tuple-element.66.spans), channel_id=1, source_target_pairs={{0,1},{1,0},{2,3},{3,2},{4,5},{5,4},{6,7},{7,6},{8,9},{9,8},{10,11... | collective-permute-start | bytes 98312 | tf_op jit(solution)/shard_map/ppermute | solution.py:473
  15.0 1.2 %collective-permute-start.1 = (f32[8,768]{1,0:T(8,128)S(1)}, f32[8,768]{1,0:T(8,128)S(1)}, u32[]{:S(2)}, u32[]{:S(2)}) collective-permute-start(f32[8,768]{1,0:T(8,128)S(1)} %pool.1), channel_id=1, source_target_pairs={{0,2},{1,3},{2,0},{3,1},{4,6},{5,7},{6,4},{7,5},{8,10},{9,11},{10,... | collective-permute-start | bytes 73736 | tf_op jit(solution)/shard_map/ppermute | solution.py:489
  16.2 3.9 %collective-permute-start.3 = (f32[8,768]{1,0:T(8,128)S(1)}, f32[8,768]{1,0:T(8,128)S(1)}, u32[]{:S(2)}, u32[]{:S(2)}) collective-permute-start(f32[8,768]{1,0:T(8,128)S(1)} %add.6), channel_id=1, source_target_pairs={{0,1},{1,0},{2,3},{3,2},{4,5},{5,4},{6,7},{7,6},{8,9},{9,8},{10,11... | collective-permute-start | bytes 73736 | tf_op jit(solution)/shard_map/ppermute | solution.py:489
  20.1 4.1 %collective-permute-start.4 = (bf16[8,768]{1,0:T(8,128)(2,1)S(1)}, bf16[8,768]{1,0:T(8,128)(2,1)S(1)}, u32[]{:S(2)}, u32[]{:S(2)}) collective-permute-start(bf16[8,768]{1,0:T(8,128)(2,1)S(1)} %add.7), channel_id=1, source_target_pairs={{0,18},{1,19},{2,16},{3,17},{4,22},{5,23},{6,20},{7,21},{8,26},{9,... | collective-permute-start | bytes 36872 | tf_op jit(solution)/shard_map/ppermute | solution.py:489
  24.2 8.3 %collective-permute-start.6 = (bf16[16,768]{1,0:T(8,128)(2,1)S(1)}, bf16[16,768]{1,0:T(8,128)(2,1)S(1)}, u32[]{:S(2)}, u32[]{:S(2)}) collective-permute-start(bf16[16,768]{1,0:T(8,128)(2,1)S(1)} %pad_maximum_fusion), channel_id=1, source_target_pairs={{0,6},{1,7},{2,4},{3,5},{4,2},{5,3},{6,0},{7,1},{8,14},{9,15},{10,... | collective-permute-start | bytes 73736 | tf_op jit(solution)/shard_map/ppermute | solution.py:489
  26.0 6.5 %collective-permute-start.7 = (bf16[16,768]{1,0:T(8,128)(2,1)S(1)}, bf16[16,768]{1,0:T(8,128)(2,1)S(1)}, u32[]{:S(2)}, u32[]{:S(2)}) collective-permute-start(bf16[16,768]{1,0:T(8,128)(2,1)S(1)} %pad_maximum_fusion), channel_id=1, source_target_pairs={{0,10},{1,11},{2,8},{3,9},{4,14},{5,15},{6,12},{7,13},{8,2},{9,3},... | collective-permute-start | bytes 73736 | tf_op jit(solution)/shard_map/ppermute | solution.py:489
  27.2 5.3 %collective-permute-start.8 = (bf16[16,768]{1,0:T(8,128)(2,1)S(1)}, bf16[16,768]{1,0:T(8,128)(2,1)S(1)}, u32[]{:S(2)}, u32[]{:S(2)}) collective-permute-start(bf16[16,768]{1,0:T(8,128)(2,1)S(1)} %pad_maximum_fusion), channel_id=1, source_target_pairs={{0,14},{1,15},{2,12},{3,13},{4,10},{5,11},{6,8},{7,9},{8,6},{9,7},... | collective-permute-start | bytes 73736 | tf_op jit(solution)/shard_map/ppermute | solution.py:489
  27.7 3.7 %collective-permute-start.5 = (f32[4,768]{1,0:T(4,128)S(1)}, f32[4,768]{1,0:T(4,128)S(1)}, u32[]{:S(2)}, u32[]{:S(2)}) collective-permute-start(f32[4,768]{1,0:T(4,128)S(1)} %get-tuple-element.117.mine), channel_id=1, source_target_pairs={{0,1},{1,0},{2,3},{3,2},{4,5},{5,4},{6,7},{7,6},{8,9},{9,8},{10,11... | collective-permute-start | bytes 36872 | tf_op jit(solution)/shard_map/ppermute | solution.py:489

commit v3 on v2

--- a/solution.py
+++ b/solution.py
@@ -48,11 +48,34 @@
     return jnp.concatenate([rows * low, rows * high], axis=0)
 
 
+class Pieces:
+    def __init__(self, src, dst, sem, pieces):
+        rows = dst.shape[0] // pieces
+        cuts = [pl.ds(k * rows, rows) for k in range(pieces)]
+        self.copies = [pltpu.make_async_copy(src.at[cut], dst.at[cut], sem) for cut in cuts]
+
+    def start(self):
+        for copy in self.copies:
+            copy.start()
+
+    def wait(self):
+        for copy in self.copies:
+            copy.wait()
+
+
 def load_all(pairs, sems):
-    copies = [pltpu.make_async_copy(src, dst, sems.at[i]) for i, (src, dst) in enumerate(pairs)]
+    copies = [Pieces(src, dst, sems.at[i], pieces) for i, (src, dst, pieces) in enumerate(pairs)]
     for copy in copies:
         copy.start()
     return copies
+
+
+def in_hbm(*arrays):
+    return [pltpu.with_memory_space_constraint(x, pltpu.HBM) for x in arrays]
+
+
+def from_hbm(count):
+    return [pl.BlockSpec(memory_space=pltpu.HBM)] * count
 
 
 def front_kernel(
@@ -63,42 +86,58 @@
     clips, frames, width = audio.shape
     tokens = video.shape[1]
     side = halo.shape[2]
-    tm = lax.axis_index("tm")
-    pairs = [
-        (lengths, small.at[0]),
-        (windows, small.at[1]),
-        (pair_ids, small.at[2]),
-        (audio_in, audio),
-        (w_qkv.at[:, width : 2 * width], wk),
-        (video_in, video),
-        (w_query, ask_w),
-        (w_qkv.at[:, 2 * width : 3 * width], wv),
-        (w_qkv.at[:, 0:width], wq),
-    ]
+    chunk = 2 * LANES
+    cuts = [slice(at, at + chunk) for at in range(0, width, chunk)]
+    count = iter(range(sems.shape[0]))
+
+    def piece(src, dst, pieces=1):
+        return Pieces(src, dst, sems.at[next(count)], pieces)
+
+    def start(copies):
+        for copy in copies:
+            copy.start()
+
+    def wait(copies):
+        for copy in copies:
+            copy.wait()
+
+    ints = [piece(src, small.at[k]) for k, src in enumerate((lengths, windows, pair_ids))]
+    of_audio = piece(audio_in, audio, 2)
+    of_keys = [piece(w_qkv.at[:, width : 2 * width], wk, 2)]
+    of_video = piece(video_in, video, 2)
+    of_asking = [piece(w_query, ask_w, 2)]
+    later = [piece(w_qkv.at[:, 2 * width : 3 * width], wv, 2), piece(w_qkv.at[:, 0:width], wq, 2)]
     if two_sided:
-        pairs.append((audio_in.at[:, frames - side : frames, :], halo.at[0]))
-        pairs.append((audio_in.at[:, 0:side, :], halo.at[1]))
+        later.append(piece(audio_in.at[:, frames - side : frames, :], halo.at[0]))
+        later.append(piece(audio_in.at[:, 0:side, :], halo.at[1]))
     else:
-        start = pl.multiple_of((1 - tm) * (frames - side), side)
-        pairs.append((audio_in.at[:, pl.ds(start, side), :], halo.at[0]))
-    copies = load_all(pairs, sems)
-    for copy in copies[:5]:
-        copy.wait()
+        at = pl.multiple_of((1 - lax.axis_index("tm")) * (frames - side), side)
+        later.append(piece(audio_in.at[:, pl.ds(at, side), :], halo.at[0]))
+
+    def make_keys():
+        of_audio.wait()
+        flat = audio[...].reshape(clips * frames, width)
+        wait(of_keys)
+        for cut in cuts:
+            keys[:, :, cut] = dot_f32(flat, wk[:, cut]).astype(BF16).reshape(clips, frames, chunk)
+
+    def make_asking():
+        of_video.wait()
+        flat = video[...].reshape(clips * tokens, video.shape[2])
+        wait(of_asking)
+        for cut in cuts:
+            asking[:, :, cut] = dot_f32(flat, ask_w[:, cut]).astype(BF16).reshape(clips, tokens, chunk)
+
+    start(ints + [of_audio] + of_keys)
+    wait(ints)
+    start([of_video] + of_asking)
+    make_keys()
+    start(later)
+    make_asking()
     for k in range(3):
         for c in range(clips):
             info[k, c] = jnp.full(info.shape[2:], small[k, c], jnp.int32)
-    chunk = 2 * LANES
-    flat = audio[...].reshape(clips * frames, width)
-    for at in range(0, width, chunk):
-        part = dot_f32(flat, wk[:, at : at + chunk]).astype(BF16)
-        keys[:, :, at : at + chunk] = part.reshape(clips, frames, chunk)
-    copies[5].wait()
-    copies[6].wait()
-    flat_video = video[...].reshape(clips * tokens, video.shape[2])
-    for at in range(0, width, chunk):
-        part = dot_f32(flat_video, ask_w[:, at : at + chunk]).astype(BF16)
-        asking[:, :, at : at + chunk] = part.reshape(clips, tokens, chunk)
-    place = tm * frames + lax.broadcasted_iota(jnp.int32, (frames, 1), 0)
+    place = lax.axis_index("tm") * frames + lax.broadcasted_iota(jnp.int32, (frames, 1), 0)
     columns = [slice(pair * LANES, (pair + 1) * LANES) for pair in range(HA // 2)]
     for c in range(clips):
         valid = place < small[0, c]
@@ -119,22 +158,12 @@
         peaks[c, HA:STAT_ROWS, :] = jnp.zeros(rest, F32)
         totals[c, HA:STAT_ROWS, :] = jnp.ones(rest, F32)
     spans[...] = peaks[...] + jnp.log(totals[...])
-    for copy in copies[7:]:
-        copy.wait()
-
-
-def in_hbm(*arrays):
-    return [pltpu.with_memory_space_constraint(x, pltpu.HBM) for x in arrays]
-
-
-def from_hbm(count):
-    return [pl.BlockSpec(memory_space=pltpu.HBM)] * count
+    wait(later)
 
 
 def front(lengths, windows, pair_ids, audio, video, w_qkv, w_query, two_sided):
     clips, frames, width = audio.shape
     tokens, depth = video.shape[1:]
-    side = frames // 4
     square = VMEM((width, width), BF16)
     sides = 2 if two_sided else 1
     stat = VMEM((clips, STAT_ROWS, tokens), F32)
@@ -148,7 +177,7 @@
             VMEM((clips, frames, HA * tokens), BF16),
             VMEM((clips, frames, width), BF16),
             VMEM((clips, frames, width), BF16),
-            VMEM((sides, clips, side, width), BF16),
+            VMEM((sides, clips, frames // 4, width), BF16),
             square,
             square,
             square,
@@ -161,7 +190,7 @@
             VMEM((clips, tokens, depth), BF16),
             VMEM((clips, tokens, width), BF16),
             stat,
-            pltpu.SemaphoreType.DMA((9 + sides,)),
+            pltpu.SemaphoreType.DMA((7 + sides + 2 * (width // (2 * LANES)),)),
         ],
         compiler_params=params(24),
         cost_estimate=cost(2_000_000_000, 8_000_000, 800_000),
@@ -221,41 +250,52 @@
             out[i, :, cols] = (top / total).astype(BF16)
 
 
-def project_kernel(
-    two_sided, tasks, info, audio, keys, wq, wv, w_out, w_audio, w_video,
-    queries, values, wout, waudio, wvideo, done, sems,
-):
+def project(flat, weight, out):
+    clips, frames, width = out.shape
+    chunk = 2 * LANES
+    for at in range(0, width, chunk):
+        part = dot_f32(flat, weight[:, at : at + chunk]).astype(BF16)
+        out[:, :, at : at + chunk] = part.reshape(clips, frames, chunk)
+
+
+def values_kernel(audio, wv, values):
     clips, frames, width = audio.shape
-    copies = load_all([(w_video, wvideo), (w_out, wout), (w_audio, waudio)], sems)
-    chunk = 2 * LANES
-    flat = audio[...].reshape(clips * frames, width)
-    for weight, out in ((wv, values), (wq, queries)):
-        for at in range(0, width, chunk):
-            part = dot_f32(flat, weight[:, at : at + chunk]).astype(BF16)
-            out[:, :, at : at + chunk] = part.reshape(clips, frames, chunk)
+    project(audio[...].reshape(clips * frames, width), wv, values)
+
+
+def make_values(audio, wv):
+    return pl.pallas_call(
+        values_kernel,
+        name="values",
+        out_shape=VMEM(audio.shape, BF16),
+        in_specs=whole(2),
+        out_specs=pl.BlockSpec(memory_space=VMEM),
+        compiler_params=params(16),
+        cost_estimate=cost(600_000_000, 2_000_000),
+    )(audio, wv)
+
+
+def queries_kernel(two_sided, tasks, info, audio, keys, values, wq, queries, done):
+    clips, frames, width = audio.shape
+    project(audio[...].reshape(clips * frames, width), wq, queries)
     attend(two_sided, tasks, info, queries, keys, values, None, None, None, None, done)
-    for copy in copies:
-        copy.wait()
 
 
 def context_of(tasks, frames, width):
     return VMEM((max(len(tasks), 1), frames // 2, width), BF16)
 
 
-def project(two_sided, tasks, info, audio, keys, wq, wv, w_out, w_audio, w_video):
+def make_queries(two_sided, tasks, info, audio, keys, values, wq):
     clips, frames, width = audio.shape
-    out = VMEM(audio.shape, BF16)
-    square = VMEM((width, width), BF16)
-    return pl.pallas_call(
-        functools.partial(project_kernel, two_sided, tasks),
-        name="project",
-        out_shape=[out, out, square, square, square, context_of(tasks, frames, width)],
-        in_specs=whole(5) + from_hbm(3),
-        out_specs=whole(6),
-        scratch_shapes=[pltpu.SemaphoreType.DMA((3,))],
+    return pl.pallas_call(
+        functools.partial(queries_kernel, two_sided, tasks),
+        name="queries",
+        out_shape=[VMEM(audio.shape, BF16), context_of(tasks, frames, width)],
+        in_specs=whole(5),
+        out_specs=whole(2),
         compiler_params=params(16),
-        cost_estimate=cost(1_200_000_000, 5_000_000),
-    )(info, audio, keys, wq, wv, *in_hbm(w_out, w_audio, w_video))
+        cost_estimate=cost(80_000_000_000, 3_000_000, 100_000),
+    )(info, audio, keys, values, wq)
 
 
 def inner_kernel(two_sided, tasks, info, queries, keys, values, done):
@@ -506,20 +546,20 @@
     peaks, spans, info, weights, keys, held_audio, halo, wq, wk, wv = front(
         lengths, windows, pair_ids, audio, video, w_qkv, w_query, two_sided
     )
+
+    def spread(halo):
+        if not two_sided:
+            return move(halo, 0, 1)
+        upward = lax.ppermute(halo[0], "tm", [(i, i + 1) for i in range(tm - 1)])
+        downward = lax.ppermute(halo[1], "tm", [(i + 1, i) for i in range(tm - 1)])
+        return jnp.stack([upward, downward])
+
+    near = spread(halo)
     others = others_on_tm(spans)
-    if two_sided:
-        near = jnp.stack(
-            [
-                lax.ppermute(halo[0], "tm", [(i, i + 1) for i in range(tm - 1)]),
-                lax.ppermute(halo[1], "tm", [(i + 1, i) for i in range(tm - 1)]),
-            ]
-        )
-    else:
-        near = move(halo, 0, 1)
-    queries, values, wout, waudio, wvideo, part_a = project(
-        two_sided, plan[0], info, held_audio, keys, wq, wv, w_out, w_audio_embed, w_video_embed
-    )
-    found = pool(peaks, spans, others, weights, values, wvideo)
+    values = make_values(held_audio, wv)
+    queries, part_a = make_queries(two_sided, plan[0], info, held_audio, keys, values, wq)
+    others, (queries, part_a) = lax.optimization_barrier((others, (queries, part_a)))
+    found = pool(peaks, spans, others, weights, values, w_video_embed)
     local = (info, queries, keys, values)
     if plan[1]:
         moved, part_b = beside(
@@ -530,7 +570,7 @@
     found = found + moved
 
     def share(x):
-        return lax.psum(x, "tm") if two_sided else x + move(x, 0, 1)
+        return lax.psum(x, "tm") if two_sided else x + move(x, 1, 1)
 
     found, (part_c, near_k, near_v) = beside(
         share, found, lambda *held: outer(two_sided, plan[2], *held), (*local, near, wk, wv)
@@ -542,23 +582,22 @@
         lambda x: move(x, 2 * top + 1),
         held,
         lambda *held: mix(two_sided, plan, *held[:8], held[8:]),
-        (*local, near_k, near_v, held_audio, wout, part_a, part_b, part_c),
+        (*local, near_k, near_v, held_audio, w_out, part_a, part_b, part_c),
     )
     held = jnp.concatenate([held, moved], axis=0)
     masks = masks + [top]
-    other_sum = None
+    if two_sided:
+        frame_sum = lax.psum(frame_sum, "tm")
+        other_sum = jnp.zeros_like(frame_sum)
+    else:
+        other_sum = move(frame_sum, 0, 1)
     while top > 1:
         step = 4 if top % 4 == 0 else 2
         top //= step
         moves = [k * top for k in range(1, step)]
         held = jnp.concatenate([held] + [move(held, 2 * m + 1) for m in moves], axis=0)
         masks = masks + [mask ^ m for m in moves for mask in masks]
-    if two_sided:
-        frame_sum = lax.psum(frame_sum, "tm")
-        other_sum = jnp.zeros_like(frame_sum)
-    else:
-        other_sum = move(frame_sum, 0, 1)
-    audio_embed, unit_audio = audio_head(info, frame_sum, other_sum, waudio)
+    audio_embed, unit_audio = audio_head(info, frame_sum, other_sum, w_audio_embed)
     logits, row_loss, video_embed = logits_and_loss(masks, info, unit_audio, held)
     return (audio_mixed, audio_embed, video_embed, logits, row_loss.reshape(clips))
 

time: 33.8 us -> 31.8 us (0.941)
  starting transfers between devices: 12 us -> 9.58 us
  waiting for transfers between devices: 4.67 us -> 6.24 us
  Pallas kernels: 15.4 us -> 14.2 us
    ppermute x8, starting transfers between devices: 11.9 us -> 6.55 us  [move(): return lax.ppermute(x, ('batch', 'tm'), pairs)]
    ppermute x8, waiting for transfers between devices: 2.51 us -> 6.24 us  [move(): return lax.ppermute(x, ('batch', 'tm'), pairs)]
    ppermute x1, starting transfers between devices: 0.08 us -> 3.03 us  [others_on_tm(): lax.ppermute(x, 'tm', [(i, (i + shift) % count) for i in range(count)])]
    ppermute x1, waiting for transfers between devices: 2.16 us -> 0.01 us  [others_on_tm(): lax.ppermute(x, 'tm', [(i, (i + shift) % count) for i in range(count)])]
    pallas_call x1 -> x2, Pallas kernels: 3.36 us -> 2.07 us  [the longest x1 1.29 us: make_queries(): pl.pallas_call(functools.partial(queries_kernel, two_sided, tasks), name=...]
    unnamed x5 -> x11, local copies, waits for them, and re-layouts: 0.89 us -> 0.91 us
  transfers between devices with their start and end apart: 9 -> 9, of which waited for: 5 -> 5; matrix products, arithmetic and copies ran while one was open for 3% -> 3% of each run, Pallas kernels for 28% -> 26%
where the time goes in v3:
time: 31.8 us; the launch traced here: 31.7 us
  Pallas kernels  14.2 us (45%)
  starting transfers between devices  9.58 us (30%)
  waiting for transfers between devices  6.24 us (20%)
  local copies, waits for them, and re-layouts  0.91 us (3%)
  between operations  0.75 us (2%)
    ppermute x8, starting transfers between devices, move(): return lax.ppermute(x, ('batch', 'tm'), pairs)  6.55 us
    ppermute x8, waiting for transfers between devices, move(): return lax.ppermute(x, ('batch', 'tm'), pairs)  6.24 us
    pallas_call x1, Pallas kernels, front(): pl.pallas_call(functools.partial(front_kernel, two_sided), name='front',...  4.83 us
    ppermute x1, starting transfers between devices, others_on_tm(): lax.ppermute(x, 'tm', [(i, (i + shift) % count) for i in range(count)])  3.03 us
    pallas_call x1, Pallas kernels, outer(): pl.pallas_call(functools.partial(outer_kernel, two_sided, tasks), name='o...  1.92 us
    pallas_call x1, Pallas kernels, mix(): pl.pallas_call(functools.partial(mix_kernel, two_sided, plan), name='mix'...  1.71 us
    pallas_call x1, Pallas kernels, make_queries(): pl.pallas_call(functools.partial(queries_kernel, two_sided, tasks), name=...  1.29 us
    pallas_call x1, Pallas kernels, logits_and_loss(): pl.pallas_call(functools.partial(logits_kernel, masks), name='logits_and_...  1.1 us
  transfers between devices with their start and end apart: 9, of which 5 were waited for; matrix products, arithmetic and copies ran while one was open for 3% of the time, Pallas kernels for 26%

profile of v3, /device:TPU:0, one launch (start us, length us, event | category | flops | bytes accessed | tf_op | source)
XLA Modules:
  0.0 31.7 jit_solution(7194451431495190664)
XLA Ops:
  0.6 4.8 %front.1 = (f32[4,16,128]{2,1,0:T(8,128)S(1)}, f32[4,16,128]{2,1,0:T(8,128)S(1)}, s32[3,4,8,128]{3,2,1,0:T(8,128)S(1)}, bf16[4,128,1536]{2,1,0:T(8,128)(2,1)S(1)...) custom-call(s32[4]{0:T(128)} %lengths.1, ...), custom_call_target="tpu_custom_call" | custom-call | flops 2000000000 | bytes 8000000 | tf_op jit(solution)/shard_map/front/pallas_call | solution.py:170
  5.5 3.0 %collective-permute-start = (f32[4,16,128]{2,1,0:T(8,128)S(1)}, f32[4,16,128]{2,1,0:T(8,128)S(1)}, u32[]{:S(2)}, u32[]{:S(2)}) collective-permute-start(f32[4,16,128]{2,1,0:T(8,128)S(1)} %get-tuple-element.65.spans), channel_id=1, source_target_pairs={{0,1},{1,0},{2,3},{3,2},{4,5},{5,4},{6,7},{7,6},{8,9},{9,8},{10,11... | collective-permute-start | bytes 98312 | tf_op jit(solution)/shard_map/ppermute | solution.py:513
  8.5 0.1 collective-permute-start.2
  8.6 0.8 %values.1 = bf16[4,128,768]{2,1,0:T(8,128)(2,1)S(1)} custom-call(bf16[4,128,768]{2,1,0:T(8,128)(2,1)S(1)} %get-tuple-element.108.audio, bf16[768,768]{1,0:T(8,128)(2,1)S(1)} %get-tuple-element.91.wv), custom_call_target="tpu_custom_call" | custom-call | flops 600000000 | bytes 2000000 | tf_op jit(solution)/shard_map/values/pallas_call | solution.py:267
  9.4 0.0 copy-start
  9.4 1.3 %queries.1 = (bf16[4,128,768]{2,1,0:T(8,128)(2,1)S(1)}, bf16[1,64,768]{2,1,0:T(8,128)(2,1)S(1)}) custom-call(s32[3,4,8,128]{3,2,1,0:T(8,128)S(1)} %get-tuple-element.102.info, bf16[4,128,768]{2,1,0:T(8,128)(2,1)S(1)} %get-tuple-element.108.audio, bf16[4,128,768]{2,1,0:T(8,128)(2,1)S(1)} %get-tuple-element.104.keys, bf16[4,128,768]{2,1,0:T(8,128)(2,1)S(1)} %values.1, ...), custom_call_target="tpu_custom_call" | custom-call | flops 80000000000 | bytes 3000000 | tf_op jit(solution)/shard_map/queries/pallas_call | solution.py:290
  10.7 0.0 collective-permute-done
  10.7 0.0 copy-done
  10.7 1.0 %pool.1 = f32[8,768]{1,0:T(8,128)S(1)} custom-call(f32[4,16,128]{2,1,0:T(8,128)S(1)} %get-tuple-element.64.peaks, f32[4,16,128]{2,1,0:T(8,128)S(1)} %get-tuple-element.65.spans, f32[1,4,16,128]{3,2,1,0:T(8,128)S(1)} %bitcast.2, bf16[4,128,1536]{2,1,0:T(8,128)(2,1)S(1)} %get-tuple-element.74.weights, bf16[4,128,768]{2,1,0:T(8,128)(2,1)S(1)} %values.1, ...), custom_call_target="tpu_custom_call" | custom-call | flops 200000000 | bytes 2000000 | tf_op jit(solution)/shard_map/pool/pallas_call | solution.py:425
  11.7 0.0 collective-permute-start.1
  11.7 0.5 %inner.1.rest_1_ = bf16[1,64,768]{2,1,0:T(8,128)(2,1)S(1)} custom-call(s32[3,4,8,128]{3,2,1,0:T(8,128)S(1)} %get-tuple-element.102.info, bf16[4,128,768]{2,1,0:T(8,128)(2,1)S(1)} %get-tuple-element.103.queries, bf16[4,128,768]{2,1,0:T(8,128)(2,1)S(1)} %get-tuple-element.104.keys, bf16[4,128,768]{2,1,0:T(8,128)(2,1)S(1)} %values.1), custom_call_target="tpu_custom_call" | custom-call | flops 300000000 | bytes 2000000 | tf_op jit(solution)/shard_map/inner/pallas_call | solution.py:307
  12.2 0.7 %collective-permute-done.1 = f32[8,768]{1,0:T(8,128)S(1)} collective-permute-done((f32[8,768]{1,0:T(8,128)S(1)}, f32[8,768]{1,0:T(8,128)S(1)}, u32[]{:S(2)}, u32[]{:S(2)}) %collective-permute-start.1) | collective-permute-done | bytes 24608 | tf_op jit(solution)/shard_map/ppermute | solution.py:529
  12.9 2.0 %collective-permute-done.2.near = bf16[1,4,32,768]{3,2,1,0:T(8,128)(2,1)S(1)} collective-permute-done((bf16[1,4,32,768]{3,2,1,0:T(8,128)(2,1)S(1)}, bf16[1,4,32,768]{3,2,1,0:T(8,128)(2,1)S(1)}, u32[]{:S(2)}, u32[]{:S(2)}) %collective-permute-start.2) | collective-permute-done | bytes 196640 | tf_op jit(solution)/shard_map/ppermute | solution.py:529
  14.9 0.0 copy-start.2
  14.9 0.0 collective-permute-start.3
  14.9 1.9 %outer.1 = (bf16[4,64,768]{2,1,0:T(8,128)(2,1)S(1)}, bf16[1,4,32,768]{3,2,1,0:T(8,128)(2,1)S(1)}, bf16[1,4,32,768]{3,2,1,0:T(8,128)(2,1)S(1)}) custom-call(s32[3,4,8,128]{3,2,1,0:T(8,128)S(1)} %get-tuple-element.102.info, bf16[4,128,768]{2,1,0:T(8,128)(2,1)S(1)} %get-tuple-element.103.queries, bf16[4,128,768]{2,1,0:T(8,128)(2,1)S(1)} %get-tuple-element.104.keys, ...), custom_call_target="tpu_custom_call" | custom-call | flops 1000000000 | bytes 5000000 | tf_op jit(solution)/shard_map/outer/pallas_call | solution.py:334
  16.8 1.3 %collective-permute-done.3 = f32[8,768]{1,0:T(8,128)S(1)} collective-permute-done((f32[8,768]{1,0:T(8,128)S(1)}, f32[8,768]{1,0:T(8,128)S(1)}, u32[]{:S(2)}, u32[]{:S(2)}) %collective-permute-start.3) | collective-permute-done | bytes 24608 | tf_op jit(solution)/shard_map/ppermute | solution.py:529
  18.1 2.1 %collective-permute-start.4 = (bf16[8,768]{1,0:T(8,128)(2,1)S(1)}, bf16[8,768]{1,0:T(8,128)(2,1)S(1)}, u32[]{:S(2)}, u32[]{:S(2)}) collective-permute-start(bf16[8,768]{1,0:T(8,128)(2,1)S(1)} %add.7), channel_id=1, source_target_pairs={{0,18},{1,19},{2,16},{3,17},{4,22},{5,23},{6,20},{7,21},{8,26},{9,... | collective-permute-start | bytes 36872 | tf_op jit(solution)/shard_map/ppermute | solution.py:529
  20.2 0.0 copy-done.2
  20.2 1.7 %mix.1 = (bf16[4,128,768]{2,1,0:T(8,128)(2,1)S(1)}, f32[4,768]{1,0:T(4,128)S(1)}) custom-call(s32[3,4,8,128]{3,2,1,0:T(8,128)S(1)} %get-tuple-element.102.info, bf16[4,128,768]{2,1,0:T(8,128)(2,1)S(1)} %get-tuple-element.103.queries, bf16[4,128,768]{2,1,0:T(8,128)(2,1)S(1)} %get-tuple-element.104.keys, bf16[4,128,768]{2,1,0:T(8,128)(2,1)S(1)} %values.1, ...), custom_call_target="tpu_custom_call" | custom-call | flops 1000000000 | bytes 5000000 | tf_op jit(solution)/shard_map/mix/pallas_call | solution.py:375
  21.9 0.0 copy-start.1
  21.9 0.3 collective-permute-done.4
  22.2 1.8 %collective-permute-start.6 = (bf16[16,768]{1,0:T(8,128)(2,1)S(1)}, bf16[16,768]{1,0:T(8,128)(2,1)S(1)}, u32[]{:S(2)}, u32[]{:S(2)}) collective-permute-start(bf16[16,768]{1,0:T(8,128)(2,1)S(1)} %pad_maximum_fusion), channel_id=1, source_target_pairs={{0,6},{1,7},{2,4},{3,5},{4,2},{5,3},{6,0},{7,1},{8,14},{9,15},{10,... | collective-permute-start | bytes 73736 | tf_op jit(solution)/shard_map/ppermute | solution.py:529
  24.1 1.2 %collective-permute-start.7 = (bf16[16,768]{1,0:T(8,128)(2,1)S(1)}, bf16[16,768]{1,0:T(8,128)(2,1)S(1)}, u32[]{:S(2)}, u32[]{:S(2)}) collective-permute-start(bf16[16,768]{1,0:T(8,128)(2,1)S(1)} %pad_maximum_fusion), channel_id=1, source_target_pairs={{0,10},{1,11},{2,8},{3,9},{4,14},{5,15},{6,12},{7,13},{8,2},{9,3},... | collective-permute-start | bytes 73736 | tf_op jit(solution)/shard_map/ppermute | solution.py:529
  25.2 0.5 %collective-permute-start.8 = (bf16[16,768]{1,0:T(8,128)(2,1)S(1)}, bf16[16,768]{1,0:T(8,128)(2,1)S(1)}, u32[]{:S(2)}, u32[]{:S(2)}) collective-permute-start(bf16[16,768]{1,0:T(8,128)(2,1)S(1)} %pad_maximum_fusion), channel_id=1, source_target_pairs={{0,14},{1,15},{2,12},{3,13},{4,10},{5,11},{6,8},{7,9},{8,6},{9,7},... | collective-permute-start | bytes 73736 | tf_op jit(solution)/shard_map/ppermute | solution.py:529
  25.8 0.8 %collective-permute-start.5 = (f32[4,768]{1,0:T(4,128)S(1)}, f32[4,768]{1,0:T(4,128)S(1)}, u32[]{:S(2)}, u32[]{:S(2)}) collective-permute-start(f32[4,768]{1,0:T(4,128)S(1)} %get-tuple-element.116.mine), channel_id=1, source_target_pairs={{0,1},{1,0},{2,3},{3,2},{4,5},{5,4},{6,7},{7,6},{8,9},{9,8},{10,11... | collective-permute-start | bytes 36872 | tf_op jit(solution)/shard_map/ppermute | solution.py:529
  26.6 0.9 %copy.19 = bf16[4,128,768]{2,1,0:T(8,128)(2,1)} copy(bf16[4,128,768]{2,1,0:T(8,128)(2,1)S(1)} %get-tuple-element.123) | data formatting | bytes 1572864
  27.5 2.0 %collective-permute-done.5.other = f32[4,768]{1,0:T(4,128)S(1)} collective-permute-done((f32[4,768]{1,0:T(4,128)S(1)}, f32[4,768]{1,0:T(4,128)S(1)}, u32[]{:S(2)}, u32[]{:S(2)}) %collective-permute-start.5) | collective-permute-done | bytes 12320 | tf_op jit(solution)/shard_map/ppermute | solution.py:529
  29.5 0.0 copy-done.1
  29.5 1.0 %audio_head.1 = (f32[4,768]{1,0:T(4,128)}, f32[4,768]{1,0:T(4,128)S(1)}) custom-call(s32[3,4,8,128]{3,2,1,0:T(8,128)S(1)} %get-tuple-element.102.info, f32[4,768]{1,0:T(4,128)S(1)} %get-tuple-element.116.mine, f32[4,768]{1,0:T(4,128)S(1)} %collective-permute-done.5.other, bf16[768,768]{1,0:T(8,128)(2,1)S(1)} %copy-done.1), custom_call_target="tpu_custom_call" | custom-call | flops 20000000 | bytes 1200000 | tf_op jit(solution)/shard_map/audio_head/pallas_call | solution.py:453
  30.5 0.0 collective-permute-done.6
  30.5 0.0 collective-permute-done.7
  30.5 0.0 collective-permute-done.8
  30.6 1.1 %logits_and_loss.1 = (f32[4,64]{1,0:T(4,128)}, f32[1,4]{1,0:T(1,128)}, f32[4,768]{1,0:T(4,128)}) custom-call(s32[3,4,8,128]{3,2,1,0:T(8,128)S(1)} %get-tuple-element.102.info, f32[4,768]{1,0:T(4,128)S(1)} %get-tuple-element.118.audio, bf16[64,768]{1,0:T(8,128)(2,1)S(1)} %constant_dynamic-update-slice_fusion.held), custom_call_target="tpu_custom_call" | custom-call | flops 20000000 | bytes 300000 | tf_op jit(solution)/shard_map/logits_and_loss/pallas_call | solution.py:493
  (8 shorter events, 0.0 us)
Async XLA Ops:
  5.5 5.2 %collective-permute-start = (f32[4,16,128]{2,1,0:T(8,128)S(1)}, f32[4,16,128]{2,1,0:T(8,128)S(1)}, u32[]{:S(2)}, u32[]{:S(2)}) collective-permute-start(f32[4,16,128]{2,1,0:T(8,128)S(1)} %get-tuple-element.65.spans), channel_id=1, source_target_pairs={{0,1},{1,0},{2,3},{3,2},{4,5},{5,4},{6,7},{7,6},{8,9},{9,8},{10,11... | collective-permute-start | bytes 98312 | tf_op jit(solution)/shard_map/ppermute | solution.py:513
  8.5 6.4 %collective-permute-start.2 = (bf16[1,4,32,768]{3,2,1,0:T(8,128)(2,1)S(1)}, bf16[1,4,32,768]{3,2,1,0:T(8,128)(2,1)S(1)}, u32[]{:S(2)}, u32[]{:S(2)}) collective-permute-start(bf16[1,4,32,768]{3,2,1,0:T(8,128)(2,1)S(1)} %get-tuple-element.82), channel_id=1, source_target_pairs={{0,1},{1,0},{2,3},{3,2},{4,5},{5,4},{6,7},{7,6},{8,9},{9,8},{10,11... | collective-permute-start | bytes 589832 | tf_op jit(solution)/shard_map/ppermute | solution.py:529
  9.4 1.3 %copy-start = (bf16[768,768]{1,0:T(8,128)(2,1)S(1)}, bf16[768,768]{1,0:T(8,128)(2,1)}, u32[]{:S(2)}) copy-start(bf16[768,768]{1,0:T(8,128)(2,1)} %wvideo.1) | copy-start | bytes 3538948
  11.7 1.2 %collective-permute-start.1 = (f32[8,768]{1,0:T(8,128)S(1)}, f32[8,768]{1,0:T(8,128)S(1)}, u32[]{:S(2)}, u32[]{:S(2)}) collective-permute-start(f32[8,768]{1,0:T(8,128)S(1)} %pool.1), channel_id=1, source_target_pairs={{0,2},{1,3},{2,0},{3,1},{4,6},{5,7},{6,4},{7,5},{8,10},{9,11},{10,... | collective-permute-start | bytes 73736 | tf_op jit(solution)/shard_map/ppermute | solution.py:529
  14.9 5.3 %copy-start.2 = (bf16[768,768]{1,0:T(8,128)(2,1)S(1)}, bf16[768,768]{1,0:T(8,128)(2,1)}, u32[]{:S(2)}) copy-start(bf16[768,768]{1,0:T(8,128)(2,1)} %wout) | copy-start | bytes 3538948
  14.9 3.3 %collective-permute-start.3 = (f32[8,768]{1,0:T(8,128)S(1)}, f32[8,768]{1,0:T(8,128)S(1)}, u32[]{:S(2)}, u32[]{:S(2)}) collective-permute-start(f32[8,768]{1,0:T(8,128)S(1)} %add.6), channel_id=1, source_target_pairs={{0,3},{1,2},{2,1},{3,0},{4,7},{5,6},{6,5},{7,4},{8,11},{9,10},{10,... | collective-permute-start | bytes 73736 | tf_op jit(solution)/shard_map/ppermute | solution.py:529
  18.1 4.1 %collective-permute-start.4 = (bf16[8,768]{1,0:T(8,128)(2,1)S(1)}, bf16[8,768]{1,0:T(8,128)(2,1)S(1)}, u32[]{:S(2)}, u32[]{:S(2)}) collective-permute-start(bf16[8,768]{1,0:T(8,128)(2,1)S(1)} %add.7), channel_id=1, source_target_pairs={{0,18},{1,19},{2,16},{3,17},{4,22},{5,23},{6,20},{7,21},{8,26},{9,... | collective-permute-start | bytes 36872 | tf_op jit(solution)/shard_map/ppermute | solution.py:529
  21.9 7.6 %copy-start.1 = (bf16[768,768]{1,0:T(8,128)(2,1)S(1)}, bf16[768,768]{1,0:T(8,128)(2,1)}, u32[]{:S(2)}) copy-start(bf16[768,768]{1,0:T(8,128)(2,1)} %waudio.1) | copy-start | bytes 3538948
  22.2 8.3 %collective-permute-start.6 = (bf16[16,768]{1,0:T(8,128)(2,1)S(1)}, bf16[16,768]{1,0:T(8,128)(2,1)S(1)}, u32[]{:S(2)}, u32[]{:S(2)}) collective-permute-start(bf16[16,768]{1,0:T(8,128)(2,1)S(1)} %pad_maximum_fusion), channel_id=1, source_target_pairs={{0,6},{1,7},{2,4},{3,5},{4,2},{5,3},{6,0},{7,1},{8,14},{9,15},{10,... | collective-permute-start | bytes 73736 | tf_op jit(solution)/shard_map/ppermute | solution.py:529
  24.1 6.5 %collective-permute-start.7 = (bf16[16,768]{1,0:T(8,128)(2,1)S(1)}, bf16[16,768]{1,0:T(8,128)(2,1)S(1)}, u32[]{:S(2)}, u32[]{:S(2)}) collective-permute-start(bf16[16,768]{1,0:T(8,128)(2,1)S(1)} %pad_maximum_fusion), channel_id=1, source_target_pairs={{0,10},{1,11},{2,8},{3,9},{4,14},{5,15},{6,12},{7,13},{8,2},{9,3},... | collective-permute-start | bytes 73736 | tf_op jit(solution)/shard_map/ppermute | solution.py:529
  25.2 5.3 %collective-permute-start.8 = (bf16[16,768]{1,0:T(8,128)(2,1)S(1)}, bf16[16,768]{1,0:T(8,128)(2,1)S(1)}, u32[]{:S(2)}, u32[]{:S(2)}) collective-permute-start(bf16[16,768]{1,0:T(8,128)(2,1)S(1)} %pad_maximum_fusion), channel_id=1, source_target_pairs={{0,14},{1,15},{2,12},{3,13},{4,10},{5,11},{6,8},{7,9},{8,6},{9,7},... | collective-permute-start | bytes 73736 | tf_op jit(solution)/shard_map/ppermute | solution.py:529
  25.8 3.7 %collective-permute-start.5 = (f32[4,768]{1,0:T(4,128)S(1)}, f32[4,768]{1,0:T(4,128)S(1)}, u32[]{:S(2)}, u32[]{:S(2)}) collective-permute-start(f32[4,768]{1,0:T(4,128)S(1)} %get-tuple-element.116.mine), channel_id=1, source_target_pairs={{0,1},{1,0},{2,3},{3,2},{4,5},{5,4},{6,7},{7,6},{8,9},{9,8},{10,11... | collective-permute-start | bytes 36872 | tf_op jit(solution)/shard_map/ppermute | solution.py:529

commit v4 on v3

--- a/solution.py
+++ b/solution.py
@@ -16,6 +16,7 @@
 BF16 = jnp.bfloat16
 LANES = 128
 STAT_ROWS = 16
+STAGED = 3
 NT = (((1,), (1,)), ((), ()))
 VMEM = pltpu.VMEM
 MIB = 1 << 20
@@ -207,6 +208,7 @@
     lane = lax.broadcasted_iota(jnp.int32, (block, LANES), 1)
     ones = jnp.ones((span, LANES), BF16)
     columns = [slice(pair * LANES, (pair + 1) * LANES) for pair in range(HA // 2)]
+    units = []
     for i, (c, half) in enumerate(tasks):
         if half == "inner":
             b = tm
@@ -214,7 +216,7 @@
         else:
             b = 1 - tm if half == "outer" else half
             way = 0 if half == "outer" else half
-            key, value = ext_k.at[i % 2], ext_v.at[i % 2]
+            key, value = ext_k.at[i], ext_v.at[i]
             first = tm * frames + b * block - side
             for own, near, ext in ((keys, near_k, key), (values, near_v, value)):
                 if half == "outer":
@@ -234,20 +236,25 @@
             allowed = allowed & (key_pos >= 0) & (key_pos < last)
         allowed = jnp.concatenate([allowed, allowed], axis=0)
         rows = pl.ds(pl.multiple_of(b * block, block), block)
+        units += [(i, c, rows, key, value, allowed, cols) for cols in columns]
+    size = STAGED * len(columns)
+    for at in range(0, len(units), size):
+        some = units[at : at + size]
         scores = [
-            dot_nt(split_heads(queries[c, rows, cols], HS**-0.5), key[:, cols]) for cols in columns
+            dot_nt(split_heads(queries[c, rows, cols], HS**-0.5), key[:, cols])
+            for i, c, rows, key, value, allowed, cols in some
         ]
-        scores = [jnp.where(allowed, s, NEG_LARGE) for s in scores]
+        scores = [jnp.where(unit[5], s, NEG_LARGE) for s, unit in zip(scores, some)]
         highest = [jnp.max(s, axis=1, keepdims=True) for s in scores]
         rising = [jnp.exp(s - peak).astype(BF16) for s, peak in zip(scores, highest)]
         mixes = [
             dot_f32(r, jnp.concatenate([value[:, cols], ones], axis=1))
-            for r, cols in zip(rising, columns)
+            for r, (i, c, rows, key, value, allowed, cols) in zip(rising, some)
         ]
-        for mix, cols in zip(mixes, columns):
+        for mix, unit in zip(mixes, some):
             top = jnp.where(lane < HS, mix[:block, :LANES], mix[block:, :LANES])
             total = jnp.where(lane < HS, mix[:block, LANES:], mix[block:, LANES:])
-            out[i, :, cols] = (top / total).astype(BF16)
+            out[unit[0], :, unit[6]] = (top / total).astype(BF16)
 
 
 def project(flat, weight, out):
@@ -315,43 +322,22 @@
     )(info, queries, keys, values)
 
 
-def outer_kernel(
-    two_sided, tasks, info, queries, keys, values, near, wk, wv, done, near_k, near_v, ext_k, ext_v
-):
-    sides, clips, side, width = near.shape
-    flat = near[...].reshape(sides * clips * side, width)
-    chunk = 2 * LANES
-    for weight, out in ((wk, near_k), (wv, near_v)):
-        for at in range(0, width, chunk):
-            part = dot_f32(flat, weight[:, at : at + chunk]).astype(BF16)
-            out[:, :, :, at : at + chunk] = part.reshape(sides, clips, side, chunk)
-    attend(two_sided, tasks, info, queries, keys, values, near_k, near_v, ext_k, ext_v, done)
-
-
-def outer(two_sided, tasks, info, queries, keys, values, near, wk, wv):
-    clips, frames, width = queries.shape
-    beyond = VMEM(near.shape, BF16)
-    return pl.pallas_call(
-        functools.partial(outer_kernel, two_sided, tasks),
-        name="outer",
-        out_shape=[context_of(tasks, frames, width), beyond, beyond],
-        in_specs=whole(7),
-        out_specs=whole(3),
-        scratch_shapes=[VMEM((2, frames, width), BF16)] * 2,
-        compiler_params=params(16),
-        cost_estimate=cost(1_000_000_000, 5_000_000, 400_000),
-    )(info, queries, keys, values, near, wk, wv)
-
-
 def mix_kernel(
-    two_sided, plan, info, queries, keys, values, near_k, near_v, audio, wout, *rest
+    two_sided, plan, info, queries, keys, values, near, wk, wv, audio, wout, *rest
 ):
     count = len(plan) - 1
     before = rest[:count]
-    mixed, frame_sum, context, done, ext_k, ext_v = rest[count:]
+    mixed, frame_sum, context, done, near_k, near_v, ext_k, ext_v = rest[count:]
     clips, frames, width = queries.shape
+    sides, side = near.shape[0], near.shape[2]
     block = frames // 2
+    chunk = 2 * LANES
     tm = lax.axis_index("tm")
+    beyond = near[...].reshape(sides * clips * side, width)
+    for weight, out in ((wk, near_k), (wv, near_v)):
+        for at in range(0, width, chunk):
+            part = dot_f32(beyond, weight[:, at : at + chunk]).astype(BF16)
+            out[:, :, :, at : at + chunk] = part.reshape(sides, clips, side, chunk)
     attend(two_sided, plan[-1], info, queries, keys, values, near_k, near_v, ext_k, ext_v, done)
     for tasks, held in zip(plan, (*before, done)):
         for i, (c, half) in enumerate(tasks):
@@ -359,7 +345,6 @@
             context[c, pl.ds(pl.multiple_of(b * block, block), block), :] = held[i]
     place = tm * frames + lax.broadcasted_iota(jnp.int32, (frames, 1), 0)
     flat = context[...].reshape(clips * frames, width)
-    chunk = 2 * LANES
     for at in range(0, width, chunk):
         cols = slice(at, at + chunk)
         part = dot_f32(flat, wout[:, cols]).reshape(clips, frames, chunk)
@@ -370,19 +355,21 @@
             frame_sum[c : c + 1, cols] = jnp.sum(kept, axis=0, keepdims=True)
 
 
-def mix(two_sided, plan, info, queries, keys, values, near_k, near_v, audio, wout, before):
+def mix(two_sided, plan, info, queries, keys, values, near, wk, wv, audio, wout, before):
     clips, frames, width = queries.shape
+    beyond = VMEM(near.shape, BF16)
     return pl.pallas_call(
         functools.partial(mix_kernel, two_sided, plan),
         name="mix",
         out_shape=[VMEM(audio.shape, BF16), VMEM((clips, width), F32)],
-        in_specs=whole(8 + len(before)),
+        in_specs=whole(9 + len(before)),
         out_specs=whole(2),
         scratch_shapes=[VMEM((clips, frames, width), BF16), context_of(plan[-1], frames, width)]
-        + [VMEM((2, frames, width), BF16)] * 2,
-        compiler_params=params(16),
-        cost_estimate=cost(1_000_000_000, 5_000_000, 400_000),
-    )(info, queries, keys, values, near_k, near_v, audio, wout, *before)
+        + [beyond, beyond]
+        + [VMEM((len(plan[-1]), frames, width), BF16)] * 2,
+        compiler_params=params(32),
+        cost_estimate=cost(2_000_000_000, 8_000_000, 400_000),
+    )(info, queries, keys, values, near, wk, wv, audio, wout, *before)
 
 
 def pool_kernel(peaks, spans, others, weights, values, wvideo, out):
@@ -441,19 +428,27 @@
     return jnp.concatenate([info[k, c, 0:1, 0:1] for c in range(info.shape[1])], axis=0)
 
 
-def audio_head_kernel(info, mine, other, waudio, out, held):
+def in_parts(x):
+    high = x.astype(BF16)
+    rest = x - high.astype(F32)
+    middle = rest.astype(BF16)
+    low = (rest - middle.astype(F32)).astype(BF16)
+    return jnp.concatenate([high, middle, low], axis=0)
+
+
+def audio_head_kernel(info, mine, other, waudio, out, parts):
     mean = ((mine[...] + other[...]) / column_of(info, 0).astype(F32)).astype(BF16)
     found = unit_rows(dot_f32(mean, waudio[...]))
     out[...] = found
-    held[...] = found
+    parts[...] = in_parts(found)
 
 
 def audio_head(info, mine, other, waudio):
-    shape = (mine.shape[0], waudio.shape[1])
+    clips, width = mine.shape[0], waudio.shape[1]
     return pl.pallas_call(
         audio_head_kernel,
         name="audio_head",
-        out_shape=[jax.ShapeDtypeStruct(shape, F32), VMEM(shape, F32)],
+        out_shape=[jax.ShapeDtypeStruct((clips, width), F32), VMEM((3 * clips, width), BF16)],
         in_specs=whole(4),
         out_specs=whole(2),
         compiler_params=params(8),
@@ -461,21 +456,28 @@
     )(info, mine, other, waudio)
 
 
-def logits_kernel(masks, info, audio, held, logits, row_loss, video_embed, units):
-    clips = audio.shape[0]
+def logits_kernel(masks, info, parts, held, logits, row_loss, video_embed, ordered):
+    clips = logits.shape[0]
+    total = held.shape[0]
     place = lax.axis_index("batch")
     core = lax.rem(place, 2)
     chip = lax.div(place, 2)
-    found = unit_rows(held[...].astype(F32))
     rows = 2 * clips
+    wide = held[...].astype(F32)
     for j, mask in enumerate(masks):
         at = pl.multiple_of((chip ^ mask) * rows, rows)
-        units[pl.ds(at, rows), :] = found[j * rows : (j + 1) * rows]
-    video_embed[...] = jnp.where(core == 0, found[:clips], found[clips:rows])
-    found = LOGIT_SCALE * lax.dot_general(
-        audio[...], units[...], NT, precision=lax.Precision.HIGHEST, preferred_element_type=F32
-    )
-    found = found + LOGIT_BIAS
+        ordered[pl.ds(at, rows), :] = wide[j * rows : (j + 1) * rows]
+    own = unit_rows(wide[:rows])
+    video_embed[...] = jnp.where(core == 0, own[:clips], own[clips:])
+    wide = ordered[...]
+    scale = LOGIT_SCALE / jnp.sqrt(jnp.sum(wide * wide, axis=1, keepdims=True) + 1e-06)
+    square = lax.broadcasted_iota(jnp.int32, (total, total), 0) == lax.broadcasted_iota(
+        jnp.int32, (total, total), 1
+    )
+    scale = jnp.sum(jnp.where(square, scale, 0.0), axis=0, keepdims=True)
+    found = dot_nt(parts[...], wide.astype(BF16))
+    found = found[:clips] + found[clips : 2 * clips] + found[2 * clips :]
+    found = found * scale + LOGIT_BIAS
     logits[...] = found
     column = lax.broadcasted_iota(jnp.int32, found.shape, 1)
     signed = jnp.where(column == column_of(info, 2), -found, found)
@@ -487,9 +489,9 @@
     row_loss[...] = jnp.sum(jnp.where(square, loss, 0.0), axis=0, keepdims=True)
 
 
-def logits_and_loss(masks, info, audio, held):
-    clips, width = audio.shape
-    total = held.shape[0]
+def logits_and_loss(masks, info, parts, held):
+    clips = info.shape[1]
+    total, width = held.shape
     return pl.pallas_call(
         functools.partial(logits_kernel, masks),
         name="logits_and_loss",
@@ -503,7 +505,7 @@
         scratch_shapes=[VMEM((total, width), F32)],
         compiler_params=params(8),
         cost_estimate=cost(20_000_000, 300_000),
-    )(info, audio, held)
+    )(info, parts, held)
 
 
 def others_on_tm(x):
@@ -527,6 +529,16 @@
     tm = lax.axis_size("tm")
     pairs = [(b * tm + t, (b ^ mask) * tm + (t ^ flip)) for b in range(batch) for t in range(tm)]
     return lax.ppermute(x, ("batch", "tm"), pairs)
+
+
+def chip_masks(chips):
+    top = chips // 2
+    groups = [(top,)]
+    while top > 1:
+        step = 4 if top % 4 == 0 else 2
+        top //= step
+        groups.append((3 * top, top, 2 * top) if step == 4 else (top,))
+    return groups
 
 
 def per_device(
@@ -537,12 +549,11 @@
     chips = lax.axis_size("batch") // 2
     two_sided = tm > 2
     if two_sided:
-        plan = ((), (), tuple((c, 0) for c in range(clips)), tuple((c, 1) for c in range(clips)))
+        plan = ((), (), tuple((c, half) for c in range(clips) for half in range(2)))
     else:
         inside = tuple((c, "inner") for c in range(clips))
         outside = tuple((c, "outer") for c in range(clips))
-        cut = clips // 2
-        plan = (inside[:1], inside[1:2], inside[2:] + outside[:cut], outside[cut:])
+        plan = (inside[:1], inside[1:], outside)
     peaks, spans, info, weights, keys, held_audio, halo, wq, wk, wv = front(
         lengths, windows, pair_ids, audio, video, w_qkv, w_query, two_sided
     )
@@ -572,31 +583,22 @@
     def share(x):
         return lax.psum(x, "tm") if two_sided else x + move(x, 1, 1)
 
-    found, (part_c, near_k, near_v) = beside(
-        share, found, lambda *held: outer(two_sided, plan[2], *held), (*local, near, wk, wv)
+    found, (audio_mixed, frame_sum) = beside(
+        share,
+        found,
+        lambda *held: mix(two_sided, plan, *held[:9], held[9:]),
+        (*local, near, wk, wv, held_audio, w_out, part_a, part_b),
     )
     held = found.astype(BF16)
-    masks = [0]
-    top = chips // 2
-    moved, (audio_mixed, frame_sum) = beside(
-        lambda x: move(x, 2 * top + 1),
-        held,
-        lambda *held: mix(two_sided, plan, *held[:8], held[8:]),
-        (*local, near_k, near_v, held_audio, w_out, part_a, part_b, part_c),
-    )
-    held = jnp.concatenate([held, moved], axis=0)
-    masks = masks + [top]
     if two_sided:
         frame_sum = lax.psum(frame_sum, "tm")
         other_sum = jnp.zeros_like(frame_sum)
     else:
         other_sum = move(frame_sum, 0, 1)
-    while top > 1:
-        step = 4 if top % 4 == 0 else 2
-        top //= step
-        moves = [k * top for k in range(1, step)]
-        held = jnp.concatenate([held] + [move(held, 2 * m + 1) for m in moves], axis=0)
-        masks = masks + [mask ^ m for m in moves for mask in masks]
+    masks = [0]
+    for group in chip_masks(chips):
+        held = jnp.concatenate([held] + [move(held, 2 * m + (m > 1)) for m in group], axis=0)
+        masks = masks + [mask ^ m for m in group for mask in masks]
     audio_embed, unit_audio = audio_head(info, frame_sum, other_sum, w_audio_embed)
     logits, row_loss, video_embed = logits_and_loss(masks, info, unit_audio, held)
     return (audio_mixed, audio_embed, video_embed, logits, row_loss.reshape(clips))

time: 31.8 us -> 29.6 us (0.931)
  waiting for transfers between devices: 6.24 us -> 4.89 us
  Pallas kernels: 14.2 us -> 13.1 us
    pallas_call x1 -> x0, Pallas kernels: 1.92 us -> none  [outer(): pl.pallas_call(functools.partial(outer_kernel, two_sided, tasks), name='o...]
    ppermute x8, waiting for transfers between devices: 6.24 us -> 4.88 us  [move(): return lax.ppermute(x, ('batch', 'tm'), pairs)]
    pallas_call x1, Pallas kernels: 1.71 us -> 2.39 us  [mix(): pl.pallas_call(functools.partial(mix_kernel, two_sided, plan), name='mix'...]
    pallas_call x1, Pallas kernels: 0.52 us -> 0.9 us  [inner(): pl.pallas_call(functools.partial(inner_kernel, two_sided, tasks), name='i...]
  transfers between devices with their start and end apart: 9 -> 9, of which waited for: 5 -> 5; matrix products, arithmetic and copies ran while one was open for 3% -> 3% of each run, Pallas kernels for 26% -> 25%
where the time goes in v4:
time: 29.6 us; the launch traced here: 29.5 us
  Pallas kernels  13.1 us (44%)
  starting transfers between devices  9.87 us (33%)
  waiting for transfers between devices  4.89 us (17%)
  local copies, waits for them, and re-layouts  0.91 us (3%)
  between operations  0.72 us (2%)
    ppermute x8, starting transfers between devices, move(): return lax.ppermute(x, ('batch', 'tm'), pairs)  6.84 us
    ppermute x8, waiting for transfers between devices, move(): return lax.ppermute(x, ('batch', 'tm'), pairs)  4.88 us
    pallas_call x1, Pallas kernels, front(): pl.pallas_call(functools.partial(front_kernel, two_sided), name='front',...  4.83 us
    ppermute x1, starting transfers between devices, others_on_tm(): lax.ppermute(x, 'tm', [(i, (i + shift) % count) for i in range(count)])  3.03 us
    pallas_call x1, Pallas kernels, mix(): pl.pallas_call(functools.partial(mix_kernel, two_sided, plan), name='mix'...  2.39 us
    pallas_call x1, Pallas kernels, make_queries(): pl.pallas_call(functools.partial(queries_kernel, two_sided, tasks), name=...  1.29 us
    pallas_call x1, Pallas kernels, audio_head(): pl.pallas_call(audio_head_kernel, name='audio_head', out_shape=[jax.Shape...  1.03 us
    pallas_call x1, Pallas kernels, pool(): pl.pallas_call(pool_kernel, name='pool', out_shape=VMEM((2 * clips, wvide...  0.97 us
  transfers between devices with their start and end apart: 9, of which 5 were waited for; matrix products, arithmetic and copies ran while one was open for 3% of the time, Pallas kernels for 25%

profile of v4, /device:TPU:0, one launch (start us, length us, event | category | flops | bytes accessed | tf_op | source)
XLA Modules:
  0.0 29.5 jit_solution(18166627962694979179)
XLA Ops:
  0.6 4.8 %front.1 = (f32[4,16,128]{2,1,0:T(8,128)S(1)}, f32[4,16,128]{2,1,0:T(8,128)S(1)}, s32[3,4,8,128]{3,2,1,0:T(8,128)S(1)}, bf16[4,128,1536]{2,1,0:T(8,128)(2,1)S(1)...) custom-call(s32[4]{0:T(128)} %lengths.1, ...), custom_call_target="tpu_custom_call" | custom-call | flops 2000000000 | bytes 8000000 | tf_op jit(solution)/shard_map/front/pallas_call | solution.py:171
  5.5 3.0 %collective-permute-start = (f32[4,16,128]{2,1,0:T(8,128)S(1)}, f32[4,16,128]{2,1,0:T(8,128)S(1)}, u32[]{:S(2)}, u32[]{:S(2)}) collective-permute-start(f32[4,16,128]{2,1,0:T(8,128)S(1)} %get-tuple-element.50.spans), channel_id=1, source_target_pairs={{0,1},{1,0},{2,3},{3,2},{4,5},{5,4},{6,7},{7,6},{8,9},{9,8},{10,11... | collective-permute-start | bytes 98312 | tf_op jit(solution)/shard_map/ppermute | solution.py:515
  8.5 0.1 collective-permute-start.2
  8.6 0.8 %values.1 = bf16[4,128,768]{2,1,0:T(8,128)(2,1)S(1)} custom-call(bf16[4,128,768]{2,1,0:T(8,128)(2,1)S(1)} %get-tuple-element.79.audio, bf16[768,768]{1,0:T(8,128)(2,1)S(1)} %get-tuple-element.78.wv), custom_call_target="tpu_custom_call" | custom-call | flops 600000000 | bytes 2000000 | tf_op jit(solution)/shard_map/values/pallas_call | solution.py:274
  9.4 0.0 copy-start
  9.4 1.3 %queries.1 = (bf16[4,128,768]{2,1,0:T(8,128)(2,1)S(1)}, bf16[1,64,768]{2,1,0:T(8,128)(2,1)S(1)}) custom-call(s32[3,4,8,128]{3,2,1,0:T(8,128)S(1)} %get-tuple-element.72.info, bf16[4,128,768]{2,1,0:T(8,128)(2,1)S(1)} %get-tuple-element.79.audio, bf16[4,128,768]{2,1,0:T(8,128)(2,1)S(1)} %get-tuple-element.74.keys, bf16[4,128,768]{2,1,0:T(8,128)(2,1)S(1)} %values.1, ...), custom_call_target="tpu_custom_call" | custom-call | flops 80000000000 | bytes 3000000 | tf_op jit(solution)/shard_map/queries/pallas_call | solution.py:297
  10.7 0.0 collective-permute-done
  10.7 0.0 copy-done
  10.7 1.0 %pool.1 = f32[8,768]{1,0:T(8,128)S(1)} custom-call(f32[4,16,128]{2,1,0:T(8,128)S(1)} %get-tuple-element.49.peaks, f32[4,16,128]{2,1,0:T(8,128)S(1)} %get-tuple-element.50.spans, f32[1,4,16,128]{3,2,1,0:T(8,128)S(1)} %bitcast.2, bf16[4,128,1536]{2,1,0:T(8,128)(2,1)S(1)} %get-tuple-element.59.weights, bf16[4,128,768]{2,1,0:T(8,128)(2,1)S(1)} %values.1, ...), custom_call_target="tpu_custom_call" | custom-call | flops 200000000 | bytes 2000000 | tf_op jit(solution)/shard_map/pool/pallas_call | solution.py:412
  11.7 0.0 copy-start.2
  11.7 0.0 collective-permute-start.1
  11.7 0.9 %inner.1.rest_1_ = bf16[3,64,768]{2,1,0:T(8,128)(2,1)S(1)} custom-call(s32[3,4,8,128]{3,2,1,0:T(8,128)S(1)} %get-tuple-element.72.info, bf16[4,128,768]{2,1,0:T(8,128)(2,1)S(1)} %get-tuple-element.73.queries, bf16[4,128,768]{2,1,0:T(8,128)(2,1)S(1)} %get-tuple-element.74.keys, bf16[4,128,768]{2,1,0:T(8,128)(2,1)S(1)} %values.1), custom_call_target="tpu_custom_call" | custom-call | flops 300000000 | bytes 2000000 | tf_op jit(solution)/shard_map/inner/pallas_call | solution.py:314
  12.6 0.3 %collective-permute-done.1 = f32[8,768]{1,0:T(8,128)S(1)} collective-permute-done((f32[8,768]{1,0:T(8,128)S(1)}, f32[8,768]{1,0:T(8,128)S(1)}, u32[]{:S(2)}, u32[]{:S(2)}) %collective-permute-start.1) | collective-permute-done | bytes 24608 | tf_op jit(solution)/shard_map/ppermute | solution.py:531
  12.9 2.0 %collective-permute-done.2.near = bf16[1,4,32,768]{3,2,1,0:T(8,128)(2,1)S(1)} collective-permute-done((bf16[1,4,32,768]{3,2,1,0:T(8,128)(2,1)S(1)}, bf16[1,4,32,768]{3,2,1,0:T(8,128)(2,1)S(1)}, u32[]{:S(2)}, u32[]{:S(2)}) %collective-permute-start.2) | collective-permute-done | bytes 196640 | tf_op jit(solution)/shard_map/ppermute | solution.py:531
  14.9 0.0 collective-permute-start.3
  14.9 0.0 copy-done.2
  14.9 2.4 %mix.1 = (bf16[4,128,768]{2,1,0:T(8,128)(2,1)S(1)}, f32[4,768]{1,0:T(4,128)S(1)}) custom-call(s32[3,4,8,128]{3,2,1,0:T(8,128)S(1)} %get-tuple-element.72.info, bf16[4,128,768]{2,1,0:T(8,128)(2,1)S(1)} %get-tuple-element.73.queries, bf16[4,128,768]{2,1,0:T(8,128)(2,1)S(1)} %get-tuple-element.74.keys, bf16[4,128,768]{2,1,0:T(8,128)(2,1)S(1)} %values.1, ...), custom_call_target="tpu_custom_call" | custom-call | flops 2000000000 | bytes 8000000 | tf_op jit(solution)/shard_map/mix/pallas_call | solution.py:361
  17.3 0.0 copy-start.1
  17.3 0.8 %collective-permute-done.3 = f32[8,768]{1,0:T(8,128)S(1)} collective-permute-done((f32[8,768]{1,0:T(8,128)S(1)}, f32[8,768]{1,0:T(8,128)S(1)}, u32[]{:S(2)}, u32[]{:S(2)}) %collective-permute-start.3) | collective-permute-done | bytes 24608 | tf_op jit(solution)/shard_map/ppermute | solution.py:531
  18.1 2.5 %collective-permute-start.5 = (bf16[8,768]{1,0:T(8,128)(2,1)S(1)}, bf16[8,768]{1,0:T(8,128)(2,1)S(1)}, u32[]{:S(2)}, u32[]{:S(2)}) collective-permute-start(bf16[8,768]{1,0:T(8,128)(2,1)S(1)} %add.7), channel_id=1, source_target_pairs={{0,18},{1,19},{2,16},{3,17},{4,22},{5,23},{6,20},{7,21},{8,26},{9,... | collective-permute-start | bytes 36872 | tf_op jit(solution)/shard_map/ppermute | solution.py:531
  20.6 1.3 %collective-permute-start.4 = (f32[4,768]{1,0:T(4,128)S(1)}, f32[4,768]{1,0:T(4,128)S(1)}, u32[]{:S(2)}, u32[]{:S(2)}) collective-permute-start(f32[4,768]{1,0:T(4,128)S(1)} %get-tuple-element.86.mine), channel_id=1, source_target_pairs={{0,1},{1,0},{2,3},{3,2},{4,5},{5,4},{6,7},{7,6},{8,9},{9,8},{10,11... | collective-permute-start | bytes 36872 | tf_op jit(solution)/shard_map/ppermute | solution.py:531
  22.0 0.9 %copy.19 = bf16[4,128,768]{2,1,0:T(8,128)(2,1)} copy(bf16[4,128,768]{2,1,0:T(8,128)(2,1)S(1)} %get-tuple-element.93) | data formatting | bytes 1572864
  22.8 0.0 collective-permute-done.5
  22.8 1.8 %collective-permute-start.6 = (bf16[16,768]{1,0:T(8,128)(2,1)S(1)}, bf16[16,768]{1,0:T(8,128)(2,1)S(1)}, u32[]{:S(2)}, u32[]{:S(2)}) collective-permute-start(bf16[16,768]{1,0:T(8,128)(2,1)S(1)} %pad_maximum_fusion), channel_id=1, source_target_pairs={{0,14},{1,15},{2,12},{3,13},{4,10},{5,11},{6,8},{7,9},{8,6},{9,7},... | collective-permute-start | bytes 73736 | tf_op jit(solution)/shard_map/ppermute | solution.py:531
  24.6 0.5 %collective-permute-start.7 = (bf16[16,768]{1,0:T(8,128)(2,1)S(1)}, bf16[16,768]{1,0:T(8,128)(2,1)S(1)}, u32[]{:S(2)}, u32[]{:S(2)}) collective-permute-start(bf16[16,768]{1,0:T(8,128)(2,1)S(1)} %pad_maximum_fusion), channel_id=1, source_target_pairs={{0,4},{1,5},{2,6},{3,7},{4,0},{5,1},{6,2},{7,3},{8,12},{9,13},{10,... | collective-permute-start | bytes 73736 | tf_op jit(solution)/shard_map/ppermute | solution.py:531
  25.2 0.6 %collective-permute-start.8 = (bf16[16,768]{1,0:T(8,128)(2,1)S(1)}, bf16[16,768]{1,0:T(8,128)(2,1)S(1)}, u32[]{:S(2)}, u32[]{:S(2)}) collective-permute-start(bf16[16,768]{1,0:T(8,128)(2,1)S(1)} %pad_maximum_fusion), channel_id=1, source_target_pairs={{0,10},{1,11},{2,8},{3,9},{4,14},{5,15},{6,12},{7,13},{8,2},{9,3},... | collective-permute-start | bytes 73736 | tf_op jit(solution)/shard_map/ppermute | solution.py:531
  25.8 0.0 collective-permute-done.4.other
  25.8 0.0 copy-done.1
  25.8 1.0 %audio_head.1 = (f32[4,768]{1,0:T(4,128)}, bf16[12,768]{1,0:T(8,128)(2,1)S(1)}) custom-call(s32[3,4,8,128]{3,2,1,0:T(8,128)S(1)} %get-tuple-element.72.info, f32[4,768]{1,0:T(4,128)S(1)} %get-tuple-element.86.mine, f32[4,768]{1,0:T(4,128)S(1)} %collective-permute-done.4.other, bf16[768,768]{1,0:T(8,128)(2,1)S(1)} %copy-done.1), custom_call_target="tpu_custom_call" | custom-call | flops 20000000 | bytes 1200000 | tf_op jit(solution)/shard_map/audio_head/pallas_call | solution.py:448
  26.8 0.3 collective-permute-done.6
  27.1 1.5 %collective-permute-done.7 = bf16[16,768]{1,0:T(8,128)(2,1)S(1)} collective-permute-done((bf16[16,768]{1,0:T(8,128)(2,1)S(1)}, bf16[16,768]{1,0:T(8,128)(2,1)S(1)}, u32[]{:S(2)}, u32[]{:S(2)}) %collective-permute-start.7) | collective-permute-done | bytes 24608 | tf_op jit(solution)/shard_map/ppermute | solution.py:531
  28.6 0.0 collective-permute-done.8
  28.6 0.9 %logits_and_loss.1 = (f32[4,64]{1,0:T(4,128)}, f32[1,4]{1,0:T(1,128)}, f32[4,768]{1,0:T(4,128)}) custom-call(s32[3,4,8,128]{3,2,1,0:T(8,128)S(1)} %get-tuple-element.72.info, bf16[12,768]{1,0:T(8,128)(2,1)S(1)} %get-tuple-element.88.parts, bf16[64,768]{1,0:T(8,128)(2,1)S(1)} %constant_dynamic-update-slice_fusion.held), custom_call_target="tpu_custom_call" | custom-call | flops 20000000 | bytes 300000 | tf_op jit(solution)/shard_map/logits_and_loss/pallas_call | solution.py:495
  (8 shorter events, 0.0 us)
Async XLA Ops:
  5.5 5.2 %collective-permute-start = (f32[4,16,128]{2,1,0:T(8,128)S(1)}, f32[4,16,128]{2,1,0:T(8,128)S(1)}, u32[]{:S(2)}, u32[]{:S(2)}) collective-permute-start(f32[4,16,128]{2,1,0:T(8,128)S(1)} %get-tuple-element.50.spans), channel_id=1, source_target_pairs={{0,1},{1,0},{2,3},{3,2},{4,5},{5,4},{6,7},{7,6},{8,9},{9,8},{10,11... | collective-permute-start | bytes 98312 | tf_op jit(solution)/shard_map/ppermute | solution.py:515
  8.5 6.4 %collective-permute-start.2 = (bf16[1,4,32,768]{3,2,1,0:T(8,128)(2,1)S(1)}, bf16[1,4,32,768]{3,2,1,0:T(8,128)(2,1)S(1)}, u32[]{:S(2)}, u32[]{:S(2)}) collective-permute-start(bf16[1,4,32,768]{3,2,1,0:T(8,128)(2,1)S(1)} %get-tuple-element.67), channel_id=1, source_target_pairs={{0,1},{1,0},{2,3},{3,2},{4,5},{5,4},{6,7},{7,6},{8,9},{9,8},{10,11... | collective-permute-start | bytes 589832 | tf_op jit(solution)/shard_map/ppermute | solution.py:531
  9.4 1.3 %copy-start = (bf16[768,768]{1,0:T(8,128)(2,1)S(1)}, bf16[768,768]{1,0:T(8,128)(2,1)}, u32[]{:S(2)}) copy-start(bf16[768,768]{1,0:T(8,128)(2,1)} %wvideo.1) | copy-start | bytes 3538948
  11.7 3.2 %copy-start.2 = (bf16[768,768]{1,0:T(8,128)(2,1)S(1)}, bf16[768,768]{1,0:T(8,128)(2,1)}, u32[]{:S(2)}) copy-start(bf16[768,768]{1,0:T(8,128)(2,1)} %wout) | copy-start | bytes 3538948
  11.7 1.2 %collective-permute-start.1 = (f32[8,768]{1,0:T(8,128)S(1)}, f32[8,768]{1,0:T(8,128)S(1)}, u32[]{:S(2)}, u32[]{:S(2)}) collective-permute-start(f32[8,768]{1,0:T(8,128)S(1)} %pool.1), channel_id=1, source_target_pairs={{0,2},{1,3},{2,0},{3,1},{4,6},{5,7},{6,4},{7,5},{8,10},{9,11},{10,... | collective-permute-start | bytes 73736 | tf_op jit(solution)/shard_map/ppermute | solution.py:531
  14.9 3.3 %collective-permute-start.3 = (f32[8,768]{1,0:T(8,128)S(1)}, f32[8,768]{1,0:T(8,128)S(1)}, u32[]{:S(2)}, u32[]{:S(2)}) collective-permute-start(f32[8,768]{1,0:T(8,128)S(1)} %add.6), channel_id=1, source_target_pairs={{0,3},{1,2},{2,1},{3,0},{4,7},{5,6},{6,5},{7,4},{8,11},{9,10},{10,... | collective-permute-start | bytes 73736 | tf_op jit(solution)/shard_map/ppermute | solution.py:531
  17.3 8.5 %copy-start.1 = (bf16[768,768]{1,0:T(8,128)(2,1)S(1)}, bf16[768,768]{1,0:T(8,128)(2,1)}, u32[]{:S(2)}) copy-start(bf16[768,768]{1,0:T(8,128)(2,1)} %waudio.1) | copy-start | bytes 3538948
  18.1 4.7 %collective-permute-start.5 = (bf16[8,768]{1,0:T(8,128)(2,1)S(1)}, bf16[8,768]{1,0:T(8,128)(2,1)S(1)}, u32[]{:S(2)}, u32[]{:S(2)}) collective-permute-start(bf16[8,768]{1,0:T(8,128)(2,1)S(1)} %add.7), channel_id=1, source_target_pairs={{0,18},{1,19},{2,16},{3,17},{4,22},{5,23},{6,20},{7,21},{8,26},{9,... | collective-permute-start | bytes 36872 | tf_op jit(solution)/shard_map/ppermute | solution.py:531
  20.6 5.1 %collective-permute-start.4 = (f32[4,768]{1,0:T(4,128)S(1)}, f32[4,768]{1,0:T(4,128)S(1)}, u32[]{:S(2)}, u32[]{:S(2)}) collective-permute-start(f32[4,768]{1,0:T(4,128)S(1)} %get-tuple-element.86.mine), channel_id=1, source_target_pairs={{0,1},{1,0},{2,3},{3,2},{4,5},{5,4},{6,7},{7,6},{8,9},{9,8},{10,11... | collective-permute-start | bytes 36872 | tf_op jit(solution)/shard_map/ppermute | solution.py:531
  22.8 4.3 %collective-permute-start.6 = (bf16[16,768]{1,0:T(8,128)(2,1)S(1)}, bf16[16,768]{1,0:T(8,128)(2,1)S(1)}, u32[]{:S(2)}, u32[]{:S(2)}) collective-permute-start(bf16[16,768]{1,0:T(8,128)(2,1)S(1)} %pad_maximum_fusion), channel_id=1, source_target_pairs={{0,14},{1,15},{2,12},{3,13},{4,10},{5,11},{6,8},{7,9},{8,6},{9,7},... | collective-permute-start | bytes 73736 | tf_op jit(solution)/shard_map/ppermute | solution.py:531
  24.6 3.9 %collective-permute-start.7 = (bf16[16,768]{1,0:T(8,128)(2,1)S(1)}, bf16[16,768]{1,0:T(8,128)(2,1)S(1)}, u32[]{:S(2)}, u32[]{:S(2)}) collective-permute-start(bf16[16,768]{1,0:T(8,128)(2,1)S(1)} %pad_maximum_fusion), channel_id=1, source_target_pairs={{0,4},{1,5},{2,6},{3,7},{4,0},{5,1},{6,2},{7,3},{8,12},{9,13},{10,... | collective-permute-start | bytes 73736 | tf_op jit(solution)/shard_map/ppermute | solution.py:531
  25.2 3.4 %collective-permute-start.8 = (bf16[16,768]{1,0:T(8,128)(2,1)S(1)}, bf16[16,768]{1,0:T(8,128)(2,1)S(1)}, u32[]{:S(2)}, u32[]{:S(2)}) collective-permute-start(bf16[16,768]{1,0:T(8,128)(2,1)S(1)} %pad_maximum_fusion), channel_id=1, source_target_pairs={{0,10},{1,11},{2,8},{3,9},{4,14},{5,15},{6,12},{7,13},{8,2},{9,3},... | collective-permute-start | bytes 73736 | tf_op jit(solution)/shard_map/ppermute | solution.py:531

commit v5 on v4

--- a/solution.py
+++ b/solution.py
@@ -82,7 +82,7 @@
 def front_kernel(
     two_sided, lengths, windows, pair_ids, audio_in, video_in, w_qkv, w_query,
     peaks, spans, info, weights, keys, audio, halo, wq, wk, wv,
-    small, ask_w, video, asking, totals, sems,
+    small, ask_w, video, totals, sems,
 ):
     clips, frames, width = audio.shape
     tokens = video.shape[1]
@@ -122,42 +122,44 @@
         for cut in cuts:
             keys[:, :, cut] = dot_f32(flat, wk[:, cut]).astype(BF16).reshape(clips, frames, chunk)
 
-    def make_asking():
-        of_video.wait()
-        flat = video[...].reshape(clips * tokens, video.shape[2])
-        wait(of_asking)
-        for cut in cuts:
-            asking[:, :, cut] = dot_f32(flat, ask_w[:, cut]).astype(BF16).reshape(clips, tokens, chunk)
-
     start(ints + [of_audio] + of_keys)
     wait(ints)
     start([of_video] + of_asking)
     make_keys()
     start(later)
-    make_asking()
     for k in range(3):
         for c in range(clips):
             info[k, c] = jnp.full(info.shape[2:], small[k, c], jnp.int32)
+    rest = (clips, STAT_ROWS - HA, tokens)
+    peaks[:, HA:STAT_ROWS, :] = jnp.zeros(rest, F32)
+    totals[:, HA:STAT_ROWS, :] = jnp.ones(rest, F32)
     place = lax.axis_index("tm") * frames + lax.broadcasted_iota(jnp.int32, (frames, 1), 0)
-    columns = [slice(pair * LANES, (pair + 1) * LANES) for pair in range(HA // 2)]
+    of_video.wait()
+    wait(of_asking)
+
+    def meet(c, pair, rows):
+        both = split_heads(rows, HS**-0.5)
+        scores = dot_nt(keys[c, :, pair * LANES : (pair + 1) * LANES], both)
+        scores = jnp.where(place < small[0, c], scores, NEG_LARGE)
+        peak = jnp.max(scores, axis=0, keepdims=True)
+        rising = jnp.exp(scores - peak)
+        total = jnp.sum(rising, axis=0, keepdims=True)
+        weights[c, :, pair * 2 * tokens : (pair + 1) * 2 * tokens] = rising.astype(BF16)
+        for k in range(2):
+            row = slice(2 * pair + k, 2 * pair + k + 1)
+            peaks[c, row, :] = peak[:, k * tokens : (k + 1) * tokens]
+            totals[c, row, :] = total[:, k * tokens : (k + 1) * tokens]
+
+    def ask(c):
+        return dot_f32(video[c], ask_w[...]).astype(BF16)
+
+    ahead = ask(0)
     for c in range(clips):
-        valid = place < small[0, c]
-        scores = [
-            dot_nt(keys[c, :, cols], split_heads(asking[c, :, cols], HS**-0.5)) for cols in columns
-        ]
-        scores = [jnp.where(valid, s, NEG_LARGE) for s in scores]
-        highest = [jnp.max(s, axis=0, keepdims=True) for s in scores]
-        rising = [jnp.exp(s - peak) for s, peak in zip(scores, highest)]
-        sums = [jnp.sum(r, axis=0, keepdims=True) for r in rising]
+        now = ahead
+        if c + 1 < clips:
+            ahead = ask(c + 1)
         for pair in range(HA // 2):
-            weights[c, :, pair * 2 * tokens : (pair + 1) * 2 * tokens] = rising[pair].astype(BF16)
-            for k in range(2):
-                row = slice(2 * pair + k, 2 * pair + k + 1)
-                peaks[c, row, :] = highest[pair][:, k * tokens : (k + 1) * tokens]
-                totals[c, row, :] = sums[pair][:, k * tokens : (k + 1) * tokens]
-        rest = (STAT_ROWS - HA, tokens)
-        peaks[c, HA:STAT_ROWS, :] = jnp.zeros(rest, F32)
-        totals[c, HA:STAT_ROWS, :] = jnp.ones(rest, F32)
+            meet(c, pair, now[:, pair * LANES : (pair + 1) * LANES])
     spans[...] = peaks[...] + jnp.log(totals[...])
     wait(later)
 
@@ -189,7 +191,6 @@
             pltpu.SMEM((3, clips), jnp.int32),
             VMEM((depth, width), BF16),
             VMEM((clips, tokens, depth), BF16),
-            VMEM((clips, tokens, width), BF16),
             stat,
             pltpu.SemaphoreType.DMA((7 + sides + 2 * (width // (2 * LANES)),)),
         ],
@@ -433,7 +434,7 @@
     rest = x - high.astype(F32)
     middle = rest.astype(BF16)
     low = (rest - middle.astype(F32)).astype(BF16)
-    return jnp.concatenate([high, middle, low], axis=0)
+    return jnp.concatenate([high, middle, low, jnp.zeros_like(low)], axis=0)
 
 
 def audio_head_kernel(info, mine, other, waudio, out, parts):
@@ -448,7 +449,7 @@
     return pl.pallas_call(
         audio_head_kernel,
         name="audio_head",
-        out_shape=[jax.ShapeDtypeStruct((clips, width), F32), VMEM((3 * clips, width), BF16)],
+        out_shape=[jax.ShapeDtypeStruct((clips, width), F32), VMEM((4 * clips, width), BF16)],
         in_specs=whole(4),
         out_specs=whole(2),
         compiler_params=params(8),
@@ -476,7 +477,7 @@
     )
     scale = jnp.sum(jnp.where(square, scale, 0.0), axis=0, keepdims=True)
     found = dot_nt(parts[...], wide.astype(BF16))
-    found = found[:clips] + found[clips : 2 * clips] + found[2 * clips :]
+    found = found[:clips] + found[clips : 2 * clips] + found[2 * clips : 3 * clips]
     found = found * scale + LOGIT_BIAS
     logits[...] = found
     column = lax.broadcasted_iota(jnp.int32, found.shape, 1)

time: 29.6 us -> 29.3 us (0.990)
  Pallas kernels: 13.1 us -> 12.8 us
    pallas_call x1, Pallas kernels: 4.83 us -> 4.52 us  [front(): pl.pallas_call(functools.partial(front_kernel, two_sided), name='front',...]
where the time goes in v5:
time: 29.3 us; the launch traced here: 29.2 us
  Pallas kernels  12.8 us (44%)
  starting transfers between devices  9.86 us (34%)
  waiting for transfers between devices  4.89 us (17%)
  local copies, waits for them, and re-layouts  0.91 us (3%)
  between operations  0.72 us (2%)
    ppermute x8, starting transfers between devices, move(): return lax.ppermute(x, ('batch', 'tm'), pairs)  6.83 us
    ppermute x8, waiting for transfers between devices, move(): return lax.ppermute(x, ('batch', 'tm'), pairs)  4.89 us
    pallas_call x1, Pallas kernels, front(): pl.pallas_call(functools.partial(front_kernel, two_sided), name='front',...  4.52 us
    ppermute x1, starting transfers between devices, others_on_tm(): lax.ppermute(x, 'tm', [(i, (i + shift) % count) for i in range(count)])  3.03 us
    pallas_call x1, Pallas kernels, mix(): pl.pallas_call(functools.partial(mix_kernel, two_sided, plan), name='mix'...  2.39 us
    pallas_call x1, Pallas kernels, make_queries(): pl.pallas_call(functools.partial(queries_kernel, two_sided, tasks), name=...  1.29 us
    pallas_call x1, Pallas kernels, audio_head(): pl.pallas_call(audio_head_kernel, name='audio_head', out_shape=[jax.Shape...  1.03 us
    pallas_call x1, Pallas kernels, pool(): pl.pallas_call(pool_kernel, name='pool', out_shape=VMEM((2 * clips, wvide...  0.97 us
  transfers between devices with their start and end apart: 9, of which 5 were waited for; matrix products, arithmetic and copies ran while one was open for 3% of the time, Pallas kernels for 25%

profile of v5, /device:TPU:0, one launch (start us, length us, event | category | flops | bytes accessed | tf_op | source)
XLA Modules:
  0.0 29.2 jit_solution(13995590870220246918)
XLA Ops:
  0.6 4.5 %front.1 = (f32[4,16,128]{2,1,0:T(8,128)S(1)}, f32[4,16,128]{2,1,0:T(8,128)S(1)}, s32[3,4,8,128]{3,2,1,0:T(8,128)S(1)}, bf16[4,128,1536]{2,1,0:T(8,128)(2,1)S(1)...) custom-call(s32[4]{0:T(128)} %lengths.1, ...), custom_call_target="tpu_custom_call" | custom-call | flops 2000000000 | bytes 8000000 | tf_op jit(solution)/shard_map/front/pallas_call | solution.py:173
  5.2 3.0 %collective-permute-start = (f32[4,16,128]{2,1,0:T(8,128)S(1)}, f32[4,16,128]{2,1,0:T(8,128)S(1)}, u32[]{:S(2)}, u32[]{:S(2)}) collective-permute-start(f32[4,16,128]{2,1,0:T(8,128)S(1)} %get-tuple-element.50.spans), channel_id=1, source_target_pairs={{0,1},{1,0},{2,3},{3,2},{4,5},{5,4},{6,7},{7,6},{8,9},{9,8},{10,11... | collective-permute-start | bytes 98312 | tf_op jit(solution)/shard_map/ppermute | solution.py:516
  8.2 0.1 collective-permute-start.2
  8.3 0.8 %values.1 = bf16[4,128,768]{2,1,0:T(8,128)(2,1)S(1)} custom-call(bf16[4,128,768]{2,1,0:T(8,128)(2,1)S(1)} %get-tuple-element.79.audio, bf16[768,768]{1,0:T(8,128)(2,1)S(1)} %get-tuple-element.78.wv), custom_call_target="tpu_custom_call" | custom-call | flops 600000000 | bytes 2000000 | tf_op jit(solution)/shard_map/values/pallas_call | solution.py:275
  9.1 0.0 copy-start
  9.1 1.3 %queries.1 = (bf16[4,128,768]{2,1,0:T(8,128)(2,1)S(1)}, bf16[1,64,768]{2,1,0:T(8,128)(2,1)S(1)}) custom-call(s32[3,4,8,128]{3,2,1,0:T(8,128)S(1)} %get-tuple-element.72.info, bf16[4,128,768]{2,1,0:T(8,128)(2,1)S(1)} %get-tuple-element.79.audio, bf16[4,128,768]{2,1,0:T(8,128)(2,1)S(1)} %get-tuple-element.74.keys, bf16[4,128,768]{2,1,0:T(8,128)(2,1)S(1)} %values.1, ...), custom_call_target="tpu_custom_call" | custom-call | flops 80000000000 | bytes 3000000 | tf_op jit(solution)/shard_map/queries/pallas_call | solution.py:298
  10.4 0.0 collective-permute-done
  10.4 0.0 copy-done
  10.4 1.0 %pool.1 = f32[8,768]{1,0:T(8,128)S(1)} custom-call(f32[4,16,128]{2,1,0:T(8,128)S(1)} %get-tuple-element.49.peaks, f32[4,16,128]{2,1,0:T(8,128)S(1)} %get-tuple-element.50.spans, f32[1,4,16,128]{3,2,1,0:T(8,128)S(1)} %bitcast.2, bf16[4,128,1536]{2,1,0:T(8,128)(2,1)S(1)} %get-tuple-element.59.weights, bf16[4,128,768]{2,1,0:T(8,128)(2,1)S(1)} %values.1, ...), custom_call_target="tpu_custom_call" | custom-call | flops 200000000 | bytes 2000000 | tf_op jit(solution)/shard_map/pool/pallas_call | solution.py:413
  11.4 0.0 copy-start.2
  11.4 0.0 collective-permute-start.1
  11.4 0.9 %inner.1.rest_1_ = bf16[3,64,768]{2,1,0:T(8,128)(2,1)S(1)} custom-call(s32[3,4,8,128]{3,2,1,0:T(8,128)S(1)} %get-tuple-element.72.info, bf16[4,128,768]{2,1,0:T(8,128)(2,1)S(1)} %get-tuple-element.73.queries, bf16[4,128,768]{2,1,0:T(8,128)(2,1)S(1)} %get-tuple-element.74.keys, bf16[4,128,768]{2,1,0:T(8,128)(2,1)S(1)} %values.1), custom_call_target="tpu_custom_call" | custom-call | flops 300000000 | bytes 2000000 | tf_op jit(solution)/shard_map/inner/pallas_call | solution.py:315
  12.3 0.3 %collective-permute-done.1 = f32[8,768]{1,0:T(8,128)S(1)} collective-permute-done((f32[8,768]{1,0:T(8,128)S(1)}, f32[8,768]{1,0:T(8,128)S(1)}, u32[]{:S(2)}, u32[]{:S(2)}) %collective-permute-start.1) | collective-permute-done | bytes 24608 | tf_op jit(solution)/shard_map/ppermute | solution.py:532
  12.6 2.0 %collective-permute-done.2.near = bf16[1,4,32,768]{3,2,1,0:T(8,128)(2,1)S(1)} collective-permute-done((bf16[1,4,32,768]{3,2,1,0:T(8,128)(2,1)S(1)}, bf16[1,4,32,768]{3,2,1,0:T(8,128)(2,1)S(1)}, u32[]{:S(2)}, u32[]{:S(2)}) %collective-permute-start.2) | collective-permute-done | bytes 196640 | tf_op jit(solution)/shard_map/ppermute | solution.py:532
  14.6 0.0 collective-permute-start.3
  14.6 0.0 copy-done.2
  14.6 2.4 %mix.1 = (bf16[4,128,768]{2,1,0:T(8,128)(2,1)S(1)}, f32[4,768]{1,0:T(4,128)S(1)}) custom-call(s32[3,4,8,128]{3,2,1,0:T(8,128)S(1)} %get-tuple-element.72.info, bf16[4,128,768]{2,1,0:T(8,128)(2,1)S(1)} %get-tuple-element.73.queries, bf16[4,128,768]{2,1,0:T(8,128)(2,1)S(1)} %get-tuple-element.74.keys, bf16[4,128,768]{2,1,0:T(8,128)(2,1)S(1)} %values.1, ...), custom_call_target="tpu_custom_call" | custom-call | flops 2000000000 | bytes 8000000 | tf_op jit(solution)/shard_map/mix/pallas_call | solution.py:362
  17.0 0.0 copy-start.1
  17.0 0.8 %collective-permute-done.3 = f32[8,768]{1,0:T(8,128)S(1)} collective-permute-done((f32[8,768]{1,0:T(8,128)S(1)}, f32[8,768]{1,0:T(8,128)S(1)}, u32[]{:S(2)}, u32[]{:S(2)}) %collective-permute-start.3) | collective-permute-done | bytes 24608 | tf_op jit(solution)/shard_map/ppermute | solution.py:532
  17.8 2.5 %collective-permute-start.5 = (bf16[8,768]{1,0:T(8,128)(2,1)S(1)}, bf16[8,768]{1,0:T(8,128)(2,1)S(1)}, u32[]{:S(2)}, u32[]{:S(2)}) collective-permute-start(bf16[8,768]{1,0:T(8,128)(2,1)S(1)} %add.7), channel_id=1, source_target_pairs={{0,18},{1,19},{2,16},{3,17},{4,22},{5,23},{6,20},{7,21},{8,26},{9,... | collective-permute-start | bytes 36872 | tf_op jit(solution)/shard_map/ppermute | solution.py:532
  20.3 1.3 %collective-permute-start.4 = (f32[4,768]{1,0:T(4,128)S(1)}, f32[4,768]{1,0:T(4,128)S(1)}, u32[]{:S(2)}, u32[]{:S(2)}) collective-permute-start(f32[4,768]{1,0:T(4,128)S(1)} %get-tuple-element.86.mine), channel_id=1, source_target_pairs={{0,1},{1,0},{2,3},{3,2},{4,5},{5,4},{6,7},{7,6},{8,9},{9,8},{10,11... | collective-permute-start | bytes 36872 | tf_op jit(solution)/shard_map/ppermute | solution.py:532
  21.6 0.9 %copy.19 = bf16[4,128,768]{2,1,0:T(8,128)(2,1)} copy(bf16[4,128,768]{2,1,0:T(8,128)(2,1)S(1)} %get-tuple-element.93) | data formatting | bytes 1572864
  22.5 0.0 collective-permute-done.5
  22.5 1.8 %collective-permute-start.6 = (bf16[16,768]{1,0:T(8,128)(2,1)S(1)}, bf16[16,768]{1,0:T(8,128)(2,1)S(1)}, u32[]{:S(2)}, u32[]{:S(2)}) collective-permute-start(bf16[16,768]{1,0:T(8,128)(2,1)S(1)} %pad_maximum_fusion), channel_id=1, source_target_pairs={{0,14},{1,15},{2,12},{3,13},{4,10},{5,11},{6,8},{7,9},{8,6},{9,7},... | collective-permute-start | bytes 73736 | tf_op jit(solution)/shard_map/ppermute | solution.py:532
  24.3 0.5 %collective-permute-start.7 = (bf16[16,768]{1,0:T(8,128)(2,1)S(1)}, bf16[16,768]{1,0:T(8,128)(2,1)S(1)}, u32[]{:S(2)}, u32[]{:S(2)}) collective-permute-start(bf16[16,768]{1,0:T(8,128)(2,1)S(1)} %pad_maximum_fusion), channel_id=1, source_target_pairs={{0,4},{1,5},{2,6},{3,7},{4,0},{5,1},{6,2},{7,3},{8,12},{9,13},{10,... | collective-permute-start | bytes 73736 | tf_op jit(solution)/shard_map/ppermute | solution.py:532
  24.9 0.6 %collective-permute-start.8 = (bf16[16,768]{1,0:T(8,128)(2,1)S(1)}, bf16[16,768]{1,0:T(8,128)(2,1)S(1)}, u32[]{:S(2)}, u32[]{:S(2)}) collective-permute-start(bf16[16,768]{1,0:T(8,128)(2,1)S(1)} %pad_maximum_fusion), channel_id=1, source_target_pairs={{0,10},{1,11},{2,8},{3,9},{4,14},{5,15},{6,12},{7,13},{8,2},{9,3},... | collective-permute-start | bytes 73736 | tf_op jit(solution)/shard_map/ppermute | solution.py:532
  25.4 0.0 collective-permute-done.4.other
  25.5 0.0 copy-done.1
  25.5 1.0 %audio_head.1 = (f32[4,768]{1,0:T(4,128)}, bf16[16,768]{1,0:T(8,128)(2,1)S(1)}) custom-call(s32[3,4,8,128]{3,2,1,0:T(8,128)S(1)} %get-tuple-element.72.info, f32[4,768]{1,0:T(4,128)S(1)} %get-tuple-element.86.mine, f32[4,768]{1,0:T(4,128)S(1)} %collective-permute-done.4.other, bf16[768,768]{1,0:T(8,128)(2,1)S(1)} %copy-done.1), custom_call_target="tpu_custom_call" | custom-call | flops 20000000 | bytes 1200000 | tf_op jit(solution)/shard_map/audio_head/pallas_call | solution.py:449
  26.5 0.3 collective-permute-done.6
  26.8 1.5 %collective-permute-done.7 = bf16[16,768]{1,0:T(8,128)(2,1)S(1)} collective-permute-done((bf16[16,768]{1,0:T(8,128)(2,1)S(1)}, bf16[16,768]{1,0:T(8,128)(2,1)S(1)}, u32[]{:S(2)}, u32[]{:S(2)}) %collective-permute-start.7) | collective-permute-done | bytes 24608 | tf_op jit(solution)/shard_map/ppermute | solution.py:532
  28.3 0.0 collective-permute-done.8
  28.3 0.9 %logits_and_loss.1 = (f32[4,64]{1,0:T(4,128)}, f32[1,4]{1,0:T(1,128)}, f32[4,768]{1,0:T(4,128)}) custom-call(s32[3,4,8,128]{3,2,1,0:T(8,128)S(1)} %get-tuple-element.72.info, bf16[16,768]{1,0:T(8,128)(2,1)S(1)} %get-tuple-element.88.parts, bf16[64,768]{1,0:T(8,128)(2,1)S(1)} %constant_dynamic-update-slice_fusion.held), custom_call_target="tpu_custom_call" | custom-call | flops 20000000 | bytes 300000 | tf_op jit(solution)/shard_map/logits_and_loss/pallas_call | solution.py:496
  (8 shorter events, 0.0 us)
Async XLA Ops:
  5.2 5.2 %collective-permute-start = (f32[4,16,128]{2,1,0:T(8,128)S(1)}, f32[4,16,128]{2,1,0:T(8,128)S(1)}, u32[]{:S(2)}, u32[]{:S(2)}) collective-permute-start(f32[4,16,128]{2,1,0:T(8,128)S(1)} %get-tuple-element.50.spans), channel_id=1, source_target_pairs={{0,1},{1,0},{2,3},{3,2},{4,5},{5,4},{6,7},{7,6},{8,9},{9,8},{10,11... | collective-permute-start | bytes 98312 | tf_op jit(solution)/shard_map/ppermute | solution.py:516
  8.2 6.4 %collective-permute-start.2 = (bf16[1,4,32,768]{3,2,1,0:T(8,128)(2,1)S(1)}, bf16[1,4,32,768]{3,2,1,0:T(8,128)(2,1)S(1)}, u32[]{:S(2)}, u32[]{:S(2)}) collective-permute-start(bf16[1,4,32,768]{3,2,1,0:T(8,128)(2,1)S(1)} %get-tuple-element.67), channel_id=1, source_target_pairs={{0,1},{1,0},{2,3},{3,2},{4,5},{5,4},{6,7},{7,6},{8,9},{9,8},{10,11... | collective-permute-start | bytes 589832 | tf_op jit(solution)/shard_map/ppermute | solution.py:532
  9.1 1.3 %copy-start = (bf16[768,768]{1,0:T(8,128)(2,1)S(1)}, bf16[768,768]{1,0:T(8,128)(2,1)}, u32[]{:S(2)}) copy-start(bf16[768,768]{1,0:T(8,128)(2,1)} %wvideo.1) | copy-start | bytes 3538948
  11.4 3.2 %copy-start.2 = (bf16[768,768]{1,0:T(8,128)(2,1)S(1)}, bf16[768,768]{1,0:T(8,128)(2,1)}, u32[]{:S(2)}) copy-start(bf16[768,768]{1,0:T(8,128)(2,1)} %wout) | copy-start | bytes 3538948
  11.4 1.2 %collective-permute-start.1 = (f32[8,768]{1,0:T(8,128)S(1)}, f32[8,768]{1,0:T(8,128)S(1)}, u32[]{:S(2)}, u32[]{:S(2)}) collective-permute-start(f32[8,768]{1,0:T(8,128)S(1)} %pool.1), channel_id=1, source_target_pairs={{0,2},{1,3},{2,0},{3,1},{4,6},{5,7},{6,4},{7,5},{8,10},{9,11},{10,... | collective-permute-start | bytes 73736 | tf_op jit(solution)/shard_map/ppermute | solution.py:532
  14.6 3.3 %collective-permute-start.3 = (f32[8,768]{1,0:T(8,128)S(1)}, f32[8,768]{1,0:T(8,128)S(1)}, u32[]{:S(2)}, u32[]{:S(2)}) collective-permute-start(f32[8,768]{1,0:T(8,128)S(1)} %add.6), channel_id=1, source_target_pairs={{0,3},{1,2},{2,1},{3,0},{4,7},{5,6},{6,5},{7,4},{8,11},{9,10},{10,... | collective-permute-start | bytes 73736 | tf_op jit(solution)/shard_map/ppermute | solution.py:532
  17.0 8.5 %copy-start.1 = (bf16[768,768]{1,0:T(8,128)(2,1)S(1)}, bf16[768,768]{1,0:T(8,128)(2,1)}, u32[]{:S(2)}) copy-start(bf16[768,768]{1,0:T(8,128)(2,1)} %waudio.1) | copy-start | bytes 3538948
  17.8 4.7 %collective-permute-start.5 = (bf16[8,768]{1,0:T(8,128)(2,1)S(1)}, bf16[8,768]{1,0:T(8,128)(2,1)S(1)}, u32[]{:S(2)}, u32[]{:S(2)}) collective-permute-start(bf16[8,768]{1,0:T(8,128)(2,1)S(1)} %add.7), channel_id=1, source_target_pairs={{0,18},{1,19},{2,16},{3,17},{4,22},{5,23},{6,20},{7,21},{8,26},{9,... | collective-permute-start | bytes 36872 | tf_op jit(solution)/shard_map/ppermute | solution.py:532
  20.3 5.1 %collective-permute-start.4 = (f32[4,768]{1,0:T(4,128)S(1)}, f32[4,768]{1,0:T(4,128)S(1)}, u32[]{:S(2)}, u32[]{:S(2)}) collective-permute-start(f32[4,768]{1,0:T(4,128)S(1)} %get-tuple-element.86.mine), channel_id=1, source_target_pairs={{0,1},{1,0},{2,3},{3,2},{4,5},{5,4},{6,7},{7,6},{8,9},{9,8},{10,11... | collective-permute-start | bytes 36872 | tf_op jit(solution)/shard_map/ppermute | solution.py:532
  22.5 4.2 %collective-permute-start.6 = (bf16[16,768]{1,0:T(8,128)(2,1)S(1)}, bf16[16,768]{1,0:T(8,128)(2,1)S(1)}, u32[]{:S(2)}, u32[]{:S(2)}) collective-permute-start(bf16[16,768]{1,0:T(8,128)(2,1)S(1)} %pad_maximum_fusion), channel_id=1, source_target_pairs={{0,14},{1,15},{2,12},{3,13},{4,10},{5,11},{6,8},{7,9},{8,6},{9,7},... | collective-permute-start | bytes 73736 | tf_op jit(solution)/shard_map/ppermute | solution.py:532
  24.3 3.9 %collective-permute-start.7 = (bf16[16,768]{1,0:T(8,128)(2,1)S(1)}, bf16[16,768]{1,0:T(8,128)(2,1)S(1)}, u32[]{:S(2)}, u32[]{:S(2)}) collective-permute-start(bf16[16,768]{1,0:T(8,128)(2,1)S(1)} %pad_maximum_fusion), channel_id=1, source_target_pairs={{0,4},{1,5},{2,6},{3,7},{4,0},{5,1},{6,2},{7,3},{8,12},{9,13},{10,... | collective-permute-start | bytes 73736 | tf_op jit(solution)/shard_map/ppermute | solution.py:532
  24.9 3.4 %collective-permute-start.8 = (bf16[16,768]{1,0:T(8,128)(2,1)S(1)}, bf16[16,768]{1,0:T(8,128)(2,1)S(1)}, u32[]{:S(2)}, u32[]{:S(2)}) collective-permute-start(bf16[16,768]{1,0:T(8,128)(2,1)S(1)} %pad_maximum_fusion), channel_id=1, source_target_pairs={{0,10},{1,11},{2,8},{3,9},{4,14},{5,15},{6,12},{7,13},{8,2},{9,3},... | collective-permute-start | bytes 73736 | tf_op jit(solution)/shard_map/ppermute | solution.py:532
